TPU v7x, 32 devices: a whole 2x2x4 slice. The times are simulated.
32 devices in a mesh: dp: 16 (over z, y, x), mp: 2 (over core).
Axes of the slice: x: 2, y: 2, z: 4, core: 2. Of those that a mesh axis runs over, the one named last changes fastest.
Arguments:
- query_grad: bfloat16 [2048, 7168], P('mp', 'dp'), may hold values from -6 to 6
- basis_in: bfloat16 [2048, 2048], P(None, 'mp'), may hold values from -0.125 to 0.125
- basis_out: bfloat16 [7168, 7168], P('mp', 'dp'), may hold values from -0.0625 to 0.0625
- eigen_scales: float32 [2048, 7168], P('mp', 'dp'), may hold values from 0.006 to 240
- inputs: bfloat16 [8192, 2048], P('dp', 'mp'), may hold values from -6 to 6
- out_grads: bfloat16 [8192, 7168], P('dp', 'mp'), may hold values from -0.00015258789 to 0.00015258789
- segment_ids: int32 [8192], P('dp'), may hold values from 0 to 31, as said below
Outputs:
- sequence_scores: float32 [32], P('dp')
Inputs may be any that keep to these rules, and one draw needn't show every extreme that they name: `segment_ids`: the tokens of each index of dp form 2 runs of one or more tokens, each run one whole sequence; sequence numbers are given to the runs in an arbitrary order, each number to exactly one run.
All inputs are finite; a program needn't handle non-finite values.
Results may differ from a plain program's by a relative error of at most 0.024.
Values may be sent and summed in bfloat16 or wider, within the bound.
A program may use at most 128 MiB of HBM per device.

v0:
```python
import jax
import jax.numpy as jnp
from jax import lax
from jax.sharding import PartitionSpec as P

D = 2048
F = 7168
SEQ_DEV = 2


damping_ratio = 0.1


def on_device(query_grad, basis_in, basis_out, eigen_scales, inputs, out_grads, segment_ids):
    column_basis = lax.all_gather(basis_out, "mp", axis=0, tiled=True)
    turned = jnp.dot(
        lax.all_gather(query_grad, "dp", axis=1, tiled=True),
        column_basis,
        preferred_element_type=jnp.float32,
    ).astype(jnp.bfloat16)
    rotated_full = lax.all_gather(turned, "mp", axis=0, tiled=True)
    rotated = lax.dot_general(
        basis_in, rotated_full, (((0,), (0,)), ((), ())), preferred_element_type=jnp.float32
    )
    scale_sum = lax.psum(jnp.sum(eigen_scales), ("dp", "mp"))
    damping = damping_ratio * scale_sum / (D * F)
    rescaled = (rotated / (eigen_scales + damping)).astype(jnp.bfloat16)
    row_basis = lax.all_to_all(column_basis, "dp", split_axis=0, concat_axis=1, tiled=True)
    back_block = lax.dot_general(
        lax.all_gather(rescaled, "dp", axis=1, tiled=True),
        row_basis,
        (((1,), (1,)), ((), ())),
        preferred_element_type=jnp.float32,
    ).astype(jnp.bfloat16)
    inputs_full, grads_full = (
        lax.all_gather(inputs, "mp", axis=1, tiled=True),
        lax.all_gather(out_grads, "mp", axis=1, tiled=True),
    )
    projected = jnp.dot(inputs_full, basis_in, preferred_element_type=jnp.float32)
    pulled = lax.dot_general(
        grads_full,
        lax.all_gather(back_block, "dp", axis=1, tiled=True),
        (((1,), (1,)), ((), ())),
        preferred_element_type=jnp.float32,
    )
    partial_value = jnp.sum(projected * pulled, axis=1)
    seq_count = SEQ_DEV * lax.axis_size("dp")
    onehot = (segment_ids[:, None] == jnp.arange(seq_count, dtype=jnp.int32)[None, :]).astype(
        jnp.float32
    )
    token_score = lax.psum(partial_value, "mp")
    seq_terms = jnp.dot(token_score, onehot, precision=lax.Precision.HIGHEST)
    return lax.psum_scatter(seq_terms, "dp", scatter_dimension=0, tiled=True)


def solution(mesh):
    return jax.shard_map(
        on_device,
        mesh=mesh,
        in_specs=(
            P("mp", "dp"),
            P(None, "mp"),
            P("mp", "dp"),
            P("mp", "dp"),
            P("dp", "mp"),
            P("dp", "mp"),
            P("dp"),
        ),
        out_specs=P("dp"),
        check_vma=False,
    )
```

profile of v0, /device:TPU:0, one launch (start us, length us, event | category | flops | bytes accessed | tf_op | source)
XLA Modules:
  0.0 843.7 jit_solution(10680076171426073265)
XLA Ops:
  6.5 0.0 all-gather.12.cloned.1.call-start
  6.5 0.7 all-gather.12.cloned.1.call-update
  7.3 0.0 all-gather.10.cloned.1.call-start
  7.3 0.7 all-gather.10.cloned.1.call-update
  8.0 0.0 copy-start
  8.0 0.0 all-gather.14.cloned.1.call-start
  8.1 20.5 %all-gather.12.cloned.1.call-done = bf16[7168,448]{0,1:T(8,128)(2,1)} async-done(((bf16[3584,448]{0,1:T(8,128)(2,1)}), bf16[7168,448]{0,1:T(8,128)(2,1)}) %all-gather.12.cloned.1.call-update) | async-done | bytes 6422544 | tf_op jit(solution)/shard_map/all_gather | solution.py:15
  28.6 175.8 %all-gather.10.cloned.1.call-done = bf16[1024,7168]{0,1:T(8,128)(2,1)} async-done(((bf16[1024,448]{0,1:T(8,128)(2,1)}), bf16[1024,7168]{0,1:T(8,128)(2,1)}) %all-gather.10.cloned.1.call-update) | async-done | bytes 14680080 | tf_op jit(solution)/shard_map/all_gather | solution.py:17
  204.4 12.8 %convolution_convert_fusion.1 = bf16[1024,448]{0,1:T(8,128)(2,1)} fusion(bf16[7168,448]{0,1:T(8,128)(2,1)} %all-gather.12.cloned.1.call-done, bf16[1024,7168]{0,1:T(8,128)(2,1)} %all-gather.10.cloned.1.call-done), kind=kOutput, calls=%fused_computation.5 | convolution fusion | flops 6577127424 | bytes 22020096 | tf_op jit(solution)/shard_map/dot_general | solution.py:16
  217.2 0.0 all-gather.14.cloned.1.call-update
  217.2 0.0 all-gather.16.cloned.1.call-start
  217.3 0.0 copy-done
  217.3 1.1 reduce_sum.18
  218.3 38.6 %psum.14 = f32[]{:T(128)} all-reduce(f32[]{:T(128)} %reduce_sum.18), channel_id=1, replica_groups=mesh['dp'=16,'mp'=2] {'dp','mp'}, use_global_device_ids=true, to_apply=%region_1.0 | all-reduce | flops 1 | bytes 8 | tf_op jit(solution)/shard_map/psum | solution.py:25
  257.6 0.0 all-gather.14.cloned.1.call-done
  257.6 5.7 fusion.1
  263.4 0.0 all-gather.16.cloned.1.call-update
  263.4 9.7 %copy.9 = bf16[7168,448]{1,0:T(8,128)(2,1)} copy(bf16[7168,448]{0,1:T(8,128)(2,1)} %all-gather.12.cloned.1.call-done) | data formatting | bytes 12845056 | tf_op jit(solution)/shard_map/all_gather | solution.py:15
  273.1 6.6 all-to-all-start
  279.6 0.0 all-gather.8.cloned.1.call-start
  279.7 0.5 all-gather.8.cloned.1.call-update
  280.2 0.0 all-gather.20.cloned.1.call-start
  280.3 0.5 all-gather.20.cloned.1.call-update
  280.8 0.2 all-gather.18.cloned.1.call-start
  281.0 185.8 %all-to-all-done = bf16[16,448,448]{2,1,0:T(8,128)(2,1)} async-done(((bf16[16,448,448]{2,1,0:T(8,128)(2,1)}), bf16[16,448,448]{2,1,0:T(8,128)(2,1)}, u32[]{:S(2)}, u32[]{:S(2)}) %all-to-all-start) | async-done | bytes 6422560 | tf_op jit(solution)/shard_map/all_to_all | solution.py:28
  466.9 10.3 %copy.10 = bf16[448,16,448]{2,1,0:T(8,128)(2,1)} copy(bf16[448,16,448]{2,0,1:T(8,128)(2,1)} %bitcast.2) | data formatting | bytes 12845056 | tf_op jit(solution)/shard_map/all_to_all | solution.py:28
  477.2 12.7 %all_to_all.17 = bf16[448,7168]{1,0:T(8,128)(2,1)} reshape(bf16[448,16,448]{2,1,0:T(8,128)(2,1)} %copy.10) | data formatting | bytes 12845056 | tf_op jit(solution)/shard_map/all_to_all | solution.py:28
  489.9 0.0 copy-start.2
  489.9 83.7 %all-gather.16.cloned.1.call-done = bf16[1024,7168]{0,1:T(8,128)(2,1)} async-done(((bf16[1024,448]{0,1:T(8,128)(2,1)}), bf16[1024,7168]{0,1:T(8,128)(2,1)}) %all-gather.16.cloned.1.call-update) | async-done | bytes 14680080 | tf_op jit(solution)/shard_map/all_gather | solution.py:30
  573.6 12.9 %convolution_convert_fusion = bf16[1024,448]{0,1:T(8,128)(2,1)} fusion(bf16[448,7168]{1,0:T(8,128)(2,1)} %all_to_all.17, bf16[1024,7168]{0,1:T(8,128)(2,1)} %all-gather.16.cloned.1.call-done), kind=kOutput, calls=%fused_computation.4 | convolution fusion | flops 6577127424 | bytes 22020096 | tf_op jit(solution)/shard_map/dot_general | solution.py:29
  586.5 0.0 all-gather.18.cloned.1.call-update
  586.5 0.0 copy-done.2
  586.5 0.6 dynamic-slice
  587.7 0.0 all-gather.8.cloned.1.call-done
  587.8 5.2 fusion.3
  592.9 0.0 copy-start.1
  592.9 12.5 %all-gather.20.cloned.1.call-done = bf16[512,7168]{1,0:T(8,128)(2,1)} async-done(((bf16[512,3584]{1,0:T(8,128)(2,1)}), bf16[512,7168]{1,0:T(8,128)(2,1)}) %all-gather.20.cloned.1.call-update) | async-done | bytes 7340048 | tf_op jit(solution)/shard_map/all_gather | solution.py:37
  605.5 175.8 %all-gather.18.cloned.1.call-done = bf16[1024,7168]{0,1:T(8,128)(2,1)} async-done(((bf16[1024,448]{0,1:T(8,128)(2,1)}), bf16[1024,7168]{0,1:T(8,128)(2,1)}) %all-gather.18.cloned.1.call-update) | async-done | bytes 14680080 | tf_op jit(solution)/shard_map/all_gather | solution.py:42
  781.3 13.4 %fusion = f32[512]{0:T(512)S(1)} fusion(f32[512,1024]{1,0:T(8,128)S(1)} %fusion.3, bf16[512,7168]{1,0:T(8,128)(2,1)} %all-gather.20.cloned.1.call-done, bf16[1024,7168]{0,1:T(8,128)(2,1)} %all-gather.18.cloned.1.call-done), kind=kOutput, calls=%fused_computation.1 | convolution fusion | flops 7517240832 | bytes 24119296 | tf_op jit(solution)/shard_map/dot_general | solution.py:40
  794.7 2.5 psum.15
  797.1 0.0 copy-done.1
  797.2 0.3 convolution_bitcast_fusion
  797.4 38.9 %all-reduce = f32[32]{0:T(128)S(1)} all-reduce(f32[32]{0:T(128)S(1)} %convolution_bitcast_fusion), channel_id=2, replica_groups=mesh['dp'=16,'mp'=2] {'dp'}, use_global_device_ids=true, to_apply=%region_4.0.clone | all-reduce | flops 32 | bytes 256
  836.3 0.6 dynamic-slice.1
Async XLA Ops:
  6.5 22.1 %all-gather.12.cloned.1.call-start = ((), (), s32[]{:S(2)}) async-start(), calls=%async_computation.3 | async-start | bytes 9633792 | tf_op jit(solution)/shard_map/all_gather | solution.py:15
  7.3 197.2 %all-gather.10.cloned.1.call-start = ((), (), s32[]{:S(2)}) async-start(), calls=%async_computation.2 | async-start | bytes 15597568 | tf_op jit(solution)/shard_map/all_gather | solution.py:17
  8.0 209.3 %copy-start = (f32[1024,448]{0,1:T(8,128)S(1)}, f32[1024,448]{0,1:T(8,128)}, u32[]{:S(2)}) copy-start(f32[1024,448]{0,1:T(8,128)} %param.10) | copy-start | bytes 5505028
  8.0 249.6 %all-gather.14.cloned.1.call-start = ((), (), s32[]{:S(2)}) async-start(), calls=%async_computation.4 | async-start | bytes 2752512 | tf_op jit(solution)/shard_map/all_gather | solution.py:21
  217.2 356.4 %all-gather.16.cloned.1.call-start = ((), (), s32[]{:S(2)}) async-start(), calls=%async_computation.5 | async-start | bytes 15597568 | tf_op jit(solution)/shard_map/all_gather | solution.py:30
  273.1 193.8 %all-to-all-start = ((bf16[16,448,448]{2,1,0:T(8,128)(2,1)}), bf16[16,448,448]{2,1,0:T(8,128)(2,1)}, u32[]{:S(2)}, u32[]{:S(2)}) async-start(bf16[16,448,448]{2,1,0:T(8,128)(2,1)} %bitcast.25), calls=%async_computation | async-start | bytes 14680064 | tf_op jit(solution)/shard_map/all_to_all | solution.py:28
  279.6 308.1 %all-gather.8.cloned.1.call-start = ((), (), s32[]{:S(2)}) async-start(), calls=%async_computation.1 | async-start | bytes 3145728 | tf_op jit(solution)/shard_map/all_gather | solution.py:36
  280.2 325.2 %all-gather.20.cloned.1.call-start = ((), (), s32[]{:S(2)}) async-start(), calls=%async_computation.7 | async-start | bytes 11010048 | tf_op jit(solution)/shard_map/all_gather | solution.py:37
  280.8 500.5 %all-gather.18.cloned.1.call-start = ((), (), s32[]{:S(2)}) async-start(), calls=%async_computation.6 | async-start | bytes 15597568 | tf_op jit(solution)/shard_map/all_gather | solution.py:42
  489.9 96.6 %copy-start.2 = (u32[32]{0:T(128)S(1)}, u32[32]{0:T(128)}, u32[]{:S(2)}) copy-start(u32[32]{0:T(128)} %constant.9) | copy-start | bytes 388
  592.9 204.2 %copy-start.1 = (s32[512]{0:T(512)S(1)}, s32[512]{0:T(512)}, u32[]{:S(2)}) copy-start(s32[512]{0:T(512)} %param.13) | copy-start | bytes 6148
Sparse Core Ops, SparseCore 0:
  8.9 19.6 all-gather.11
  31.3 173.0 all-gather.9
  217.3 8.3 all-gather.13
  263.5 310.0 all-gather.15
  575.0 9.5 all-gather.7
  585.9 19.4 all-gather.19
  608.2 173.0 all-gather.17
where the time goes:
time: 845 us; the launch traced here: 844 us
  waiting for transfers between devices  657 us (78%)
  blocking collectives  79.9 us (9%)
  matrix products  50.1 us (6%)
  local copies, waits for them, and re-layouts  33.9 us (4%)
  between operations  14.9 us (2%)
    all_to_all x1, waiting for transfers between devices, on_device(): lax.all_to_all(column_basis, 'dp', split_axis=0, concat_axis=1, tiled=True)  186 us
    all_gather x1, waiting for transfers between devices, on_device(): lax.all_gather(query_grad, 'dp', axis=1, tiled=True)  176 us
    all_gather x1, waiting for transfers between devices, on_device(): lax.all_gather(back_block, 'dp', axis=1, tiled=True)  176 us
    all_gather x1, waiting for transfers between devices, on_device(): lax.all_gather(rescaled, 'dp', axis=1, tiled=True)  83.7 us
    unnamed x1, blocking collectives  38.9 us
    psum x1, blocking collectives, on_device(): scale_sum = lax.psum(jnp.sum(eigen_scales), ('dp', 'mp'))  38.6 us
    all_to_all x2, local copies, waits for them, and re-layouts, on_device(): lax.all_to_all(column_basis, 'dp', split_axis=0, concat_axis=1, tiled=True)  23.1 us
    all_gather x1, waiting for transfers between devices, on_device(): column_basis = lax.all_gather(basis_out, 'mp', axis=0, tiled=True)  20.5 us
  transfers between devices with their start and end apart: 8, of which 6 were waited for; matrix products, arithmetic and copies ran while one was open for 5% of the time, Pallas kernels for 0%

commit v1 on v0

v1 whole, which is shorter than its diff:
```python
import jax
import jax.numpy as jnp
from jax import lax
from jax.sharding import PartitionSpec as P

IN = 4
damping_ratio = 0.1
BF = jnp.bfloat16
F32 = jnp.float32


def on_device(query_grad, basis_in, basis_out, eigen_scales, inputs, out_grads, segment_ids):
    n = lax.axis_size("dp")
    outer = n // IN
    d_in = basis_in.shape[0]
    fc = basis_out.shape[1]
    f_all = fc * n
    tok = inputs.shape[0]
    me = lax.axis_index("dp")
    o, p = me // IN, me % IN

    def swap(v, j):
        return lax.ppermute(v, "dp", [(i, i ^ j) for i in range(n)])

    def right(v):
        return lax.ppermute(v, "dp", [(i, i + IN) for i in range(n - IN)])

    def left(v):
        return lax.ppermute(v, "dp", [(i, i - IN) for i in range(IN, n)])

    def line_gather(v):
        rights, lefts = [], []
        a = b = v
        for _ in range(outer - 1):
            a, b = right(a), left(b)
            rights.append(a)
            lefts.append(b)
        held = jnp.stack(rights[::-1] + [v] + lefts)
        return lax.dynamic_slice_in_dim(held, outer - 1 - o, outer, axis=0)

    part_sum = jnp.broadcast_to(jnp.sum(eigen_scales), (1, 128))
    sums = lax.all_gather(part_sum, ("dp", "mp"), axis=0, tiled=True)
    damping = damping_ratio * jnp.sum(sums[:, 0]) / (d_in * f_all)

    w_full = lax.all_gather(query_grad, "mp", axis=0, tiled=True)
    u = lax.dot_general(
        basis_in, w_full, (((0,), (0,)), ((), ())), preferred_element_type=F32
    ).astype(BF)
    u_all = line_gather(u)

    rows = basis_out.reshape(-1, IN, fc, fc)
    q = []
    for j in range(IN):
        sent = lax.dynamic_index_in_dim(rows, p ^ j, axis=1, keepdims=False)
        got = swap(sent, j) if j else sent
        q.append(lax.all_gather(got, "mp", axis=0, tiled=True))

    terms = {}
    for j in (3, 1, 2, 0):
        y = lax.dot_general(u_all, q[j], (((0, 2), (0, 1)), ((), ())), preferred_element_type=F32)
        terms[j] = swap(y.astype(BF), j).astype(F32) if j else y
    rotated = terms[0] + terms[1] + terms[2] + terms[3]
    rescaled = (rotated / (eigen_scales + damping)).astype(BF)

    res = [swap(rescaled, j) if j else rescaled for j in range(IN)]
    q_cat = jnp.concatenate(q, axis=2)
    res_cat = jnp.concatenate(res, axis=1)
    part = lax.dot_general(
        q_cat, res_cat, (((2,), (1,)), ((), ())), preferred_element_type=F32
    ).astype(BF)

    def block(k):
        return lax.dynamic_index_in_dim(part, k % outer, axis=0, keepdims=False).astype(F32)

    a = b = None
    for t in range(outer - 1):
        va = block(outer - 1 - t + o)
        vb = block(o + t + 1)
        if a is not None:
            va, vb = va + a, vb + b
        a = right(va.astype(BF)).astype(F32)
        b = left(vb.astype(BF)).astype(F32)
    back = (block(o) + a + b).astype(BF)
    back_all = line_gather(back)

    x_full = lax.all_gather(inputs, "mp", axis=1, tiled=True)
    proj = jnp.dot(x_full, basis_in, preferred_element_type=F32)
    proj_bf = proj.astype(BF)
    proj_all = jnp.concatenate([proj] + [swap(proj_bf, j).astype(F32) for j in range(1, IN)])
    cols = out_grads.reshape(tok, -1, IN, fc)
    g = []
    for j in range(IN):
        sent = lax.dynamic_index_in_dim(cols, p ^ j, axis=2, keepdims=False).transpose(1, 0, 2)
        g.append(swap(sent, j) if j else sent)
    g_all = lax.all_gather(jnp.concatenate(g, axis=1), "mp", axis=0, tiled=True)
    ids = jnp.concatenate([segment_ids] + [swap(segment_ids, j) for j in range(1, IN)])

    pulled = lax.dot_general(
        g_all, back_all, (((0, 2), (0, 1)), ((), ())), preferred_element_type=F32
    )
    score = jnp.sum(proj_all * pulled, axis=1)
    seq_count = 2 * n
    onehot = (ids[:, None] == jnp.arange(seq_count, dtype=jnp.int32)[None, :]).astype(F32)
    seq_terms = jnp.dot(score, onehot, precision=lax.Precision.HIGHEST)
    every = lax.all_gather(seq_terms[None], ("dp", "mp"), axis=0, tiled=True)
    return lax.dynamic_slice_in_dim(jnp.sum(every, axis=0), 2 * me, 2)


def solution(mesh):
    return jax.shard_map(
        on_device,
        mesh=mesh,
        in_specs=(
            P("mp", "dp"),
            P(None, "mp"),
            P("mp", "dp"),
            P("mp", "dp"),
            P("dp", "mp"),
            P("dp", "mp"),
            P("dp"),
        ),
        out_specs=P("dp"),
        check_vma=False,
    )
```

time: 845 us -> 597 us (0.71)
  waiting for transfers between devices: 657 us -> 223 us
  starting transfers between devices: 6.97 us -> 77.8 us
  local copies, waits for them, and re-layouts: 33.9 us -> 98.2 us
  other arithmetic: 1.07 us -> 22.8 us
  blocking collectives: 79.9 us -> 101 us
    all_gather x7, waiting for transfers between devices: 468 us -> 0.05 us  [the longest x4 0.03 us: on_device(): q.append(lax.all_gather(got, 'mp', axis=0, tiled=True))]
    ppermute x0 -> x36, waiting for transfers between devices: none -> 222 us  [the longest x18 129 us: swap(): return lax.ppermute(v, 'dp', [(i, i ^ j) for i in range(n)])]
    all_to_all x1 -> x0, waiting for transfers between devices: 186 us -> none  [on_device(): lax.all_to_all(column_basis, 'dp', split_axis=0, concat_axis=1, tiled=True)]
    ppermute x0 -> x36, starting transfers between devices: none -> 77.6 us  [the longest x9 39.6 us: right(): return lax.ppermute(v, 'dp', [(i, i + IN) for i in range(n - IN)])]
    unnamed x1 -> x2, blocking collectives: 38.9 us -> 101 us
    psum x2 -> x0, blocking collectives: 41.1 us -> none  [the longest x1 38.6 us: on_device(): scale_sum = lax.psum(jnp.sum(eigen_scales), ('dp', 'mp'))]
    dynamic_slice x0 -> x6, local copies, waits for them, and re-layouts: none -> 34.8 us  [the longest x5 34.2 us: on_device(): sent = lax.dynamic_index_in_dim(rows, p ^ j, axis=1, keepdims=False)]
    unnamed x8 -> x41, local copies, waits for them, and re-layouts: 1.18 us -> 35.4 us
  transfers between devices with their start and end apart: 8 -> 43, of which waited for: 6 -> 20; matrix products, arithmetic and copies ran while one was open for 5% -> 24% of each run, Pallas kernels for 0% -> 0%
where the time goes in v1:
time: 597 us; the launch traced here: 595 us
  waiting for transfers between devices  223 us (37%)
  blocking collectives  101 us (17%)
  local copies, waits for them, and re-layouts  98.2 us (16%)
  starting transfers between devices  77.8 us (13%)
  matrix products  57.7 us (10%)
  other arithmetic  22.8 us (4%)
  between operations  14.6 us (2%)
    ppermute x18, waiting for transfers between devices, swap(): return lax.ppermute(v, 'dp', [(i, i ^ j) for i in range(n)])  129 us
    unnamed x2, blocking collectives  101 us
    ppermute x9, waiting for transfers between devices, right(): return lax.ppermute(v, 'dp', [(i, i + IN) for i in range(n - IN)])  55.2 us
    ppermute x9, starting transfers between devices, right(): return lax.ppermute(v, 'dp', [(i, i + IN) for i in range(n - IN)])  39.6 us
    ppermute x9, waiting for transfers between devices, left(): return lax.ppermute(v, 'dp', [(i, i - IN) for i in range(IN, n)])  37.8 us
    unnamed x41, local copies, waits for them, and re-layouts  35.4 us
    dynamic_slice x5, local copies, waits for them, and re-layouts, on_device(): sent = lax.dynamic_index_in_dim(rows, p ^ j, axis=1, keepdims=False)  34.2 us
    ppermute x18, starting transfers between devices, swap(): return lax.ppermute(v, 'dp', [(i, i ^ j) for i in range(n)])  26.2 us
  transfers between devices with their start and end apart: 43, of which 20 were waited for; matrix products, arithmetic and copies ran while one was open for 24% of the time, Pallas kernels for 0%

profile of v1, /device:TPU:0, one launch (start us, length us, event | category | flops | bytes accessed | tf_op | source)
XLA Modules:
  0.0 595.0 jit_solution(4106032049841323477)
XLA Ops:
  7.3 9.4 %reshape.12 = bf16[2,4,448,448]{2,1,0,3:T(4,128)(2,1)} reshape(bf16[3584,448]{0,1:T(8,128)(2,1)} %param.9) | data formatting | bytes 6422528 | tf_op jit(solution)/shard_map/reshape | solution.py:51
  16.8 13.3 %constant_dynamic-slice_fusion.3 = (bf16[2,1,448,448]{2,1,0,3:T(2,128)(2,1)S(1)}, bf16[2,1,448,448]{2,1,0,3:T(2,128)(2,1)}, bf16[2,1,448,448]{2,1,0,3:T(2,128)(2,1)}, bf16[2,1,448,448]{2,1,0,3:T(2,128)(2,1)}) fusion(bf16[2,4,448,448]{2,1,0,3:T(4,128)(2,1)} %reshape.12, s32[]{:T(128)S(6)} %select_n.75, s32[]{:T(128)S(6)} %select_n.78, s32[]{:T(128)S(6)} %select_n.77, ...), kind=kLoop, calls=%fused_computation.79 | loop fusion | bytes 6422544 | tf_op jit(solution)/shard_map/jit(dynamic_index_in_dim)/dynamic_slice | solution.py:54
  30.1 5.7 copy.47
  38.7 20.6 %collective-permute-done.6 = bf16[2,448,448]{2,1,0:T(8,128)(2,1)S(1)} collective-permute-done((bf16[2,448,448]{2,1,0:T(8,128)(2,1)}, bf16[2,448,448]{2,1,0:T(8,128)(2,1)S(1)}, u32[]{:S(2)}, u32[]{:S(2)}) %collective-permute-start.6) | collective-permute-done | bytes 802848 | tf_op jit(solution)/shard_map/ppermute | solution.py:23
  60.3 5.7 copy.48
  67.8 20.0 %collective-permute-done.7 = bf16[2,448,448]{2,1,0:T(8,128)(2,1)S(1)} collective-permute-done((bf16[2,448,448]{2,1,0:T(8,128)(2,1)}, bf16[2,448,448]{2,1,0:T(8,128)(2,1)S(1)}, u32[]{:S(2)}, u32[]{:S(2)}) %collective-permute-start.7) | collective-permute-done | bytes 802848 | tf_op jit(solution)/shard_map/ppermute | solution.py:23
  88.8 5.7 convolution_convert_fusion
  94.5 4.4 collective-permute-start.9
  98.9 5.7 copy.49
  108.4 7.7 %collective-permute-done.9 = bf16[1024,448]{0,1:T(8,128)(2,1)} collective-permute-done((bf16[1024,448]{0,1:T(8,128)(2,1)}, bf16[1024,448]{0,1:T(8,128)(2,1)}, u32[]{:S(2)}, u32[]{:S(2)}) %collective-permute-start.9) | collective-permute-done | bytes 917536 | tf_op jit(solution)/shard_map/ppermute | solution.py:26
  116.1 5.3 collective-permute-start.10
  121.4 4.5 collective-permute-done.8
  130.4 7.3 %collective-permute-done.10 = bf16[1024,448]{0,1:T(8,128)(2,1)} collective-permute-done((bf16[1024,448]{0,1:T(8,128)(2,1)}, bf16[1024,448]{0,1:T(8,128)(2,1)}, u32[]{:S(2)}, u32[]{:S(2)}) %collective-permute-start.10) | collective-permute-done | bytes 917536 | tf_op jit(solution)/shard_map/ppermute | solution.py:26
  137.6 5.3 collective-permute-start.11
  143.0 3.7 copy.45
  146.8 3.3 collective-permute-done.13
  151.6 6.7 %collective-permute-done.11 = bf16[1024,448]{0,1:T(8,128)(2,1)} collective-permute-done((bf16[1024,448]{0,1:T(8,128)(2,1)}, bf16[1024,448]{0,1:T(8,128)(2,1)}, u32[]{:S(2)}, u32[]{:S(2)}) %collective-permute-start.11) | collective-permute-done | bytes 917536 | tf_op jit(solution)/shard_map/ppermute | solution.py:26
  171.2 5.4 bitcast_convert_fusion.2
  178.1 5.4 bitcast_convert_fusion.1
  185.1 5.4 bitcast_convert_fusion
  192.8 63.5 %all-reduce = f32[32]{0:T(128)S(1)} all-reduce(f32[32]{0:T(128)S(1)} %dynamic-update-slice), channel_id=2, replica_groups=mesh['dp'=16,'mp'=2] {'dp','mp'}, use_global_device_ids=true, to_apply=%add | all-reduce | flops 32 | bytes 256
  258.6 5.5 fusion.35
  268.0 4.0 copy.46
  274.2 4.1 copy.51
  280.6 7.2 %collective-permute-done.18 = bf16[1024,448]{0,1:T(8,128)(2,1)} collective-permute-done((bf16[1024,448]{0,1:T(8,128)(2,1)S(1)}, bf16[1024,448]{0,1:T(8,128)(2,1)}, u32[]{:S(2)}, u32[]{:S(2)}) %collective-permute-start.18) | collective-permute-done | bytes 917536 | tf_op jit(solution)/shard_map/ppermute | solution.py:23
  287.8 18.6 %collective-permute-done.19 = bf16[1024,448]{0,1:T(8,128)(2,1)} collective-permute-done((bf16[1024,448]{0,1:T(8,128)(2,1)S(1)}, bf16[1024,448]{0,1:T(8,128)(2,1)}, u32[]{:S(2)}, u32[]{:S(2)}) %collective-permute-start.19) | collective-permute-done | bytes 917536 | tf_op jit(solution)/shard_map/ppermute | solution.py:23
  306.4 10.0 %fusion.16 = bf16[4,448,1024]{2,1,0:T(8,128)(2,1)S(1)} fusion(bf16[1024,448]{0,1:T(8,128)(2,1)} %collective-permute-done.20, bf16[1024,448]{0,1:T(8,128)(2,1)} %collective-permute-done.19, bf16[1024,448]{0,1:T(8,128)(2,1)} %collective-permute-done.18, bf16[1024,448]{0,1:T(8,128)(2,1)S(1)} %fusion.35, bf16[4,448,448]{1,2,0:T(8,128)(2,1)} %copy.52, ...), kind=kOutput, calls=%fused_computation.19 | convolution fusion | flops 6618873856 | bytes 13762560 | tf_op jit(solution)/shard_map/dot_general | solution.py:68
  320.9 16.8 %collective-permute-done.21 = bf16[448,1024]{1,0:T(8,128)(2,1)S(1)} collective-permute-done((bf16[448,1024]{1,0:T(8,128)(2,1)S(1)}, bf16[448,1024]{1,0:T(8,128)(2,1)S(1)}, u32[]{:S(2)}, u32[]{:S(2)}) %collective-permute-start.21) | collective-permute-done | bytes 917536 | tf_op jit(solution)/shard_map/ppermute | solution.py:26
  340.1 5.3 collective-permute-start.22
  345.5 6.0 %copy.44 = bf16[512,3584]{0,1:T(8,128)(2,1)} copy(bf16[512,3584]{1,0:T(8,128)(2,1)} %param.12) | data formatting | bytes 7340032 | tf_op args[5]
  351.5 3.8 dynamic-slice_bitcast_fusion.5
  360.8 3.2 add_convert_fusion.1
  365.3 13.6 %collective-permute-done.3 = bf16[2,512,448]{1,2,0:T(8,128)(2,1)S(1)} collective-permute-done((bf16[2,512,448]{1,2,0:T(8,128)(2,1)}, bf16[2,512,448]{1,2,0:T(8,128)(2,1)S(1)}, u32[]{:S(2)}, u32[]{:S(2)}) %collective-permute-start.3) | collective-permute-done | bytes 917536 | tf_op jit(solution)/shard_map/ppermute | solution.py:23
  378.9 16.8 %collective-permute-done.4 = bf16[2,512,448]{1,2,0:T(8,128)(2,1)S(1)} collective-permute-done((bf16[2,512,448]{1,2,0:T(8,128)(2,1)}, bf16[2,512,448]{1,2,0:T(8,128)(2,1)S(1)}, u32[]{:S(2)}, u32[]{:S(2)}) %collective-permute-start.4) | collective-permute-done | bytes 917536 | tf_op jit(solution)/shard_map/ppermute | solution.py:23
  395.7 3.1 pad_maximum_fusion
  402.0 4.6 collective-permute-start.23
  406.6 13.1 %collective-permute-done.25 = bf16[448,1024]{1,0:T(8,128)(2,1)S(1)} collective-permute-done((bf16[448,1024]{1,0:T(8,128)(2,1)S(1)}, bf16[448,1024]{1,0:T(8,128)(2,1)S(1)}, u32[]{:S(2)}, u32[]{:S(2)}) %collective-permute-start.25) | collective-permute-done | bytes 917536 | tf_op jit(solution)/shard_map/ppermute | solution.py:29
  422.5 15.9 %collective-permute-done.26 = bf16[448,1024]{1,0:T(8,128)(2,1)} collective-permute-done((bf16[448,1024]{1,0:T(8,128)(2,1)S(1)}, bf16[448,1024]{1,0:T(8,128)(2,1)}, u32[]{:S(2)}, u32[]{:S(2)}) %collective-permute-start.26) | collective-permute-done | bytes 917536 | tf_op jit(solution)/shard_map/ppermute | solution.py:29
  443.1 14.8 %collective-permute-done.27 = bf16[448,1024]{1,0:T(8,128)(2,1)S(1)} collective-permute-done((bf16[448,1024]{1,0:T(8,128)(2,1)S(1)}, bf16[448,1024]{1,0:T(8,128)(2,1)S(1)}, u32[]{:S(2)}, u32[]{:S(2)}) %collective-permute-start.27) | collective-permute-done | bytes 917536 | tf_op jit(solution)/shard_map/ppermute | solution.py:26
  457.8 5.3 collective-permute-start.28
  463.4 4.4 collective-permute-start.34
  467.8 6.9 %fusion.53 = (bf16[512,1024]{1,0:T(8,128)(2,1)}, f32[512,1024]{1,0:T(8,128)}) fusion(bf16[512,2048]{1,0:T(8,128)(2,1)} %all-gather.10.cloned.1.call-done, bf16[2048,1024]{1,0:T(8,128)(2,1)} %param.8), kind=kOutput, calls=%fused_computation.81 | convolution fusion | flops 2148007936 | bytes 9437184 | tf_op jit(solution)/shard_map/dot_general | solution.py:87
  479.5 5.5 collective-permute-start.29
  485.0 16.1 %collective-permute-done = bf16[512,1024]{1,0:T(8,128)(2,1)} collective-permute-done((bf16[512,1024]{1,0:T(8,128)(2,1)}, bf16[512,1024]{1,0:T(8,128)(2,1)}, u32[]{:S(2)}, u32[]{:S(2)}) %collective-permute-start) | collective-permute-done | bytes 1048608 | tf_op jit(solution)/shard_map/ppermute | solution.py:23
  502.6 11.4 %collective-permute-done.1 = bf16[512,1024]{1,0:T(8,128)(2,1)} collective-permute-done((bf16[512,1024]{1,0:T(8,128)(2,1)}, bf16[512,1024]{1,0:T(8,128)(2,1)}, u32[]{:S(2)}, u32[]{:S(2)}) %collective-permute-start.1) | collective-permute-done | bytes 1048608 | tf_op jit(solution)/shard_map/ppermute | solution.py:23
  531.8 3.4 collective-permute-done.32
  536.1 12.8 %fusion = f32[2048]{0:T(1024)S(1)} fusion(f32[512,1024]{1,0:T(8,128)} %convert_element_type.99, f32[512,1024]{1,0:T(8,128)} %convert_element_type.98, f32[512,1024]{1,0:T(8,128)S(1)} %convert_element_type.97, f32[512,1024]{1,0:T(8,128)} %get-tuple-element.16, bf16[4,2048,448]{1,2,0:T(8,128)(2,1)} %all-gather.12.cloned.1.call-done, ...), kind=kOutput, calls=%fused_computation.1 | convolution fusion | flops 7526676480 | bytes 19406852 | tf_op jit(solution)/shard_map/dot_general | solution.py:98
  549.8 37.7 %all-reduce.1 = f32[1024]{0:T(1024)S(1)} all-reduce(f32[1024]{0:T(1024)S(1)} %dynamic-update-slice.1), channel_id=4, replica_groups=mesh['dp'=16,'mp'=2] {'dp','mp'}, use_global_device_ids=true, to_apply=%add.1 | all-reduce | flops 1024 | bytes 8192
  (126 shorter events, 96.6 us)
Async XLA Ops:
  6.5 82.3 %all-gather.20.cloned.1.call-start = ((), (), s32[]{:S(2)}) async-start(), calls=%async_computation.5 | async-start | bytes 2752512 | tf_op jit(solution)/shard_map/all_gather | solution.py:45
  7.3 164.0 %all-gather.14.cloned.1.call-start = ((), (), s32[]{:S(2)}) async-start(), calls=%async_computation.2 | async-start | bytes 2752512 | tf_op jit(solution)/shard_map/all_gather | solution.py:56
  35.8 23.5 %collective-permute-start.6 = (bf16[2,448,448]{2,1,0:T(8,128)(2,1)}, bf16[2,448,448]{2,1,0:T(8,128)(2,1)S(1)}, u32[]{:S(2)}, u32[]{:S(2)}) collective-permute-start(bf16[2,448,448]{2,1,0:T(8,128)(2,1)} %bitcast.109), channel_id=1, source_target_pairs={{0,2},{2,0},{4,6},{6,4},{8,10},{10,8},{12,14},{14,12},{16,18},{18,... | collective-permute-start | bytes 2408456 | tf_op jit(solution)/shard_map/ppermute | solution.py:23
  60.2 117.9 %all-gather.16.cloned.1.call-start = ((), (), s32[]{:S(2)}) async-start(), calls=%async_computation.3 | async-start | bytes 2752512 | tf_op jit(solution)/shard_map/all_gather | solution.py:56
  66.0 21.7 %collective-permute-start.7 = (bf16[2,448,448]{2,1,0:T(8,128)(2,1)}, bf16[2,448,448]{2,1,0:T(8,128)(2,1)S(1)}, u32[]{:S(2)}, u32[]{:S(2)}) collective-permute-start(bf16[2,448,448]{2,1,0:T(8,128)(2,1)} %bitcast.110), channel_id=1, source_target_pairs={{0,4},{2,6},{4,0},{6,2},{8,12},{10,14},{12,8},{14,10},{16,20},{18,... | collective-permute-start | bytes 2408456 | tf_op jit(solution)/shard_map/ppermute | solution.py:23
  88.8 96.3 %all-gather.18.cloned.1.call-start = ((), (), s32[]{:S(2)}) async-start(), calls=%async_computation.4 | async-start | bytes 2752512 | tf_op jit(solution)/shard_map/all_gather | solution.py:56
  94.5 21.5 %collective-permute-start.9 = (bf16[1024,448]{0,1:T(8,128)(2,1)}, bf16[1024,448]{0,1:T(8,128)(2,1)}, u32[]{:S(2)}, u32[]{:S(2)}) collective-permute-start(bf16[1024,448]{0,1:T(8,128)(2,1)} %convolution_convert_fusion), channel_id=1, source_target_pairs={{0,8},{2,10},{4,12},{6,14},{8,16},{10,18},{12,20},{14,22},{16,24},... | collective-permute-start | bytes 2752520 | tf_op jit(solution)/shard_map/ppermute | solution.py:26
  104.6 21.3 %collective-permute-start.8 = (bf16[2,448,448]{2,1,0:T(8,128)(2,1)}, bf16[2,448,448]{2,1,0:T(8,128)(2,1)S(1)}, u32[]{:S(2)}, u32[]{:S(2)}) collective-permute-start(bf16[2,448,448]{2,1,0:T(8,128)(2,1)} %bitcast.108), channel_id=1, source_target_pairs={{0,6},{2,4},{4,2},{6,0},{8,14},{10,12},{12,10},{14,8},{16,22},{18,... | collective-permute-start | bytes 2408456 | tf_op jit(solution)/shard_map/ppermute | solution.py:23
  107.1 22.0 %collective-permute-start.12 = (bf16[1024,448]{0,1:T(8,128)(2,1)}, bf16[1024,448]{0,1:T(8,128)(2,1)}, u32[]{:S(2)}, u32[]{:S(2)}) collective-permute-start(bf16[1024,448]{0,1:T(8,128)(2,1)} %convolution_convert_fusion), channel_id=1, source_target_pairs={{8,0},{10,2},{12,4},{14,6},{16,8},{18,10},{20,12},{22,14},{24,16},... | collective-permute-start | bytes 2752520 | tf_op jit(solution)/shard_map/ppermute | solution.py:29
  116.1 21.6 %collective-permute-start.10 = (bf16[1024,448]{0,1:T(8,128)(2,1)}, bf16[1024,448]{0,1:T(8,128)(2,1)}, u32[]{:S(2)}, u32[]{:S(2)}) collective-permute-start(bf16[1024,448]{0,1:T(8,128)(2,1)} %collective-permute-done.9), channel_id=1, source_target_pairs={{0,8},{2,10},{4,12},{6,14},{8,16},{10,18},{12,20},{14,22},{16,24},... | collective-permute-start | bytes 2752520 | tf_op jit(solution)/shard_map/ppermute | solution.py:26
  126.8 130.8 %all-gather.22.cloned.1.call-start = ((), (), s32[]{:S(2)}) async-start(), calls=%async_computation.6 | async-start | bytes 2752512 | tf_op jit(solution)/shard_map/all_gather | solution.py:56
  129.1 21.0 %collective-permute-start.13 = (bf16[1024,448]{0,1:T(8,128)(2,1)}, bf16[1024,448]{0,1:T(8,128)(2,1)S(1)}, u32[]{:S(2)}, u32[]{:S(2)}) collective-permute-start(bf16[1024,448]{0,1:T(8,128)(2,1)} %collective-permute-done.12), channel_id=1, source_target_pairs={{8,0},{10,2},{12,4},{14,6},{16,8},{18,10},{20,12},{22,14},{24,16},... | collective-permute-start | bytes 2752520 | tf_op jit(solution)/shard_map/ppermute | solution.py:29
  137.6 20.7 %collective-permute-start.11 = (bf16[1024,448]{0,1:T(8,128)(2,1)}, bf16[1024,448]{0,1:T(8,128)(2,1)}, u32[]{:S(2)}, u32[]{:S(2)}) collective-permute-start(bf16[1024,448]{0,1:T(8,128)(2,1)} %collective-permute-done.10), channel_id=1, source_target_pairs={{0,8},{2,10},{4,12},{6,14},{8,16},{10,18},{12,20},{14,22},{16,24},... | collective-permute-start | bytes 2752520 | tf_op jit(solution)/shard_map/ppermute | solution.py:26
  146.7 321.1 %all-gather.10.cloned.1.call-start = ((), (), s32[]{:S(2)}) async-start(), calls=%async_computation | async-start | bytes 3145728 | tf_op jit(solution)/shard_map/all_gather | solution.py:86
  150.1 20.1 %collective-permute-start.14 = (bf16[1024,448]{0,1:T(8,128)(2,1)S(1)}, bf16[1024,448]{0,1:T(8,128)(2,1)S(1)}, u32[]{:S(2)}, u32[]{:S(2)}) collective-permute-start(bf16[1024,448]{0,1:T(8,128)(2,1)S(1)} %collective-permute-done.13), channel_id=1, source_target_pairs={{8,0},{10,2},{12,4},{14,6},{16,8},{18,10},{20,12},{22,14},{24,16},... | collective-permute-start | bytes 2752520 | tf_op jit(solution)/shard_map/ppermute | solution.py:29
  176.6 81.0 %collective-permute-start.15 = (bf16[1024,448]{0,1:T(8,128)(2,1)}, bf16[1024,448]{0,1:T(8,128)(2,1)S(1)}, u32[]{:S(2)}, u32[]{:S(2)}) collective-permute-start(bf16[1024,448]{0,1:T(8,128)(2,1)} %bitcast_convert_fusion.2), channel_id=1, source_target_pairs={{0,2},{2,0},{4,6},{6,4},{8,10},{10,8},{12,14},{14,12},{16,18},{18,... | collective-permute-start | bytes 2752520 | tf_op jit(solution)/shard_map/ppermute | solution.py:23
  183.5 7.4 %copy-start.3 = (f32[1024,448]{0,1:T(8,128)S(1)}, f32[1024,448]{0,1:T(8,128)}, u32[]{:S(2)}) copy-start(f32[1024,448]{0,1:T(8,128)} %param.10) | copy-start | bytes 5505028
  183.5 74.1 %collective-permute-start.16 = (bf16[1024,448]{0,1:T(8,128)(2,1)}, bf16[1024,448]{0,1:T(8,128)(2,1)}, u32[]{:S(2)}, u32[]{:S(2)}) collective-permute-start(bf16[1024,448]{0,1:T(8,128)(2,1)} %bitcast_convert_fusion.1), channel_id=1, source_target_pairs={{0,4},{2,6},{4,0},{6,2},{8,12},{10,14},{12,8},{14,10},{16,20},{18,... | collective-permute-start | bytes 2752520 | tf_op jit(solution)/shard_map/ppermute | solution.py:23
  190.5 68.1 %collective-permute-start.17 = (bf16[1024,448]{0,1:T(8,128)(2,1)}, bf16[1024,448]{0,1:T(8,128)(2,1)}, u32[]{:S(2)}, u32[]{:S(2)}) collective-permute-start(bf16[1024,448]{0,1:T(8,128)(2,1)} %bitcast_convert_fusion), channel_id=1, source_target_pairs={{0,6},{2,4},{4,2},{6,0},{8,14},{10,12},{12,10},{14,8},{16,22},{18,... | collective-permute-start | bytes 2752520 | tf_op jit(solution)/shard_map/ppermute | solution.py:23
  264.1 7.9 %copy-start.1 = (bf16[4,448,448]{2,1,0:T(8,128)(2,1)S(1)}, bf16[4,448,448]{2,1,0:T(8,128)(2,1)}, u32[]{:S(2)}) copy-start(bf16[4,448,448]{2,1,0:T(8,128)(2,1)} %all-gather.14.cloned.1.call-done) | copy-start | bytes 4816900
  264.1 23.7 %collective-permute-start.18 = (bf16[1024,448]{0,1:T(8,128)(2,1)S(1)}, bf16[1024,448]{0,1:T(8,128)(2,1)}, u32[]{:S(2)}, u32[]{:S(2)}) collective-permute-start(bf16[1024,448]{0,1:T(8,128)(2,1)S(1)} %fusion.35), channel_id=1, source_target_pairs={{0,2},{2,0},{4,6},{6,4},{8,10},{10,8},{12,14},{14,12},{16,18},{18,... | collective-permute-start | bytes 2752520 | tf_op jit(solution)/shard_map/ppermute | solution.py:23
  266.4 40.0 %collective-permute-start.19 = (bf16[1024,448]{0,1:T(8,128)(2,1)S(1)}, bf16[1024,448]{0,1:T(8,128)(2,1)}, u32[]{:S(2)}, u32[]{:S(2)}) collective-permute-start(bf16[1024,448]{0,1:T(8,128)(2,1)S(1)} %fusion.35), channel_id=1, source_target_pairs={{0,4},{2,6},{4,0},{6,2},{8,12},{10,14},{12,8},{14,10},{16,20},{18,... | collective-permute-start | bytes 2752520 | tf_op jit(solution)/shard_map/ppermute | solution.py:23
  267.1 39.3 %collective-permute-start.20 = (bf16[1024,448]{0,1:T(8,128)(2,1)S(1)}, bf16[1024,448]{0,1:T(8,128)(2,1)}, u32[]{:S(2)}, u32[]{:S(2)}) collective-permute-start(bf16[1024,448]{0,1:T(8,128)(2,1)S(1)} %fusion.35), channel_id=1, source_target_pairs={{0,6},{2,4},{4,2},{6,0},{8,14},{10,12},{12,10},{14,8},{16,22},{18,... | collective-permute-start | bytes 2752520 | tf_op jit(solution)/shard_map/ppermute | solution.py:23
  318.4 19.4 %collective-permute-start.21 = (bf16[448,1024]{1,0:T(8,128)(2,1)S(1)}, bf16[448,1024]{1,0:T(8,128)(2,1)S(1)}, u32[]{:S(2)}, u32[]{:S(2)}) collective-permute-start(bf16[448,1024]{1,0:T(8,128)(2,1)S(1)} %dynamic-slice_bitcast_fusion), channel_id=1, source_target_pairs={{0,8},{2,10},{4,12},{6,14},{8,16},{10,18},{12,20},{14,22},{16,24},... | collective-permute-start | bytes 2752520 | tf_op jit(solution)/shard_map/ppermute | solution.py:26
  340.1 20.7 %collective-permute-start.22 = (bf16[448,1024]{1,0:T(8,128)(2,1)}, bf16[448,1024]{1,0:T(8,128)(2,1)}, u32[]{:S(2)}, u32[]{:S(2)}) collective-permute-start(bf16[448,1024]{1,0:T(8,128)(2,1)} %fusion.27), channel_id=1, source_target_pairs={{0,8},{2,10},{4,12},{6,14},{8,16},{10,18},{12,20},{14,22},{16,24},... | collective-permute-start | bytes 2752520 | tf_op jit(solution)/shard_map/ppermute | solution.py:26
  345.5 190.6 %all-gather.12.cloned.1.call-start = ((), (), s32[]{:S(2)}) async-start(), calls=%async_computation.1 | async-start | bytes 11010048 | tf_op jit(solution)/shard_map/all_gather | solution.py:95
  355.4 23.5 %collective-permute-start.3 = (bf16[2,512,448]{1,2,0:T(8,128)(2,1)}, bf16[2,512,448]{1,2,0:T(8,128)(2,1)S(1)}, u32[]{:S(2)}, u32[]{:S(2)}) collective-permute-start(bf16[2,512,448]{1,2,0:T(8,128)(2,1)} %get-tuple-element.14), channel_id=1, source_target_pairs={{0,2},{2,0},{4,6},{6,4},{8,10},{10,8},{12,14},{14,12},{16,18},{18,... | collective-permute-start | bytes 2752520 | tf_op jit(solution)/shard_map/ppermute | solution.py:23
  357.2 38.5 %collective-permute-start.4 = (bf16[2,512,448]{1,2,0:T(8,128)(2,1)}, bf16[2,512,448]{1,2,0:T(8,128)(2,1)S(1)}, u32[]{:S(2)}, u32[]{:S(2)}) collective-permute-start(bf16[2,512,448]{1,2,0:T(8,128)(2,1)} %get-tuple-element.13), channel_id=1, source_target_pairs={{0,4},{2,6},{4,0},{6,2},{8,12},{10,14},{12,8},{14,10},{16,20},{18,... | collective-permute-start | bytes 2752520 | tf_op jit(solution)/shard_map/ppermute | solution.py:23
  357.5 38.3 %collective-permute-start.5 = (bf16[2,512,448]{1,2,0:T(8,128)(2,1)}, bf16[2,512,448]{1,2,0:T(8,128)(2,1)}, u32[]{:S(2)}, u32[]{:S(2)}) collective-permute-start(bf16[2,512,448]{1,2,0:T(8,128)(2,1)} %get-tuple-element.12), channel_id=1, source_target_pairs={{0,6},{2,4},{4,2},{6,0},{8,14},{10,12},{12,10},{14,8},{16,22},{18,... | collective-permute-start | bytes 2752520 | tf_op jit(solution)/shard_map/ppermute | solution.py:23
  364.0 34.8 %collective-permute-start.24 = (bf16[448,1024]{1,0:T(8,128)(2,1)}, bf16[448,1024]{1,0:T(8,128)(2,1)}, u32[]{:S(2)}, u32[]{:S(2)}) collective-permute-start(bf16[448,1024]{1,0:T(8,128)(2,1)} %get-tuple-element.6), channel_id=1, source_target_pairs={{8,0},{10,2},{12,4},{14,6},{16,8},{18,10},{20,12},{22,14},{24,16},... | collective-permute-start | bytes 2752520 | tf_op jit(solution)/shard_map/ppermute | solution.py:29
  400.7 62.5 %copy-start.10 = (s32[512]{0:T(512)S(1)}, s32[512]{0:T(512)}, u32[]{:S(2)}) copy-start(s32[512]{0:T(512)} %param.13) | copy-start | bytes 6148
  400.7 19.0 %collective-permute-start.25 = (bf16[448,1024]{1,0:T(8,128)(2,1)S(1)}, bf16[448,1024]{1,0:T(8,128)(2,1)S(1)}, u32[]{:S(2)}, u32[]{:S(2)}) collective-permute-start(bf16[448,1024]{1,0:T(8,128)(2,1)S(1)} %fusion.28), channel_id=1, source_target_pairs={{8,0},{10,2},{12,4},{14,6},{16,8},{18,10},{20,12},{22,14},{24,16},... | collective-permute-start | bytes 2752520 | tf_op jit(solution)/shard_map/ppermute | solution.py:29
  402.0 20.5 %collective-permute-start.23 = (bf16[448,1024]{1,0:T(8,128)(2,1)S(1)}, bf16[448,1024]{1,0:T(8,128)(2,1)S(1)}, u32[]{:S(2)}, u32[]{:S(2)}) collective-permute-start(bf16[448,1024]{1,0:T(8,128)(2,1)S(1)} %copy-done.9), channel_id=1, source_target_pairs={{0,8},{2,10},{4,12},{6,14},{8,16},{10,18},{12,20},{14,22},{16,24},... | collective-permute-start | bytes 2752520 | tf_op jit(solution)/shard_map/ppermute | solution.py:26
  421.2 17.2 %collective-permute-start.26 = (bf16[448,1024]{1,0:T(8,128)(2,1)S(1)}, bf16[448,1024]{1,0:T(8,128)(2,1)}, u32[]{:S(2)}, u32[]{:S(2)}) collective-permute-start(bf16[448,1024]{1,0:T(8,128)(2,1)S(1)} %add_convert_fusion), channel_id=1, source_target_pairs={{8,0},{10,2},{12,4},{14,6},{16,8},{18,10},{20,12},{22,14},{24,16},... | collective-permute-start | bytes 2752520 | tf_op jit(solution)/shard_map/ppermute | solution.py:29
  440.4 17.5 %collective-permute-start.27 = (bf16[448,1024]{1,0:T(8,128)(2,1)S(1)}, bf16[448,1024]{1,0:T(8,128)(2,1)S(1)}, u32[]{:S(2)}, u32[]{:S(2)}) collective-permute-start(bf16[448,1024]{1,0:T(8,128)(2,1)S(1)} %fusion.31), channel_id=1, source_target_pairs={{0,8},{2,10},{4,12},{6,14},{8,16},{10,18},{12,20},{14,22},{16,24},... | collective-permute-start | bytes 2752520 | tf_op jit(solution)/shard_map/ppermute | solution.py:26
  441.8 36.4 %collective-permute-start.30 = (bf16[448,1024]{1,0:T(8,128)(2,1)S(1)}, bf16[448,1024]{1,0:T(8,128)(2,1)}, u32[]{:S(2)}, u32[]{:S(2)}) collective-permute-start(bf16[448,1024]{1,0:T(8,128)(2,1)S(1)} %fusion.31), channel_id=1, source_target_pairs={{8,0},{10,2},{12,4},{14,6},{16,8},{18,10},{20,12},{22,14},{24,16},... | collective-permute-start | bytes 2752520 | tf_op jit(solution)/shard_map/ppermute | solution.py:29
  457.8 16.9 %copy-start.7 = (bf16[448,1024]{1,0:T(8,128)(2,1)}, bf16[448,1024]{1,0:T(8,128)(2,1)S(1)}, u32[]{:S(2)}) copy-start(bf16[448,1024]{1,0:T(8,128)(2,1)S(1)} %collective-permute-done.27) | copy-start | bytes 2752516
  457.8 21.7 %collective-permute-start.28 = (bf16[448,1024]{1,0:T(8,128)(2,1)S(1)}, bf16[448,1024]{1,0:T(8,128)(2,1)}, u32[]{:S(2)}, u32[]{:S(2)}) collective-permute-start(bf16[448,1024]{1,0:T(8,128)(2,1)S(1)} %collective-permute-done.27), channel_id=1, source_target_pairs={{0,8},{2,10},{4,12},{6,14},{8,16},{10,18},{12,20},{14,22},{16,24},... | collective-permute-start | bytes 2752520 | tf_op jit(solution)/shard_map/ppermute | solution.py:26
  463.2 11.5 %collective-permute-start.33 = (s32[512]{0:T(512)S(1)}, s32[512]{0:T(512)S(1)}, u32[]{:S(2)}, u32[]{:S(2)}) collective-permute-start(s32[512]{0:T(512)S(1)} %copy-done.10), channel_id=1, source_target_pairs={{0,2},{2,0},{4,6},{6,4},{8,10},{10,8},{12,14},{14,12},{16,18},{18,... | collective-permute-start | bytes 6152 | tf_op jit(solution)/shard_map/ppermute | solution.py:23
  463.4 12.7 %collective-permute-start.34 = (s32[512]{0:T(512)S(1)}, s32[512]{0:T(512)S(1)}, u32[]{:S(2)}, u32[]{:S(2)}) collective-permute-start(s32[512]{0:T(512)S(1)} %copy-done.10), channel_id=1, source_target_pairs={{0,4},{2,6},{4,0},{6,2},{8,12},{10,14},{12,8},{14,10},{16,20},{18,... | collective-permute-start | bytes 6152 | tf_op jit(solution)/shard_map/ppermute | solution.py:23
  467.8 10.4 %collective-permute-start.35 = (s32[512]{0:T(512)S(1)}, s32[512]{0:T(512)S(1)}, u32[]{:S(2)}, u32[]{:S(2)}) collective-permute-start(s32[512]{0:T(512)S(1)} %copy-done.10), channel_id=1, source_target_pairs={{0,6},{2,4},{4,2},{6,0},{8,14},{10,12},{12,10},{14,8},{16,22},{18,... | collective-permute-start | bytes 6152 | tf_op jit(solution)/shard_map/ppermute | solution.py:23
  474.7 26.4 %collective-permute-start = (bf16[512,1024]{1,0:T(8,128)(2,1)}, bf16[512,1024]{1,0:T(8,128)(2,1)}, u32[]{:S(2)}, u32[]{:S(2)}) collective-permute-start(bf16[512,1024]{1,0:T(8,128)(2,1)} %get-tuple-element.15), channel_id=1, source_target_pairs={{0,2},{2,0},{4,6},{6,4},{8,10},{10,8},{12,14},{14,12},{16,18},{18,... | collective-permute-start | bytes 3145736 | tf_op jit(solution)/shard_map/ppermute | solution.py:23
  476.2 37.8 %collective-permute-start.1 = (bf16[512,1024]{1,0:T(8,128)(2,1)}, bf16[512,1024]{1,0:T(8,128)(2,1)}, u32[]{:S(2)}, u32[]{:S(2)}) collective-permute-start(bf16[512,1024]{1,0:T(8,128)(2,1)} %get-tuple-element.15), channel_id=1, source_target_pairs={{0,4},{2,6},{4,0},{6,2},{8,12},{10,14},{12,8},{14,10},{16,20},{18,... | collective-permute-start | bytes 3145736 | tf_op jit(solution)/shard_map/ppermute | solution.py:23
  478.2 38.6 %collective-permute-start.2 = (bf16[512,1024]{1,0:T(8,128)(2,1)}, bf16[512,1024]{1,0:T(8,128)(2,1)}, u32[]{:S(2)}, u32[]{:S(2)}) collective-permute-start(bf16[512,1024]{1,0:T(8,128)(2,1)} %get-tuple-element.15), channel_id=1, source_target_pairs={{0,6},{2,4},{4,2},{6,0},{8,14},{10,12},{12,10},{14,8},{16,22},{18,... | collective-permute-start | bytes 3145736 | tf_op jit(solution)/shard_map/ppermute | solution.py:23
  478.2 41.4 %collective-permute-start.31 = (bf16[448,1024]{1,0:T(8,128)(2,1)}, bf16[448,1024]{1,0:T(8,128)(2,1)}, u32[]{:S(2)}, u32[]{:S(2)}) collective-permute-start(bf16[448,1024]{1,0:T(8,128)(2,1)} %collective-permute-done.30), channel_id=1, source_target_pairs={{8,0},{10,2},{12,4},{14,6},{16,8},{18,10},{20,12},{22,14},{24,16},... | collective-permute-start | bytes 2752520 | tf_op jit(solution)/shard_map/ppermute | solution.py:29
  479.5 41.4 %collective-permute-start.29 = (bf16[448,1024]{1,0:T(8,128)(2,1)}, bf16[448,1024]{1,0:T(8,128)(2,1)}, u32[]{:S(2)}, u32[]{:S(2)}) collective-permute-start(bf16[448,1024]{1,0:T(8,128)(2,1)} %collective-permute-done.28), channel_id=1, source_target_pairs={{0,8},{2,10},{4,12},{6,14},{8,16},{10,18},{12,20},{14,22},{16,24},... | collective-permute-start | bytes 2752520 | tf_op jit(solution)/shard_map/ppermute | solution.py:26
  516.8 8.6 %copy-start.8 = (bf16[448,1024]{1,0:T(8,128)(2,1)S(1)}, bf16[448,1024]{1,0:T(8,128)(2,1)}, u32[]{:S(2)}) copy-start(bf16[448,1024]{1,0:T(8,128)(2,1)} %copy-done.7) | copy-start | bytes 2752516
  519.6 15.5 %collective-permute-start.32 = (bf16[448,1024]{1,0:T(8,128)(2,1)}, bf16[448,1024]{1,0:T(8,128)(2,1)S(1)}, u32[]{:S(2)}, u32[]{:S(2)}) collective-permute-start(bf16[448,1024]{1,0:T(8,128)(2,1)} %collective-permute-done.31), channel_id=1, source_target_pairs={{8,0},{10,2},{12,4},{14,6},{16,8},{18,10},{20,12},{22,14},{24,16},... | collective-permute-start | bytes 2752520 | tf_op jit(solution)/shard_map/ppermute | solution.py:29
  (7 other events, 13.0 us)
Sparse Core Ops, SparseCore 0:
  8.9 12.8 all-gather.19
  60.4 11.6 all-gather.13
  88.9 11.3 all-gather.15
  127.0 9.4 all-gather.17
  146.9 9.4 all-gather.21
  345.6 8.2 all-gather.9
  398.9 15.3 all-gather.11

commit v2 on v1

v2 whole, which is shorter than its diff:
```python
import jax
import jax.numpy as jnp
from jax import lax
from jax.experimental.layout import Layout, with_layout_constraint
from jax.sharding import PartitionSpec as P

IN = 4
damping_ratio = 0.1
BF = jnp.bfloat16
F32 = jnp.float32


def on_device(query_grad, basis_in, basis_out, eigen_scales, inputs, out_grads, segment_ids):
    n = lax.axis_size("dp")
    outer = n // IN
    d_in = basis_in.shape[0]
    fc = basis_out.shape[1]
    f_all = fc * n
    tok = inputs.shape[0]
    me = lax.axis_index("dp")
    o, p = me // IN, me % IN

    def swap(v, j):
        return lax.ppermute(v, "dp", [(i, i ^ j) for i in range(n)])

    def right(v):
        return lax.ppermute(v, "dp", [(i, i + IN) for i in range(n - IN)])

    def left(v):
        return lax.ppermute(v, "dp", [(i, i - IN) for i in range(IN, n)])

    def beside(pair, extras):
        moved = [swap(x, j) for x, j in extras]
        return lax.optimization_barrier((pair, moved))

    def line_gather(v, extras):
        rights, lefts = [v], [v]
        moved = []
        for t in range(outer - 1):
            pair = (right(rights[-1]), left(lefts[-1]))
            if t < len(extras):
                pair, arrived = beside(pair, extras[t])
                moved += arrived
            rights.append(pair[0])
            lefts.append(pair[1])
        blocks = [v] + [jnp.where(s <= o, rights[s], lefts[outer - s]) for s in range(1, outer)]
        return blocks, moved

    def sum_over_devices(v):
        v = v + sum(swap(v, j) for j in range(1, IN))
        shifts = [
            lax.ppermute(v, "dp", [(i, (i + s * IN) % n) for i in range(n)])
            for s in range(1, outer)
        ]
        v = v + sum(shifts)
        m = lax.axis_size("mp")
        others = [
            lax.ppermute(v, "mp", [(i, (i + s) % m) for i in range(m)]) for s in range(1, m)
        ]
        return v + sum(others)

    def pick(gathered, s):
        k = (o - s) % outer
        per = gathered.shape[1]
        part = lax.dynamic_index_in_dim(gathered, k // per, axis=0, keepdims=False)
        return lax.dynamic_index_in_dim(part, k % per, axis=0, keepdims=False)

    w_full = lax.all_gather(query_grad, "mp", axis=0, tiled=True)
    u = lax.dot_general(
        basis_in, w_full, (((0,), (0,)), ((), ())), preferred_element_type=F32
    ).astype(BF)
    rows = with_layout_constraint(basis_out, Layout(major_to_minor=(0, 1)))
    rows, u = lax.optimization_barrier((rows, u))
    rows = rows.reshape(-1, IN, fc, fc)
    sends = [lax.dynamic_index_in_dim(rows, p ^ j, axis=1, keepdims=False) for j in range(IN)]
    u_rel, got = line_gather(u, [[(sends[1], 1), (sends[2], 2)], [(sends[3], 3)]])
    got = [sends[0]] + got
    q_all = lax.all_gather(jnp.stack(got, axis=1), "mp", axis=0)
    q_rel = jnp.stack([pick(q_all, s) for s in range(outer)])

    part_sum = jnp.broadcast_to(jnp.sum(eigen_scales), (8, 128))
    damping = damping_ratio * sum_over_devices(part_sum)[:1, :1] / (d_in * f_all)
    u_cat = jnp.concatenate(u_rel, axis=1)
    u_cat, q_rel, damping = lax.optimization_barrier((u_cat, q_rel, damping))

    terms = {}
    for j in (3, 1, 2, 0):
        y = jnp.dot(u_cat, q_rel[:, j].reshape(-1, fc), preferred_element_type=F32)
        terms[j] = swap(y.astype(BF), j).astype(F32) if j else y
    rotated = terms[0] + terms[1] + terms[2] + terms[3]
    rescaled = (rotated / (eigen_scales + damping)).astype(BF)

    res = jnp.stack([swap(rescaled, j) if j else rescaled for j in range(IN)])

    def block(s):
        return lax.dot_general(
            q_rel[s], res, (((0, 2), (0, 2)), ((), ())), preferred_element_type=F32
        )

    x_full = lax.all_gather(inputs, "mp", axis=1, tiled=True)
    proj = jnp.dot(x_full, basis_in, preferred_element_type=F32).astype(BF)
    cols = out_grads.reshape(tok, -1, IN, fc)
    g_sends = [
        lax.dynamic_index_in_dim(cols, p ^ j, axis=2, keepdims=False).transpose(1, 0, 2)
        for j in range(IN)
    ]
    res, proj, g_sends = lax.optimization_barrier((res, proj, g_sends))
    extras = [
        [(g_sends[1], 1), (g_sends[2], 2)],
        [(g_sends[3], 3)],
        [(proj, 1), (proj, 2)],
    ]
    a = b = None
    moved = []
    for t in range(outer - 1):
        va, vb = block(t + 1), block(outer - 1 - t)
        if a is not None:
            va, vb = va + a, vb + b
        a, b = right(va.astype(BF)), left(vb.astype(BF))
        if t < len(extras):
            (a, b), arrived = beside((a, b), extras[t])
            moved += arrived
        a, b = a.astype(F32), b.astype(F32)
    back = (block(0) + a + b).astype(BF)

    g = [g_sends[0]] + moved[:3]
    back_rel, last = line_gather(back, [[(proj, 3)]])
    g_all = lax.all_gather(jnp.concatenate(g, axis=1), "mp", axis=0)
    projs = [proj] + moved[3:] + last
    ids = jnp.concatenate([segment_ids] + [swap(segment_ids, j) for j in range(1, IN)])
    back_rel, projs = lax.optimization_barrier((back_rel, projs))
    proj_all = jnp.concatenate(projs)
    score = 0.0
    for s in range(outer):
        pulled = lax.dot_general(
            pick(g_all, s), back_rel[s], (((1,), (0,)), ((), ())), preferred_element_type=F32
        )
        score = score + jnp.sum(proj_all.astype(F32) * pulled, axis=1)
    seq_count = 2 * n
    onehot = (ids[:, None] == jnp.arange(seq_count, dtype=jnp.int32)[None, :]).astype(F32)
    seq_terms = jnp.dot(score, onehot, precision=lax.Precision.HIGHEST)
    return lax.dynamic_slice_in_dim(sum_over_devices(seq_terms), 2 * me, 2)


def solution(mesh):
    return jax.shard_map(
        on_device,
        mesh=mesh,
        in_specs=(
            P("mp", "dp"),
            P(None, "mp"),
            P("mp", "dp"),
            P("mp", "dp"),
            P("dp", "mp"),
            P("dp", "mp"),
            P("dp"),
        ),
        out_specs=P("dp"),
        check_vma=False,
    )
```

time: 597 us -> 442 us (0.74)
  blocking collectives: 101 us -> 0 us
  local copies, waits for them, and re-layouts: 98.2 us -> 27.4 us
  waiting for transfers between devices: 223 us -> 239 us
  matrix products: 57.7 us -> 51.3 us
    unnamed x2 -> x0, blocking collectives: 101 us -> none
    dynamic_slice x6 -> x3, local copies, waits for them, and re-layouts: 34.8 us -> 4.46 us  [the longest x1 3.62 us: pick(): return lax.dynamic_index_in_dim(part, k % per, axis=0, keepdims=False)]
    ppermute x0 -> x8, waiting for transfers between devices: none -> 21.1 us  [the longest x6 19 us: sum_over_devices(): lax.ppermute(v, 'dp', [(i, (i + s * IN) % n) for i in range(n)])]
    unnamed x41 -> x58, local copies, waits for them, and re-layouts: 35.4 us -> 17.5 us
    ppermute x9, waiting for transfers between devices: 37.8 us -> 22.6 us  [left(): return lax.ppermute(v, 'dp', [(i, i - IN) for i in range(IN, n)])]
    convert_element_type x8 -> x4, other arithmetic: 18.1 us -> 5.06 us  [the longest x3 4.58 us: on_device(): a, b = (right(va.astype(BF)), left(vb.astype(BF)))]
    all_gather x5 -> x0, local copies, waits for them, and re-layouts: 12.7 us -> none  [the longest x4 12.6 us: on_device(): q.append(lax.all_gather(got, 'mp', axis=0, tiled=True))]
    ppermute x18 -> x24, waiting for transfers between devices: 129 us -> 140 us  [swap(): return lax.ppermute(v, 'dp', [(i, i ^ j) for i in range(n)])]
  transfers between devices with their start and end apart: 43 -> 54, of which waited for: 20 -> 36; matrix products, arithmetic and copies ran while one was open for 24% -> 14% of each run, Pallas kernels for 0% -> 0%
where the time goes in v2:
time: 442 us; the launch traced here: 441 us
  waiting for transfers between devices  239 us (54%)
  starting transfers between devices  83.5 us (19%)
  matrix products  51.3 us (12%)
  local copies, waits for them, and re-layouts  27.4 us (6%)
  other arithmetic  25 us (6%)
  between operations  14.6 us (3%)
    ppermute x24, waiting for transfers between devices, swap(): return lax.ppermute(v, 'dp', [(i, i ^ j) for i in range(n)])  140 us
    ppermute x9, waiting for transfers between devices, right(): return lax.ppermute(v, 'dp', [(i, i + IN) for i in range(n - IN)])  45.9 us
    ppermute x9, starting transfers between devices, right(): return lax.ppermute(v, 'dp', [(i, i + IN) for i in range(n - IN)])  32.9 us
    ppermute x24, starting transfers between devices, swap(): return lax.ppermute(v, 'dp', [(i, i ^ j) for i in range(n)])  29.3 us
    ppermute x9, waiting for transfers between devices, left(): return lax.ppermute(v, 'dp', [(i, i - IN) for i in range(IN, n)])  22.6 us
    ppermute x6, waiting for transfers between devices, sum_over_devices(): lax.ppermute(v, 'dp', [(i, (i + s * IN) % n) for i in range(n)])  19 us
    unnamed x58, local copies, waits for them, and re-layouts  17.5 us
    dot_general x4, matrix products, on_device(): lax.dot_general(pick(g_all, s), back_rel[s], (((1,), (0,)), ((), ())), pr...  17.1 us
  transfers between devices with their start and end apart: 54, of which 36 were waited for; matrix products, arithmetic and copies ran while one was open for 14% of the time, Pallas kernels for 0%

profile of v2, /device:TPU:0, one launch (start us, length us, event | category | flops | bytes accessed | tf_op | source)
XLA Modules:
  0.0 440.9 jit_solution(8460930498245267098)
XLA Ops:
  7.3 5.7 %copy.11 = bf16[3584,448]{1,0:T(8,128)(2,1)} copy(bf16[3584,448]{0,1:T(8,128)(2,1)} %param.9) | data formatting | bytes 6422528 | tf_op args[2]
  13.1 8.8 %all-gather.7.cloned.1.call-done = bf16[2048,448]{0,1:T(8,128)(2,1)} async-done(((bf16[1024,448]{0,1:T(8,128)(2,1)}), bf16[2048,448]{0,1:T(8,128)(2,1)}) %all-gather.7.cloned.1.call-update) | async-done | bytes 1835024 | tf_op jit(solution)/shard_map/all_gather | solution.py:68
  21.8 4.9 %convolution_convert_fusion.1 = bf16[1024,448]{0,1:T(8,128)(2,1)S(1)} fusion(bf16[2048,448]{0,1:T(8,128)(2,1)} %all-gather.7.cloned.1.call-done, bf16[2048,1024]{1,0:T(8,128)(2,1)} %param.8), kind=kOutput, calls=%fused_computation.53 | convolution fusion | flops 1879506944 | bytes 6946816 | tf_op jit(solution)/shard_map/dot_general | solution.py:69
  26.8 3.7 collective-permute-start
  35.1 19.3 %collective-permute-done.2 = bf16[2,448,448]{2,1,0:T(8,128)(2,1)S(1)} collective-permute-done((bf16[2,448,448]{2,1,0:T(8,128)(2,1)S(1)}, bf16[2,448,448]{2,1,0:T(8,128)(2,1)S(1)}, u32[]{:S(2)}, u32[]{:S(2)}) %collective-permute-start.2) | collective-permute-done | bytes 802848 | tf_op jit(solution)/shard_map/ppermute | solution.py:24
  55.6 4.3 collective-permute-start.4
  62.8 19.9 %collective-permute-done.6 = bf16[2,448,448]{2,1,0:T(8,128)(2,1)S(1)} collective-permute-done((bf16[2,448,448]{2,1,0:T(8,128)(2,1)S(1)}, bf16[2,448,448]{2,1,0:T(8,128)(2,1)S(1)}, u32[]{:S(2)}, u32[]{:S(2)}) %collective-permute-start.6) | collective-permute-done | bytes 802848 | tf_op jit(solution)/shard_map/ppermute | solution.py:24
  83.9 2.1 pad_maximum_fusion.3
  86.1 5.3 %collective-permute-start.8 = (bf16[1024,448]{0,1:T(8,128)(2,1)}, bf16[1024,448]{0,1:T(8,128)(2,1)}, u32[]{:S(2)}, u32[]{:S(2)}) collective-permute-start(bf16[1024,448]{0,1:T(8,128)(2,1)} %copy-done.10), channel_id=1, source_target_pairs={{0,8},{2,10},{4,12},{6,14},{8,16},{10,18},{12,20},{14,22},{16,24},... | collective-permute-start | bytes 2752520 | tf_op jit(solution)/shard_map/ppermute | solution.py:27
  100.5 2.9 collective-permute-start.14
  104.0 13.4 %collective-permute-done.14 = f32[8,128]{1,0:T(8,128)S(1)} collective-permute-done((f32[8,128]{1,0:T(8,128)S(1)}, f32[8,128]{1,0:T(8,128)S(1)}, u32[]{:S(2)}, u32[]{:S(2)}) %collective-permute-start.14) | collective-permute-done | bytes 4128 | tf_op jit(solution)/shard_map/ppermute | solution.py:52
  124.6 2.2 pad_maximum_fusion.2
  126.9 3.6 dynamic-slice_bitcast_fusion.3
  132.4 3.1 copy-done
  145.9 16.7 %collective-permute-done.18 = bf16[1024,448]{0,1:T(8,128)(2,1)S(1)} collective-permute-done((bf16[1024,448]{0,1:T(8,128)(2,1)S(1)}, bf16[1024,448]{0,1:T(8,128)(2,1)S(1)}, u32[]{:S(2)}, u32[]{:S(2)}) %collective-permute-start.18) | collective-permute-done | bytes 917536 | tf_op jit(solution)/shard_map/ppermute | solution.py:24
  162.6 18.8 %collective-permute-done.17 = bf16[1024,448]{0,1:T(8,128)(2,1)S(1)} collective-permute-done((bf16[1024,448]{0,1:T(8,128)(2,1)S(1)}, bf16[1024,448]{0,1:T(8,128)(2,1)S(1)}, u32[]{:S(2)}, u32[]{:S(2)}) %collective-permute-start.17) | collective-permute-done | bytes 917536 | tf_op jit(solution)/shard_map/ppermute | solution.py:24
  181.5 3.2 divide_convert_fusion
  188.2 5.8 %copy.12 = bf16[512,3584]{0,1:T(8,128)(2,1)} copy(bf16[512,3584]{1,0:T(8,128)(2,1)} %param.12) | data formatting | bytes 7340032 | tf_op args[5]
  194.0 3.7 dynamic-slice_bitcast_fusion.4
  197.7 6.2 %convolution_convert_fusion = bf16[512,1024]{1,0:T(8,128)(2,1)} fusion(bf16[512,2048]{1,0:T(8,128)(2,1)} %all-gather.9.cloned.1.call-done, bf16[2048,1024]{1,0:T(8,128)(2,1)} %param.8), kind=kOutput, calls=%fused_computation.52 | convolution fusion | flops 2148007936 | bytes 7340032 | tf_op jit(solution)/shard_map/dot_general | solution.py:101
  203.9 5.2 %collective-permute-done.21 = bf16[1024,448]{0,1:T(8,128)(2,1)S(1)} collective-permute-done((bf16[1024,448]{0,1:T(8,128)(2,1)}, bf16[1024,448]{0,1:T(8,128)(2,1)S(1)}, u32[]{:S(2)}, u32[]{:S(2)}) %collective-permute-start.21) | collective-permute-done | bytes 917536 | tf_op jit(solution)/shard_map/ppermute | solution.py:24
  209.1 18.6 %collective-permute-done.20 = bf16[1024,448]{0,1:T(8,128)(2,1)S(1)} collective-permute-done((bf16[1024,448]{0,1:T(8,128)(2,1)}, bf16[1024,448]{0,1:T(8,128)(2,1)S(1)}, u32[]{:S(2)}, u32[]{:S(2)}) %collective-permute-start.20) | collective-permute-done | bytes 917536 | tf_op jit(solution)/shard_map/ppermute | solution.py:24
  227.8 2.1 pad_maximum_fusion.4
  229.9 6.0 %bitcast_convert_fusion.1 = (bf16[448,1024]{1,0:T(8,128)(2,1)S(1)}, f32[448,1024,1]{1,0,2:T(8,128)}) fusion(bf16[4,1024,448]{1,2,0:T(8,128)(2,1)S(1)} %pad_maximum_fusion.4, bf16[4,4,448,448]{3,2,1,0:T(8,128)(2,1)} %copy-done), kind=kOutput, calls=%fused_computation.30 | convolution fusion | flops 1644625920 | bytes 8257536 | tf_op jit(solution)/shard_map/dot_general | solution.py:96
  245.8 13.2 %collective-permute-done.22 = bf16[448,1024]{1,0:T(8,128)(2,1)S(1)} collective-permute-done((bf16[448,1024]{1,0:T(8,128)(2,1)S(1)}, bf16[448,1024]{1,0:T(8,128)(2,1)S(1)}, u32[]{:S(2)}, u32[]{:S(2)}) %collective-permute-start.22) | collective-permute-done | bytes 917536 | tf_op jit(solution)/shard_map/ppermute | solution.py:27
  259.1 4.2 collective-permute-done.23
  263.7 19.0 %collective-permute-done.25 = bf16[2,512,448]{1,2,0:T(8,128)(2,1)S(1)} collective-permute-done((bf16[2,512,448]{1,2,0:T(8,128)(2,1)S(1)}, bf16[2,512,448]{1,2,0:T(8,128)(2,1)S(1)}, u32[]{:S(2)}, u32[]{:S(2)}) %collective-permute-start.25) | collective-permute-done | bytes 917536 | tf_op jit(solution)/shard_map/ppermute | solution.py:24
  283.3 5.2 %collective-permute-start.26 = (bf16[448,1024]{1,0:T(8,128)(2,1)S(1)}, bf16[448,1024]{1,0:T(8,128)(2,1)}, u32[]{:S(2)}, u32[]{:S(2)}) collective-permute-start(bf16[448,1024]{1,0:T(8,128)(2,1)S(1)} %get-tuple-element.102), channel_id=1, source_target_pairs={{0,8},{2,10},{4,12},{6,14},{8,16},{10,18},{12,20},{14,22},{16,24},... | collective-permute-start | bytes 2752520 | tf_op jit(solution)/shard_map/ppermute | solution.py:27
  289.8 15.6 %collective-permute-done.26 = bf16[448,1024]{1,0:T(8,128)(2,1)} collective-permute-done((bf16[448,1024]{1,0:T(8,128)(2,1)S(1)}, bf16[448,1024]{1,0:T(8,128)(2,1)}, u32[]{:S(2)}, u32[]{:S(2)}) %collective-permute-start.26) | collective-permute-done | bytes 917536 | tf_op jit(solution)/shard_map/ppermute | solution.py:27
  305.5 5.1 %collective-permute-done.27 = bf16[448,1024]{1,0:T(8,128)(2,1)} collective-permute-done((bf16[448,1024]{1,0:T(8,128)(2,1)S(1)}, bf16[448,1024]{1,0:T(8,128)(2,1)}, u32[]{:S(2)}, u32[]{:S(2)}) %collective-permute-start.27) | collective-permute-done | bytes 917536 | tf_op jit(solution)/shard_map/ppermute | solution.py:30
  310.5 2.1 pad_maximum_fusion.5
  314.1 2.4 fusion.15
  320.9 2.0 collective-permute-start.35
  322.9 3.9 fusion.20
  327.7 12.6 %collective-permute-done.32 = bf16[512,1024]{1,0:T(8,128)(2,1)S(1)} collective-permute-done((bf16[512,1024]{1,0:T(8,128)(2,1)}, bf16[512,1024]{1,0:T(8,128)(2,1)S(1)}, u32[]{:S(2)}, u32[]{:S(2)}) %collective-permute-start.32) | collective-permute-done | bytes 1048608 | tf_op jit(solution)/shard_map/ppermute | solution.py:24
  343.7 16.3 %collective-permute-done.33 = bf16[448,1024]{1,0:T(8,128)(2,1)S(1)} collective-permute-done((bf16[448,1024]{1,0:T(8,128)(2,1)S(1)}, bf16[448,1024]{1,0:T(8,128)(2,1)S(1)}, u32[]{:S(2)}, u32[]{:S(2)}) %collective-permute-start.33) | collective-permute-done | bytes 917536 | tf_op jit(solution)/shard_map/ppermute | solution.py:27
  360.0 2.7 collective-permute-done.34
  363.9 4.6 %collective-permute-start.38 = (bf16[448,1024]{1,0:T(8,128)(2,1)S(1)}, bf16[448,1024]{1,0:T(8,128)(2,1)S(1)}, u32[]{:S(2)}, u32[]{:S(2)}) collective-permute-start(bf16[448,1024]{1,0:T(8,128)(2,1)S(1)} %collective-permute-done.33), channel_id=1, source_target_pairs={{0,8},{2,10},{4,12},{6,14},{8,16},{10,18},{12,20},{14,22},{16,24},... | collective-permute-start | bytes 2752520 | tf_op jit(solution)/shard_map/ppermute | solution.py:27
  368.6 10.5 %collective-permute-done.36 = bf16[448,1024]{1,0:T(8,128)(2,1)} collective-permute-done((bf16[448,1024]{1,0:T(8,128)(2,1)S(1)}, bf16[448,1024]{1,0:T(8,128)(2,1)}, u32[]{:S(2)}, u32[]{:S(2)}) %collective-permute-start.36) | collective-permute-done | bytes 917536 | tf_op jit(solution)/shard_map/ppermute | solution.py:30
  381.1 5.3 %collective-permute-start.39 = (bf16[448,1024]{1,0:T(8,128)(2,1)S(1)}, bf16[448,1024]{1,0:T(8,128)(2,1)}, u32[]{:S(2)}, u32[]{:S(2)}) collective-permute-start(bf16[448,1024]{1,0:T(8,128)(2,1)S(1)} %collective-permute-done.38), channel_id=1, source_target_pairs={{0,8},{2,10},{4,12},{6,14},{8,16},{10,18},{12,20},{14,22},{16,24},... | collective-permute-start | bytes 2752520 | tf_op jit(solution)/shard_map/ppermute | solution.py:27
  392.3 2.2 broadcast_select_fusion.1
  394.7 2.2 broadcast_select_fusion.2
  397.0 5.3 %fusion.3 = f32[2048]{0:T(1024)S(1)} fusion(bf16[448,1024]{1,0:T(8,128)(2,1)S(1)} %broadcast_select_fusion, bf16[2,2,2048,448]{2,3,1,0:T(8,128)(2,1)} %bitcast.136, s32[]{:T(128)S(6)} %select_n.224, s32[]{:T(128)S(6)} %select_n.227, bf16[512,1024]{1,0:T(8,128)(2,1)} %copy-done.24, bf16[512,1024]{1,0:T(8,128)(2,1)} %copy-done.22, ...), kind=kOutput, calls=%fused_computation.7 | convolution fusion | flops 1900017664 | bytes 6955016 | tf_op jit(solution)/shard_map/dot_general | solution.py:135
  403.0 3.9 fusion.2
  407.0 4.0 fusion
  410.9 3.9 fusion.1
  421.9 5.4 %collective-permute-start.48 = (f32[32]{0:T(128)S(1)}, f32[32]{0:T(128)S(1)}, u32[]{:S(2)}, u32[]{:S(2)}) collective-permute-start(f32[32]{0:T(128)S(1)} %add_add_fusion.4), channel_id=1, source_target_pairs={{0,24},{2,26},{4,28},{6,30},{8,0},{10,2},{12,4},{14,6},{16,8},{18,... | collective-permute-start | bytes 392 | tf_op jit(solution)/shard_map/ppermute | solution.py:52
  428.5 4.0 collective-permute-done.46
  (169 shorter events, 85.1 us)
Async XLA Ops:
  6.5 15.3 %all-gather.7.cloned.1.call-start = ((), (), s32[]{:S(2)}) async-start(), calls=%async_computation | async-start | bytes 2752512 | tf_op jit(solution)/shard_map/all_gather | solution.py:68
  7.3 119.6 %all-gather.11.cloned.1.call-start = ((), (), s32[]{:S(2)}) async-start(), calls=%async_computation.2 | async-start | bytes 11010048 | tf_op jit(solution)/shard_map/all_gather | solution.py:78
  26.8 28.8 %collective-permute-start = (bf16[1024,448]{0,1:T(8,128)(2,1)S(1)}, bf16[1024,448]{0,1:T(8,128)(2,1)S(1)}, u32[]{:S(2)}, u32[]{:S(2)}) collective-permute-start(bf16[1024,448]{0,1:T(8,128)(2,1)S(1)} %convolution_convert_fusion.1), channel_id=1, source_target_pairs={{0,8},{2,10},{4,12},{6,14},{8,16},{10,18},{12,20},{14,22},{16,24},... | collective-permute-start | bytes 2752520 | tf_op jit(solution)/shard_map/ppermute | solution.py:27
  30.5 25.1 %collective-permute-start.1 = (bf16[1024,448]{0,1:T(8,128)(2,1)S(1)}, bf16[1024,448]{0,1:T(8,128)(2,1)S(1)}, u32[]{:S(2)}, u32[]{:S(2)}) collective-permute-start(bf16[1024,448]{0,1:T(8,128)(2,1)S(1)} %convolution_convert_fusion.1), channel_id=1, source_target_pairs={{8,0},{10,2},{12,4},{14,6},{16,8},{18,10},{20,12},{22,14},{24,16},... | collective-permute-start | bytes 2752520 | tf_op jit(solution)/shard_map/ppermute | solution.py:30
  32.1 22.3 %collective-permute-start.2 = (bf16[2,448,448]{2,1,0:T(8,128)(2,1)S(1)}, bf16[2,448,448]{2,1,0:T(8,128)(2,1)S(1)}, u32[]{:S(2)}, u32[]{:S(2)}) collective-permute-start(bf16[2,448,448]{2,1,0:T(8,128)(2,1)S(1)} %get-tuple-element.100), channel_id=1, source_target_pairs={{0,2},{2,0},{4,6},{6,4},{8,10},{10,8},{12,14},{14,12},{16,18},{18,... | collective-permute-start | bytes 2408456 | tf_op jit(solution)/shard_map/ppermute | solution.py:24
  33.6 22.0 %collective-permute-start.3 = (bf16[2,448,448]{2,1,0:T(8,128)(2,1)S(1)}, bf16[2,448,448]{2,1,0:T(8,128)(2,1)S(1)}, u32[]{:S(2)}, u32[]{:S(2)}) collective-permute-start(bf16[2,448,448]{2,1,0:T(8,128)(2,1)S(1)} %get-tuple-element.99), channel_id=1, source_target_pairs={{0,4},{2,6},{4,0},{6,2},{8,12},{10,14},{12,8},{14,10},{16,20},{18,... | collective-permute-start | bytes 2408456 | tf_op jit(solution)/shard_map/ppermute | solution.py:24
  55.6 27.1 %collective-permute-start.4 = (bf16[1024,448]{0,1:T(8,128)(2,1)S(1)}, bf16[1024,448]{0,1:T(8,128)(2,1)S(1)}, u32[]{:S(2)}, u32[]{:S(2)}) collective-permute-start(bf16[1024,448]{0,1:T(8,128)(2,1)S(1)} %collective-permute-done), channel_id=1, source_target_pairs={{0,8},{2,10},{4,12},{6,14},{8,16},{10,18},{12,20},{14,22},{16,24},... | collective-permute-start | bytes 2752520 | tf_op jit(solution)/shard_map/ppermute | solution.py:27
  59.9 22.8 %collective-permute-start.5 = (bf16[1024,448]{0,1:T(8,128)(2,1)S(1)}, bf16[1024,448]{0,1:T(8,128)(2,1)S(1)}, u32[]{:S(2)}, u32[]{:S(2)}) collective-permute-start(bf16[1024,448]{0,1:T(8,128)(2,1)S(1)} %collective-permute-done.1), channel_id=1, source_target_pairs={{8,0},{10,2},{12,4},{14,6},{16,8},{18,10},{20,12},{22,14},{24,16},... | collective-permute-start | bytes 2752520 | tf_op jit(solution)/shard_map/ppermute | solution.py:30
  61.2 21.5 %collective-permute-start.6 = (bf16[2,448,448]{2,1,0:T(8,128)(2,1)S(1)}, bf16[2,448,448]{2,1,0:T(8,128)(2,1)S(1)}, u32[]{:S(2)}, u32[]{:S(2)}) collective-permute-start(bf16[2,448,448]{2,1,0:T(8,128)(2,1)S(1)} %get-tuple-element.98), channel_id=1, source_target_pairs={{0,6},{2,4},{4,2},{6,0},{8,14},{10,12},{12,10},{14,8},{16,22},{18,... | collective-permute-start | bytes 2408456 | tf_op jit(solution)/shard_map/ppermute | solution.py:24
  86.1 111.6 %all-gather.9.cloned.1.call-start = ((), (), s32[]{:S(2)}) async-start(), calls=%async_computation.1 | async-start | bytes 3145728 | tf_op jit(solution)/shard_map/all_gather | solution.py:100
  86.1 35.9 %collective-permute-start.8 = (bf16[1024,448]{0,1:T(8,128)(2,1)}, bf16[1024,448]{0,1:T(8,128)(2,1)}, u32[]{:S(2)}, u32[]{:S(2)}) collective-permute-start(bf16[1024,448]{0,1:T(8,128)(2,1)} %copy-done.10), channel_id=1, source_target_pairs={{0,8},{2,10},{4,12},{6,14},{8,16},{10,18},{12,20},{14,22},{16,24},... | collective-permute-start | bytes 2752520 | tf_op jit(solution)/shard_map/ppermute | solution.py:27
  93.2 4.9 %collective-permute-start.11 = (f32[8,128]{1,0:T(8,128)S(1)}, f32[8,128]{1,0:T(8,128)S(1)}, u32[]{:S(2)}, u32[]{:S(2)}) collective-permute-start(f32[8,128]{1,0:T(8,128)S(1)} %broadcast_in_dim.2), channel_id=1, source_target_pairs={{0,6},{2,4},{4,2},{6,0},{8,14},{10,12},{12,10},{14,8},{16,22},{18,... | collective-permute-start | bytes 12296 | tf_op jit(solution)/shard_map/ppermute | solution.py:24
  94.8 3.6 collective-permute-start.9
  96.8 300.2 %all-gather.13.cloned.1.call-start = ((), (), s32[]{:S(2)}) async-start(), calls=%async_computation.3 | async-start | bytes 11010048 | tf_op jit(solution)/shard_map/all_gather | solution.py:128
  96.8 26.4 %collective-permute-start.7 = (bf16[1024,448]{0,1:T(8,128)(2,1)}, bf16[1024,448]{0,1:T(8,128)(2,1)}, u32[]{:S(2)}, u32[]{:S(2)}) collective-permute-start(bf16[1024,448]{0,1:T(8,128)(2,1)} %copy-done.9), channel_id=1, source_target_pairs={{8,0},{10,2},{12,4},{14,6},{16,8},{18,10},{20,12},{22,14},{24,16},... | collective-permute-start | bytes 2752520 | tf_op jit(solution)/shard_map/ppermute | solution.py:30
  100.5 16.9 %collective-permute-start.14 = (f32[8,128]{1,0:T(8,128)S(1)}, f32[8,128]{1,0:T(8,128)S(1)}, u32[]{:S(2)}, u32[]{:S(2)}) collective-permute-start(f32[8,128]{1,0:T(8,128)S(1)} %add_add_fusion.2), channel_id=1, source_target_pairs={{0,24},{2,26},{4,28},{6,30},{8,0},{10,2},{12,4},{14,6},{16,8},{18,... | collective-permute-start | bytes 12296 | tf_op jit(solution)/shard_map/ppermute | solution.py:52
  103.4 14.9 %collective-permute-start.12 = (f32[8,128]{1,0:T(8,128)S(1)}, f32[8,128]{1,0:T(8,128)S(1)}, u32[]{:S(2)}, u32[]{:S(2)}) collective-permute-start(f32[8,128]{1,0:T(8,128)S(1)} %add_add_fusion.2), channel_id=1, source_target_pairs={{0,8},{2,10},{4,12},{6,14},{8,16},{10,18},{12,20},{14,22},{16,24},... | collective-permute-start | bytes 12296 | tf_op jit(solution)/shard_map/ppermute | solution.py:52
  103.4 14.9 %collective-permute-start.13 = (f32[8,128]{1,0:T(8,128)S(1)}, f32[8,128]{1,0:T(8,128)S(1)}, u32[]{:S(2)}, u32[]{:S(2)}) collective-permute-start(f32[8,128]{1,0:T(8,128)S(1)} %add_add_fusion.2), channel_id=1, source_target_pairs={{0,16},{2,18},{4,20},{6,22},{8,24},{10,26},{12,28},{14,30},{16,0},... | collective-permute-start | bytes 12296 | tf_op jit(solution)/shard_map/ppermute | solution.py:52
  138.4 24.2 %collective-permute-start.18 = (bf16[1024,448]{0,1:T(8,128)(2,1)S(1)}, bf16[1024,448]{0,1:T(8,128)(2,1)S(1)}, u32[]{:S(2)}, u32[]{:S(2)}) collective-permute-start(bf16[1024,448]{0,1:T(8,128)(2,1)S(1)} %convolution_convert_fusion.2), channel_id=1, source_target_pairs={{0,6},{2,4},{4,2},{6,0},{8,14},{10,12},{12,10},{14,8},{16,22},{18,... | collective-permute-start | bytes 2752520 | tf_op jit(solution)/shard_map/ppermute | solution.py:24
  141.9 39.5 %collective-permute-start.17 = (bf16[1024,448]{0,1:T(8,128)(2,1)S(1)}, bf16[1024,448]{0,1:T(8,128)(2,1)S(1)}, u32[]{:S(2)}, u32[]{:S(2)}) collective-permute-start(bf16[1024,448]{0,1:T(8,128)(2,1)S(1)} %convolution_convert_fusion.3), channel_id=1, source_target_pairs={{0,4},{2,6},{4,0},{6,2},{8,12},{10,14},{12,8},{14,10},{16,20},{18,... | collective-permute-start | bytes 2752520 | tf_op jit(solution)/shard_map/ppermute | solution.py:24
  144.5 37.0 %collective-permute-start.16 = (bf16[1024,448]{0,1:T(8,128)(2,1)S(1)}, bf16[1024,448]{0,1:T(8,128)(2,1)S(1)}, u32[]{:S(2)}, u32[]{:S(2)}) collective-permute-start(bf16[1024,448]{0,1:T(8,128)(2,1)S(1)} %convolution_convert_fusion.4), channel_id=1, source_target_pairs={{0,2},{2,0},{4,6},{6,4},{8,10},{10,8},{12,14},{14,12},{16,18},{18,... | collective-permute-start | bytes 2752520 | tf_op jit(solution)/shard_map/ppermute | solution.py:24
  184.7 24.4 %collective-permute-start.21 = (bf16[1024,448]{0,1:T(8,128)(2,1)}, bf16[1024,448]{0,1:T(8,128)(2,1)S(1)}, u32[]{:S(2)}, u32[]{:S(2)}) collective-permute-start(bf16[1024,448]{0,1:T(8,128)(2,1)} %divide_convert_fusion), channel_id=1, source_target_pairs={{0,6},{2,4},{4,2},{6,0},{8,14},{10,12},{12,10},{14,8},{16,22},{18,... | collective-permute-start | bytes 2752520 | tf_op jit(solution)/shard_map/ppermute | solution.py:24
  186.2 41.5 %collective-permute-start.20 = (bf16[1024,448]{0,1:T(8,128)(2,1)}, bf16[1024,448]{0,1:T(8,128)(2,1)S(1)}, u32[]{:S(2)}, u32[]{:S(2)}) collective-permute-start(bf16[1024,448]{0,1:T(8,128)(2,1)} %divide_convert_fusion), channel_id=1, source_target_pairs={{0,4},{2,6},{4,0},{6,2},{8,12},{10,14},{12,8},{14,10},{16,20},{18,... | collective-permute-start | bytes 2752520 | tf_op jit(solution)/shard_map/ppermute | solution.py:24
  186.8 41.0 %collective-permute-start.19 = (bf16[1024,448]{0,1:T(8,128)(2,1)}, bf16[1024,448]{0,1:T(8,128)(2,1)}, u32[]{:S(2)}, u32[]{:S(2)}) collective-permute-start(bf16[1024,448]{0,1:T(8,128)(2,1)} %divide_convert_fusion), channel_id=1, source_target_pairs={{0,2},{2,0},{4,6},{6,4},{8,10},{10,8},{12,14},{14,12},{16,18},{18,... | collective-permute-start | bytes 2752520 | tf_op jit(solution)/shard_map/ppermute | solution.py:24
  237.8 21.3 %collective-permute-start.22 = (bf16[448,1024]{1,0:T(8,128)(2,1)S(1)}, bf16[448,1024]{1,0:T(8,128)(2,1)S(1)}, u32[]{:S(2)}, u32[]{:S(2)}) collective-permute-start(bf16[448,1024]{1,0:T(8,128)(2,1)S(1)} %get-tuple-element.103), channel_id=1, source_target_pairs={{0,8},{2,10},{4,12},{6,14},{8,16},{10,18},{12,20},{14,22},{16,24},... | collective-permute-start | bytes 2752520 | tf_op jit(solution)/shard_map/ppermute | solution.py:27
  239.1 24.1 %collective-permute-start.23 = (bf16[448,1024]{1,0:T(8,128)(2,1)S(1)}, bf16[448,1024]{1,0:T(8,128)(2,1)S(1)}, u32[]{:S(2)}, u32[]{:S(2)}) collective-permute-start(bf16[448,1024]{1,0:T(8,128)(2,1)S(1)} %get-tuple-element.105), channel_id=1, source_target_pairs={{8,0},{10,2},{12,4},{14,6},{16,8},{18,10},{20,12},{22,14},{24,16},... | collective-permute-start | bytes 2752520 | tf_op jit(solution)/shard_map/ppermute | solution.py:30
  240.4 23.3 %collective-permute-start.24 = (bf16[2,512,448]{1,2,0:T(8,128)(2,1)S(1)}, bf16[2,512,448]{1,2,0:T(8,128)(2,1)S(1)}, u32[]{:S(2)}, u32[]{:S(2)}) collective-permute-start(bf16[2,512,448]{1,2,0:T(8,128)(2,1)S(1)} %copy-done.17), channel_id=1, source_target_pairs={{0,2},{2,0},{4,6},{6,4},{8,10},{10,8},{12,14},{14,12},{16,18},{18,... | collective-permute-start | bytes 2752520 | tf_op jit(solution)/shard_map/ppermute | solution.py:24
  241.1 41.6 %collective-permute-start.25 = (bf16[2,512,448]{1,2,0:T(8,128)(2,1)S(1)}, bf16[2,512,448]{1,2,0:T(8,128)(2,1)S(1)}, u32[]{:S(2)}, u32[]{:S(2)}) collective-permute-start(bf16[2,512,448]{1,2,0:T(8,128)(2,1)S(1)} %copy-done.16), channel_id=1, source_target_pairs={{0,4},{2,6},{4,0},{6,2},{8,12},{10,14},{12,8},{14,10},{16,20},{18,... | collective-permute-start | bytes 2752520 | tf_op jit(solution)/shard_map/ppermute | solution.py:24
  242.5 47.4 %collective-permute-start.28 = (bf16[2,512,448]{1,2,0:T(8,128)(2,1)S(1)}, bf16[2,512,448]{1,2,0:T(8,128)(2,1)S(1)}, u32[]{:S(2)}, u32[]{:S(2)}) collective-permute-start(bf16[2,512,448]{1,2,0:T(8,128)(2,1)S(1)} %copy-done.15), channel_id=1, source_target_pairs={{0,6},{2,4},{4,2},{6,0},{8,14},{10,12},{12,10},{14,8},{16,22},{18,... | collective-permute-start | bytes 2752520 | tf_op jit(solution)/shard_map/ppermute | solution.py:24
  283.3 22.1 %collective-permute-start.26 = (bf16[448,1024]{1,0:T(8,128)(2,1)S(1)}, bf16[448,1024]{1,0:T(8,128)(2,1)}, u32[]{:S(2)}, u32[]{:S(2)}) collective-permute-start(bf16[448,1024]{1,0:T(8,128)(2,1)S(1)} %get-tuple-element.102), channel_id=1, source_target_pairs={{0,8},{2,10},{4,12},{6,14},{8,16},{10,18},{12,20},{14,22},{16,24},... | collective-permute-start | bytes 2752520 | tf_op jit(solution)/shard_map/ppermute | solution.py:27
  288.5 22.0 %collective-permute-start.27 = (bf16[448,1024]{1,0:T(8,128)(2,1)S(1)}, bf16[448,1024]{1,0:T(8,128)(2,1)}, u32[]{:S(2)}, u32[]{:S(2)}) collective-permute-start(bf16[448,1024]{1,0:T(8,128)(2,1)S(1)} %get-tuple-element.101), channel_id=1, source_target_pairs={{8,0},{10,2},{12,4},{14,6},{16,8},{18,10},{20,12},{22,14},{24,16},... | collective-permute-start | bytes 2752520 | tf_op jit(solution)/shard_map/ppermute | solution.py:30
  312.6 15.1 %collective-permute-start.31 = (bf16[512,1024]{1,0:T(8,128)(2,1)}, bf16[512,1024]{1,0:T(8,128)(2,1)S(1)}, u32[]{:S(2)}, u32[]{:S(2)}) collective-permute-start(bf16[512,1024]{1,0:T(8,128)(2,1)} %convolution_convert_fusion), channel_id=1, source_target_pairs={{0,2},{2,0},{4,6},{6,4},{8,10},{10,8},{12,14},{14,12},{16,18},{18,... | collective-permute-start | bytes 3145736 | tf_op jit(solution)/shard_map/ppermute | solution.py:24
  314.0 26.2 %collective-permute-start.32 = (bf16[512,1024]{1,0:T(8,128)(2,1)}, bf16[512,1024]{1,0:T(8,128)(2,1)S(1)}, u32[]{:S(2)}, u32[]{:S(2)}) collective-permute-start(bf16[512,1024]{1,0:T(8,128)(2,1)} %convolution_convert_fusion), channel_id=1, source_target_pairs={{0,4},{2,6},{4,0},{6,2},{8,12},{10,14},{12,8},{14,10},{16,20},{18,... | collective-permute-start | bytes 3145736 | tf_op jit(solution)/shard_map/ppermute | solution.py:24
  316.4 23.9 %collective-permute-start.29 = (bf16[448,1024]{1,0:T(8,128)(2,1)S(1)}, bf16[448,1024]{1,0:T(8,128)(2,1)S(1)}, u32[]{:S(2)}, u32[]{:S(2)}) collective-permute-start(bf16[448,1024]{1,0:T(8,128)(2,1)S(1)} %fusion.15), channel_id=1, source_target_pairs={{0,8},{2,10},{4,12},{6,14},{8,16},{10,18},{12,20},{14,22},{16,24},... | collective-permute-start | bytes 2752520 | tf_op jit(solution)/shard_map/ppermute | solution.py:27
  319.6 20.7 %collective-permute-start.30 = (bf16[448,1024]{1,0:T(8,128)(2,1)S(1)}, bf16[448,1024]{1,0:T(8,128)(2,1)S(1)}, u32[]{:S(2)}, u32[]{:S(2)}) collective-permute-start(bf16[448,1024]{1,0:T(8,128)(2,1)S(1)} %fusion.8), channel_id=1, source_target_pairs={{8,0},{10,2},{12,4},{14,6},{16,8},{18,10},{20,12},{22,14},{24,16},... | collective-permute-start | bytes 2752520 | tf_op jit(solution)/shard_map/ppermute | solution.py:30
  320.9 22.8 %collective-permute-start.35 = (bf16[512,1024]{1,0:T(8,128)(2,1)}, bf16[512,1024]{1,0:T(8,128)(2,1)S(1)}, u32[]{:S(2)}, u32[]{:S(2)}) collective-permute-start(bf16[512,1024]{1,0:T(8,128)(2,1)} %convolution_convert_fusion), channel_id=1, source_target_pairs={{0,6},{2,4},{4,2},{6,0},{8,14},{10,12},{12,10},{14,8},{16,22},{18,... | collective-permute-start | bytes 3145736 | tf_op jit(solution)/shard_map/ppermute | solution.py:24
  340.8 19.2 %collective-permute-start.33 = (bf16[448,1024]{1,0:T(8,128)(2,1)S(1)}, bf16[448,1024]{1,0:T(8,128)(2,1)S(1)}, u32[]{:S(2)}, u32[]{:S(2)}) collective-permute-start(bf16[448,1024]{1,0:T(8,128)(2,1)S(1)} %fusion.19), channel_id=1, source_target_pairs={{0,8},{2,10},{4,12},{6,14},{8,16},{10,18},{12,20},{14,22},{16,24},... | collective-permute-start | bytes 2752520 | tf_op jit(solution)/shard_map/ppermute | solution.py:27
  342.3 20.3 %collective-permute-start.34 = (bf16[448,1024]{1,0:T(8,128)(2,1)S(1)}, bf16[448,1024]{1,0:T(8,128)(2,1)S(1)}, u32[]{:S(2)}, u32[]{:S(2)}) collective-permute-start(bf16[448,1024]{1,0:T(8,128)(2,1)S(1)} %fusion.19), channel_id=1, source_target_pairs={{8,0},{10,2},{12,4},{14,6},{16,8},{18,10},{20,12},{22,14},{24,16},... | collective-permute-start | bytes 2752520 | tf_op jit(solution)/shard_map/ppermute | solution.py:30
  362.7 16.4 %collective-permute-start.36 = (bf16[448,1024]{1,0:T(8,128)(2,1)S(1)}, bf16[448,1024]{1,0:T(8,128)(2,1)}, u32[]{:S(2)}, u32[]{:S(2)}) collective-permute-start(bf16[448,1024]{1,0:T(8,128)(2,1)S(1)} %collective-permute-done.34), channel_id=1, source_target_pairs={{8,0},{10,2},{12,4},{14,6},{16,8},{18,10},{20,12},{22,14},{24,16},... | collective-permute-start | bytes 2752520 | tf_op jit(solution)/shard_map/ppermute | solution.py:30
  363.9 17.1 %collective-permute-start.38 = (bf16[448,1024]{1,0:T(8,128)(2,1)S(1)}, bf16[448,1024]{1,0:T(8,128)(2,1)S(1)}, u32[]{:S(2)}, u32[]{:S(2)}) collective-permute-start(bf16[448,1024]{1,0:T(8,128)(2,1)S(1)} %collective-permute-done.33), channel_id=1, source_target_pairs={{0,8},{2,10},{4,12},{6,14},{8,16},{10,18},{12,20},{14,22},{16,24},... | collective-permute-start | bytes 2752520 | tf_op jit(solution)/shard_map/ppermute | solution.py:27
  379.1 15.6 %collective-permute-start.37 = (bf16[448,1024]{1,0:T(8,128)(2,1)}, bf16[448,1024]{1,0:T(8,128)(2,1)}, u32[]{:S(2)}, u32[]{:S(2)}) collective-permute-start(bf16[448,1024]{1,0:T(8,128)(2,1)} %collective-permute-done.36), channel_id=1, source_target_pairs={{8,0},{10,2},{12,4},{14,6},{16,8},{18,10},{20,12},{22,14},{24,16},... | collective-permute-start | bytes 2752520 | tf_op jit(solution)/shard_map/ppermute | solution.py:30
  381.1 15.8 %collective-permute-start.39 = (bf16[448,1024]{1,0:T(8,128)(2,1)S(1)}, bf16[448,1024]{1,0:T(8,128)(2,1)}, u32[]{:S(2)}, u32[]{:S(2)}) collective-permute-start(bf16[448,1024]{1,0:T(8,128)(2,1)S(1)} %collective-permute-done.38), channel_id=1, source_target_pairs={{0,8},{2,10},{4,12},{6,14},{8,16},{10,18},{12,20},{14,22},{16,24},... | collective-permute-start | bytes 2752520 | tf_op jit(solution)/shard_map/ppermute | solution.py:27
  386.4 4.5 %collective-permute-start.42 = (s32[512]{0:T(512)S(1)}, s32[512]{0:T(512)S(1)}, u32[]{:S(2)}, u32[]{:S(2)}) collective-permute-start(s32[512]{0:T(512)S(1)} %copy-done.18), channel_id=1, source_target_pairs={{0,6},{2,4},{4,2},{6,0},{8,14},{10,12},{12,10},{14,8},{16,22},{18,... | collective-permute-start | bytes 6152 | tf_op jit(solution)/shard_map/ppermute | solution.py:24
  387.0 3.9 collective-permute-start.41
  415.4 4.5 %collective-permute-start.45 = (f32[32]{0:T(128)S(1)}, f32[32]{0:T(128)S(1)}, u32[]{:S(2)}, u32[]{:S(2)}) collective-permute-start(f32[32]{0:T(128)S(1)} %convolution_bitcast_fusion), channel_id=1, source_target_pairs={{0,6},{2,4},{4,2},{6,0},{8,14},{10,12},{12,10},{14,8},{16,22},{18,... | collective-permute-start | bytes 392 | tf_op jit(solution)/shard_map/ppermute | solution.py:24
  421.9 6.7 %collective-permute-start.48 = (f32[32]{0:T(128)S(1)}, f32[32]{0:T(128)S(1)}, u32[]{:S(2)}, u32[]{:S(2)}) collective-permute-start(f32[32]{0:T(128)S(1)} %add_add_fusion.4), channel_id=1, source_target_pairs={{0,24},{2,26},{4,28},{6,30},{8,0},{10,2},{12,4},{14,6},{16,8},{18,... | collective-permute-start | bytes 392 | tf_op jit(solution)/shard_map/ppermute | solution.py:52
  427.2 5.3 %collective-permute-start.46 = (f32[32]{0:T(128)S(1)}, f32[32]{0:T(128)S(1)}, u32[]{:S(2)}, u32[]{:S(2)}) collective-permute-start(f32[32]{0:T(128)S(1)} %add_add_fusion.4), channel_id=1, source_target_pairs={{0,8},{2,10},{4,12},{6,14},{8,16},{10,18},{12,20},{14,22},{16,24},... | collective-permute-start | bytes 392 | tf_op jit(solution)/shard_map/ppermute | solution.py:52
  427.2 5.3 %collective-permute-start.47 = (f32[32]{0:T(128)S(1)}, f32[32]{0:T(128)S(1)}, u32[]{:S(2)}, u32[]{:S(2)}) collective-permute-start(f32[32]{0:T(128)S(1)} %add_add_fusion.4), channel_id=1, source_target_pairs={{0,16},{2,18},{4,20},{6,22},{8,24},{10,26},{12,28},{14,30},{16,0},... | collective-permute-start | bytes 392 | tf_op jit(solution)/shard_map/ppermute | solution.py:52
  (34 other events, 443.5 us)
Sparse Core Ops, SparseCore 0:
  8.9 12.8 all-gather.6
  86.2 19.2 all-gather.10
  107.0 11.7 all-gather.8
  312.8 15.3 all-gather.12

commit v3 on v2

--- a/solution.py
+++ b/solution.py
@@ -29,18 +29,32 @@
     def left(v):
         return lax.ppermute(v, "dp", [(i, i - IN) for i in range(IN, n)])
 
-    def beside(pair, extras):
+    def beside(pair, extras, later):
         moved = [swap(x, j) for x, j in extras]
-        return lax.optimization_barrier((pair, moved))
+        waiting = [[x for x, _ in step] for step in later]
+        pair, moved, waiting = lax.optimization_barrier((pair, moved, waiting))
+        later = [[(x, j) for x, (_, j) in zip(xs, step)] for xs, step in zip(waiting, later)]
+        return pair, moved, later
 
-    def line_gather(v, extras):
+    def halves(v, axis):
+        return jnp.split(v, 2, axis=axis)
+
+    def plane_rest(from_x, from_y, axis):
+        first = swap(halves(from_y, axis)[0], 1)
+        second = swap(halves(from_x, axis)[1], 2)
+        return jnp.concatenate([first, second], axis=axis)
+
+    def line_gather(v, extras, tail=None):
         rights, lefts = [v], [v]
         moved = []
         for t in range(outer - 1):
             pair = (right(rights[-1]), left(lefts[-1]))
-            if t < len(extras):
-                pair, arrived = beside(pair, extras[t])
+            if extras:
+                pair, arrived, extras = beside(pair, extras[0], extras[1:])
                 moved += arrived
+            if tail is not None and t == outer - 2:
+                pair, kept = lax.optimization_barrier((pair, tail(moved)))
+                moved = (moved, kept)
             rights.append(pair[0])
             lefts.append(pair[1])
         blocks = [v] + [jnp.where(s <= o, rights[s], lefts[outer - s]) for s in range(1, outer)]
@@ -73,42 +87,57 @@
     rows, u = lax.optimization_barrier((rows, u))
     rows = rows.reshape(-1, IN, fc, fc)
     sends = [lax.dynamic_index_in_dim(rows, p ^ j, axis=1, keepdims=False) for j in range(IN)]
-    u_rel, got = line_gather(u, [[(sends[1], 1), (sends[2], 2)], [(sends[3], 3)]])
-    got = [sends[0]] + got
-    q_all = lax.all_gather(jnp.stack(got, axis=1), "mp", axis=0)
-    q_rel = jnp.stack([pick(q_all, s) for s in range(outer)])
+    x_full = lax.all_gather(inputs, "mp", axis=1, tiled=True)
+    proj = jnp.dot(x_full, basis_in, preferred_element_type=F32).astype(BF)
 
-    part_sum = jnp.broadcast_to(jnp.sum(eigen_scales), (8, 128))
-    damping = damping_ratio * sum_over_devices(part_sum)[:1, :1] / (d_in * f_all)
+    def prepare(got):
+        q_all = lax.all_gather(jnp.stack([sends[0]] + got[:3], axis=1), "mp", axis=0)
+        q_rel = jnp.stack([pick(q_all, s) for s in range(outer)])
+        part_sum = jnp.broadcast_to(jnp.sum(eigen_scales), (8, 128))
+        damping = damping_ratio * sum_over_devices(part_sum)[:1, :1] / (d_in * f_all)
+        return q_rel, damping
+
+    u_rel, (got, (q_rel, damping)) = line_gather(
+        u,
+        [[(sends[1], 1), (sends[2], 2)], [(sends[3], 3)], [(proj, 1), (proj, 2)]],
+        prepare,
+    )
+    proj_x, proj_y = got[3:]
     u_cat = jnp.concatenate(u_rel, axis=1)
-    u_cat, q_rel, damping = lax.optimization_barrier((u_cat, q_rel, damping))
 
-    terms = {}
-    for j in (3, 1, 2, 0):
-        y = jnp.dot(u_cat, q_rel[:, j].reshape(-1, fc), preferred_element_type=F32)
-        terms[j] = swap(y.astype(BF), j).astype(F32) if j else y
-    rotated = terms[0] + terms[1] + terms[2] + terms[3]
+    def term(j):
+        return jnp.dot(u_cat, q_rel[:, j].reshape(-1, fc), preferred_element_type=F32)
+
+    far = halves(term(3).astype(BF), 0)
+    far_y = swap(far[0], 1).astype(F32)
+    far_x = swap(far[1], 2).astype(F32)
+    term_y = halves(term(2), 0)
+    term_x = halves(term(1), 0)
+    term_y = jnp.concatenate([term_y[0] + far_y, term_y[1]])
+    term_x = jnp.concatenate([term_x[0], term_x[1] + far_x])
+    own = term(0)
+    got_x, got_y = swap(term_x.astype(BF), 1), swap(term_y.astype(BF), 2)
+    rotated = own + got_x.astype(F32) + got_y.astype(F32)
     rescaled = (rotated / (eigen_scales + damping)).astype(BF)
 
-    res = jnp.stack([swap(rescaled, j) if j else rescaled for j in range(IN)])
+    res_x, res_y = swap(rescaled, 1), swap(rescaled, 2)
+    res = jnp.stack([rescaled, res_x, res_y, plane_rest(res_x, res_y, 0)])
 
     def block(s):
         return lax.dot_general(
             q_rel[s], res, (((0, 2), (0, 2)), ((), ())), preferred_element_type=F32
         )
 
-    x_full = lax.all_gather(inputs, "mp", axis=1, tiled=True)
-    proj = jnp.dot(x_full, basis_in, preferred_element_type=F32).astype(BF)
     cols = out_grads.reshape(tok, -1, IN, fc)
     g_sends = [
         lax.dynamic_index_in_dim(cols, p ^ j, axis=2, keepdims=False).transpose(1, 0, 2)
         for j in range(IN)
     ]
-    res, proj, g_sends = lax.optimization_barrier((res, proj, g_sends))
+    res, g_sends = lax.optimization_barrier((res, g_sends))
     extras = [
         [(g_sends[1], 1), (g_sends[2], 2)],
         [(g_sends[3], 3)],
-        [(proj, 1), (proj, 2)],
+        [(halves(proj_y, 0)[0], 1), (halves(proj_x, 0)[1], 2)],
     ]
     a = b = None
     moved = []
@@ -117,18 +146,17 @@
         if a is not None:
             va, vb = va + a, vb + b
         a, b = right(va.astype(BF)), left(vb.astype(BF))
-        if t < len(extras):
-            (a, b), arrived = beside((a, b), extras[t])
+        if extras:
+            (a, b), arrived, extras = beside((a, b), extras[0], extras[1:])
             moved += arrived
         a, b = a.astype(F32), b.astype(F32)
     back = (block(0) + a + b).astype(BF)
 
     g = [g_sends[0]] + moved[:3]
-    back_rel, last = line_gather(back, [[(proj, 3)]])
+    back_rel, _ = line_gather(back, [])
     g_all = lax.all_gather(jnp.concatenate(g, axis=1), "mp", axis=0)
-    projs = [proj] + moved[3:] + last
+    projs = [proj, proj_x, proj_y] + moved[3:]
     ids = jnp.concatenate([segment_ids] + [swap(segment_ids, j) for j in range(1, IN)])
-    back_rel, projs = lax.optimization_barrier((back_rel, projs))
     proj_all = jnp.concatenate(projs)
     score = 0.0
     for s in range(outer):

time: 442 us -> 407 us (0.921); the launches traced: 441 us -> 401 us
  waiting for transfers between devices: 239 us -> 169 us
  starting transfers between devices: 83.5 us -> 109 us
  local copies, waits for them, and re-layouts: 27.4 us -> 35 us
  other arithmetic: 25 us -> 19.3 us
    ppermute x9, waiting for transfers between devices: 45.9 us -> 1.4 us  [right(): return lax.ppermute(v, 'dp', [(i, i + IN) for i in range(n - IN)])]
    ppermute x24 -> x27, waiting for transfers between devices: 140 us -> 106 us  [swap(): return lax.ppermute(v, 'dp', [(i, i ^ j) for i in range(n)])]
    ppermute x9, waiting for transfers between devices: 22.6 us -> 36.7 us  [left(): return lax.ppermute(v, 'dp', [(i, i - IN) for i in range(IN, n)])]
    ppermute x9, starting transfers between devices: 11.6 us -> 23.7 us  [left(): return lax.ppermute(v, 'dp', [(i, i - IN) for i in range(IN, n)])]
    ppermute x9, starting transfers between devices: 32.9 us -> 39.7 us  [right(): return lax.ppermute(v, 'dp', [(i, i + IN) for i in range(n - IN)])]
    ppermute x24 -> x27, starting transfers between devices: 29.3 us -> 35 us  [swap(): return lax.ppermute(v, 'dp', [(i, i ^ j) for i in range(n)])]
    ppermute x6, waiting for transfers between devices: 19 us -> 13.6 us  [sum_over_devices(): lax.ppermute(v, 'dp', [(i, (i + s * IN) % n) for i in range(n)])]
    select_n x6 -> x2, other arithmetic: 8.4 us -> 3.94 us  [line_gather(): jnp.where(s <= o, rights[s], lefts[outer - s])]
  transfers between devices with their start and end apart: 54 -> 57, of which waited for: 36 -> 35; matrix products, arithmetic and copies ran while one was open for 14% -> 18% of each run, Pallas kernels for 0% -> 0%
where the time goes in v3:
time: 407 us; the launch traced here: 401 us
  waiting for transfers between devices  169 us (42%)
  starting transfers between devices  109 us (27%)
  matrix products  53.4 us (13%)
  local copies, waits for them, and re-layouts  35 us (9%)
  other arithmetic  19.3 us (5%)
  between operations  14.8 us (4%)
    ppermute x27, waiting for transfers between devices, swap(): return lax.ppermute(v, 'dp', [(i, i ^ j) for i in range(n)])  106 us
    ppermute x9, starting transfers between devices, right(): return lax.ppermute(v, 'dp', [(i, i + IN) for i in range(n - IN)])  39.7 us
    ppermute x9, waiting for transfers between devices, left(): return lax.ppermute(v, 'dp', [(i, i - IN) for i in range(IN, n)])  36.7 us
    ppermute x27, starting transfers between devices, swap(): return lax.ppermute(v, 'dp', [(i, i ^ j) for i in range(n)])  35 us
    ppermute x9, starting transfers between devices, left(): return lax.ppermute(v, 'dp', [(i, i - IN) for i in range(IN, n)])  23.7 us
    unnamed x57, local copies, waits for them, and re-layouts  19.8 us
    dot_general x4, matrix products, on_device(): lax.dot_general(pick(g_all, s), back_rel[s], (((1,), (0,)), ((), ())), pr...  16.1 us
    ppermute x6, waiting for transfers between devices, sum_over_devices(): lax.ppermute(v, 'dp', [(i, (i + s * IN) % n) for i in range(n)])  13.6 us
  transfers between devices with their start and end apart: 57, of which 35 were waited for; matrix products, arithmetic and copies ran while one was open for 18% of the time, Pallas kernels for 0%

profile of v3, /device:TPU:0, one launch (start us, length us, event | category | flops | bytes accessed | tf_op | source)
XLA Modules:
  0.0 400.7 jit_solution(16624762010472129621)
XLA Ops:
  8.1 5.7 %copy.11 = bf16[3584,448]{1,0:T(8,128)(2,1)} copy(bf16[3584,448]{0,1:T(8,128)(2,1)} %param.9) | data formatting | bytes 6422528 | tf_op args[2]
  13.8 8.0 %all-gather.9.cloned.1.call-done = bf16[2048,448]{0,1:T(8,128)(2,1)} async-done(((bf16[1024,448]{0,1:T(8,128)(2,1)}), bf16[2048,448]{0,1:T(8,128)(2,1)}) %all-gather.9.cloned.1.call-update) | async-done | bytes 1835024 | tf_op jit(solution)/shard_map/all_gather | solution.py:82
  21.8 5.9 %convolution_convert_fusion.1 = bf16[1024,448]{0,1:T(8,128)(2,1)} fusion(bf16[2048,448]{0,1:T(8,128)(2,1)} %all-gather.9.cloned.1.call-done, bf16[2048,1024]{1,0:T(8,128)(2,1)} %param.8), kind=kOutput, calls=%fused_computation.52 | convolution fusion | flops 1879506944 | bytes 6946816 | tf_op jit(solution)/shard_map/dot_general | solution.py:83
  29.0 5.5 %collective-permute-start = (bf16[1024,448]{0,1:T(8,128)(2,1)}, bf16[1024,448]{0,1:T(8,128)(2,1)}, u32[]{:S(2)}, u32[]{:S(2)}) collective-permute-start(bf16[1024,448]{0,1:T(8,128)(2,1)} %convolution_convert_fusion.1), channel_id=1, source_target_pairs={{0,8},{2,10},{4,12},{6,14},{8,16},{10,18},{12,20},{14,22},{16,24},... | collective-permute-start | bytes 2752520 | tf_op jit(solution)/shard_map/ppermute | solution.py:27
  39.3 6.6 %constant_dynamic-update-slice_fusion.4 = (bf16[2048,1024]{1,0:T(8,128)(2,1)}, bf16[512,1024]{1,0:T(8,128)(2,1)}) fusion(bf16[512,2048]{1,0:T(8,128)(2,1)} %all-gather.7.cloned.1.call-done, bf16[2048,1024]{1,0:T(8,128)(2,1)} %param.8), kind=kOutput, calls=%fused_computation.86 | convolution fusion | flops 2148007936 | bytes 8388608 | tf_op jit(solution)/shard_map/dot_general | solution.py:91
  45.9 12.5 %collective-permute-done.3 = bf16[2,448,448]{2,1,0:T(8,128)(2,1)S(1)} collective-permute-done((bf16[2,448,448]{2,1,0:T(8,128)(2,1)}, bf16[2,448,448]{2,1,0:T(8,128)(2,1)S(1)}, u32[]{:S(2)}, u32[]{:S(2)}) %collective-permute-start.3) | collective-permute-done | bytes 802848 | tf_op jit(solution)/shard_map/ppermute | solution.py:24
  59.8 3.4 collective-permute-start.4
  66.1 20.0 %collective-permute-done.6 = bf16[2,448,448]{2,1,0:T(8,128)(2,1)S(1)} collective-permute-done((bf16[2,448,448]{2,1,0:T(8,128)(2,1)S(1)}, bf16[2,448,448]{2,1,0:T(8,128)(2,1)S(1)}, u32[]{:S(2)}, u32[]{:S(2)}) %collective-permute-start.6) | collective-permute-done | bytes 802848 | tf_op jit(solution)/shard_map/ppermute | solution.py:24
  90.4 5.2 %collective-permute-start.7 = (bf16[1024,448]{0,1:T(8,128)(2,1)}, bf16[1024,448]{0,1:T(8,128)(2,1)}, u32[]{:S(2)}, u32[]{:S(2)}) collective-permute-start(bf16[1024,448]{0,1:T(8,128)(2,1)} %collective-permute-done.4), channel_id=1, source_target_pairs={{0,8},{2,10},{4,12},{6,14},{8,16},{10,18},{12,20},{14,22},{16,24},... | collective-permute-start | bytes 2752520 | tf_op jit(solution)/shard_map/ppermute | solution.py:27
  100.1 11.1 %collective-permute-done.13 = f32[8,128]{1,0:T(8,128)S(1)} collective-permute-done((f32[8,128]{1,0:T(8,128)S(1)}, f32[8,128]{1,0:T(8,128)S(1)}, u32[]{:S(2)}, u32[]{:S(2)}) %collective-permute-start.13) | collective-permute-done | bytes 4128 | tf_op jit(solution)/shard_map/ppermute | solution.py:24
  119.1 3.9 collective-permute-start.16
  125.7 3.2 collective-permute-done.15
  130.5 3.9 collective-permute-done.14
  139.1 4.0 dynamic-slice_bitcast_fusion.3
  145.3 2.4 copy-done
  149.4 3.2 fusion.44
  152.5 3.1 convolution_convert_fusion.2
  158.5 3.1 fusion.43
  161.8 7.6 %collective-permute-done.20 = bf16[512,448]{0,1:T(8,128)(2,1)S(1)} collective-permute-done((bf16[512,448]{0,1:T(8,128)(2,1)S(1)}, bf16[512,448]{0,1:T(8,128)(2,1)S(1)}, u32[]{:S(2)}, u32[]{:S(2)}) %collective-permute-start.20) | collective-permute-done | bytes 458784 | tf_op jit(solution)/shard_map/ppermute | solution.py:24
  172.3 3.1 fusion.45
  175.4 15.6 %collective-permute-done.21 = bf16[1024,448]{0,1:T(8,128)(2,1)S(1)} collective-permute-done((bf16[1024,448]{0,1:T(8,128)(2,1)S(1)}, bf16[1024,448]{0,1:T(8,128)(2,1)S(1)}, u32[]{:S(2)}, u32[]{:S(2)}) %collective-permute-start.21) | collective-permute-done | bytes 917536 | tf_op jit(solution)/shard_map/ppermute | solution.py:24
  195.3 17.3 %collective-permute-done.23 = bf16[1024,448]{0,1:T(8,128)(2,1)S(1)} collective-permute-done((bf16[1024,448]{0,1:T(8,128)(2,1)S(1)}, bf16[1024,448]{0,1:T(8,128)(2,1)S(1)}, u32[]{:S(2)}, u32[]{:S(2)}) %collective-permute-start.23) | collective-permute-done | bytes 917536 | tf_op jit(solution)/shard_map/ppermute | solution.py:24
  217.1 5.9 %copy.12 = bf16[512,3584]{0,1:T(8,128)(2,1)} copy(bf16[512,3584]{1,0:T(8,128)(2,1)} %param.12) | data formatting | bytes 7340032 | tf_op args[5]
  222.9 2.5 dynamic-slice_bitcast_fusion.4
  228.1 3.1 bitcast_convert_fusion
  231.2 3.1 bitcast_convert_fusion.1
  237.2 13.5 %collective-permute-start.27 = (bf16[448,1024]{1,0:T(8,128)(2,1)S(1)}, bf16[448,1024]{1,0:T(8,128)(2,1)S(1)}, u32[]{:S(2)}, u32[]{:S(2)}) collective-permute-start(bf16[448,1024]{1,0:T(8,128)(2,1)S(1)} %get-tuple-element.115), channel_id=1, source_target_pairs={{8,0},{10,2},{12,4},{14,6},{16,8},{18,10},{20,12},{22,14},{24,16},... | collective-permute-start | bytes 2752520 | tf_op jit(solution)/shard_map/ppermute | solution.py:30
  254.5 2.5 collective-permute-done.27
  258.8 5.5 %collective-permute-start.30 = (bf16[448,1024]{1,0:T(8,128)(2,1)S(1)}, bf16[448,1024]{1,0:T(8,128)(2,1)}, u32[]{:S(2)}, u32[]{:S(2)}) collective-permute-start(bf16[448,1024]{1,0:T(8,128)(2,1)S(1)} %get-tuple-element.108), channel_id=1, source_target_pairs={{0,8},{2,10},{4,12},{6,14},{8,16},{10,18},{12,20},{14,22},{16,24},... | collective-permute-start | bytes 2752520 | tf_op jit(solution)/shard_map/ppermute | solution.py:27
  266.4 10.2 %collective-permute-done.31 = bf16[448,1024]{1,0:T(8,128)(2,1)} collective-permute-done((bf16[448,1024]{1,0:T(8,128)(2,1)S(1)}, bf16[448,1024]{1,0:T(8,128)(2,1)}, u32[]{:S(2)}, u32[]{:S(2)}) %collective-permute-start.31) | collective-permute-done | bytes 917536 | tf_op jit(solution)/shard_map/ppermute | solution.py:30
  277.5 4.1 %collective-permute-done.32 = bf16[2,512,448]{1,2,0:T(8,128)(2,1)S(1)} collective-permute-done((bf16[2,512,448]{1,2,0:T(8,128)(2,1)S(1)}, bf16[2,512,448]{1,2,0:T(8,128)(2,1)S(1)}, u32[]{:S(2)}, u32[]{:S(2)}) %collective-permute-start.32) | collective-permute-done | bytes 917536 | tf_op jit(solution)/shard_map/ppermute | solution.py:24
  285.9 2.9 collective-permute-start.33
  294.6 3.7 fusion.9
  298.3 2.7 collective-permute-done.35
  302.5 8.3 %collective-permute-done.34 = bf16[448,1024]{1,0:T(8,128)(2,1)S(1)} collective-permute-done((bf16[448,1024]{1,0:T(8,128)(2,1)S(1)}, bf16[448,1024]{1,0:T(8,128)(2,1)S(1)}, u32[]{:S(2)}, u32[]{:S(2)}) %collective-permute-start.34) | collective-permute-done | bytes 917536 | tf_op jit(solution)/shard_map/ppermute | solution.py:30
  312.7 5.5 %collective-permute-start.37 = (bf16[448,1024]{1,0:T(8,128)(2,1)S(1)}, bf16[448,1024]{1,0:T(8,128)(2,1)}, u32[]{:S(2)}, u32[]{:S(2)}) collective-permute-start(bf16[448,1024]{1,0:T(8,128)(2,1)S(1)} %fusion.8), channel_id=1, source_target_pairs={{0,8},{2,10},{4,12},{6,14},{8,16},{10,18},{12,20},{14,22},{16,24},... | collective-permute-start | bytes 2752520 | tf_op jit(solution)/shard_map/ppermute | solution.py:27
  318.2 13.5 %collective-permute-done.38 = bf16[448,1024]{1,0:T(8,128)(2,1)} collective-permute-done((bf16[448,1024]{1,0:T(8,128)(2,1)S(1)}, bf16[448,1024]{1,0:T(8,128)(2,1)}, u32[]{:S(2)}, u32[]{:S(2)}) %collective-permute-start.38) | collective-permute-done | bytes 917536 | tf_op jit(solution)/shard_map/ppermute | solution.py:30
  333.0 5.5 %collective-permute-start.41 = (bf16[448,1024]{1,0:T(8,128)(2,1)}, bf16[448,1024]{1,0:T(8,128)(2,1)}, u32[]{:S(2)}, u32[]{:S(2)}) collective-permute-start(bf16[448,1024]{1,0:T(8,128)(2,1)} %collective-permute-done.37), channel_id=1, source_target_pairs={{0,8},{2,10},{4,12},{6,14},{8,16},{10,18},{12,20},{14,22},{16,24},... | collective-permute-start | bytes 2752520 | tf_op jit(solution)/shard_map/ppermute | solution.py:27
  343.4 2.4 collective-permute-done.45
  346.9 2.3 constant_dynamic-update-slice_fusion.2
  354.4 4.4 %collective-permute-start.42 = (bf16[448,1024]{1,0:T(8,128)(2,1)}, bf16[448,1024]{1,0:T(8,128)(2,1)S(1)}, u32[]{:S(2)}, u32[]{:S(2)}) collective-permute-start(bf16[448,1024]{1,0:T(8,128)(2,1)} %collective-permute-done.41), channel_id=1, source_target_pairs={{0,8},{2,10},{4,12},{6,14},{8,16},{10,18},{12,20},{14,22},{16,24},... | collective-permute-start | bytes 2752520 | tf_op jit(solution)/shard_map/ppermute | solution.py:27
  358.9 5.7 %fusion.2 = f32[2048]{0:T(1024)S(1)} fusion(bf16[2048,1024]{1,0:T(8,128)(2,1)} %constant_dynamic-update-slice_fusion, bf16[2,2,2048,448]{2,3,1,0:T(8,128)(2,1)} %bitcast.131, s32[]{:T(128)S(6)} %select_n.211, s32[]{:T(128)S(6)} %select_n.214, bf16[448,1024]{1,0:T(8,128)(2,1)} %collective-permute-done.41, bf16[448,1024]{1,0:T(8,128)(2,1)} %collective-permute-done.39, ...), kind=kOutput, calls=%fused_computation.6 | convolution fusion | flops 1885796352 | bytes 7872521 | tf_op jit(solution)/shard_map/dot_general | solution.py:163
  365.5 2.7 fusion
  368.5 3.8 fusion.1
  372.4 3.9 fusion.3
  376.8 2.3 collective-permute-start.48
  383.7 3.2 collective-permute-start.50
  388.4 3.8 collective-permute-done.49
  (183 shorter events, 104.6 us)
Async XLA Ops:
  6.5 15.3 %all-gather.9.cloned.1.call-start = ((), (), s32[]{:S(2)}) async-start(), calls=%async_computation.1 | async-start | bytes 2752512 | tf_op jit(solution)/shard_map/all_gather | solution.py:82
  7.3 32.1 %all-gather.7.cloned.1.call-start = ((), (), s32[]{:S(2)}) async-start(), calls=%async_computation | async-start | bytes 3145728 | tf_op jit(solution)/shard_map/all_gather | solution.py:90
  8.0 131.1 %all-gather.11.cloned.1.call-start = ((), (), s32[]{:S(2)}) async-start(), calls=%async_computation.2 | async-start | bytes 11010048 | tf_op jit(solution)/shard_map/all_gather | solution.py:94
  27.7 32.1 %collective-permute-start.1 = (bf16[1024,448]{0,1:T(8,128)(2,1)}, bf16[1024,448]{0,1:T(8,128)(2,1)}, u32[]{:S(2)}, u32[]{:S(2)}) collective-permute-start(bf16[1024,448]{0,1:T(8,128)(2,1)} %convolution_convert_fusion.1), channel_id=1, source_target_pairs={{8,0},{10,2},{12,4},{14,6},{16,8},{18,10},{20,12},{22,14},{24,16},... | collective-permute-start | bytes 2752520 | tf_op jit(solution)/shard_map/ppermute | solution.py:30
  29.0 30.8 %collective-permute-start = (bf16[1024,448]{0,1:T(8,128)(2,1)}, bf16[1024,448]{0,1:T(8,128)(2,1)}, u32[]{:S(2)}, u32[]{:S(2)}) collective-permute-start(bf16[1024,448]{0,1:T(8,128)(2,1)} %convolution_convert_fusion.1), channel_id=1, source_target_pairs={{0,8},{2,10},{4,12},{6,14},{8,16},{10,18},{12,20},{14,22},{16,24},... | collective-permute-start | bytes 2752520 | tf_op jit(solution)/shard_map/ppermute | solution.py:27
  36.1 22.2 %collective-permute-start.3 = (bf16[2,448,448]{2,1,0:T(8,128)(2,1)}, bf16[2,448,448]{2,1,0:T(8,128)(2,1)S(1)}, u32[]{:S(2)}, u32[]{:S(2)}) collective-permute-start(bf16[2,448,448]{2,1,0:T(8,128)(2,1)} %get-tuple-element.105), channel_id=1, source_target_pairs={{0,4},{2,6},{4,0},{6,2},{8,12},{10,14},{12,8},{14,10},{16,20},{18,... | collective-permute-start | bytes 2408456 | tf_op jit(solution)/shard_map/ppermute | solution.py:24
  37.9 21.9 %collective-permute-start.2 = (bf16[2,448,448]{2,1,0:T(8,128)(2,1)}, bf16[2,448,448]{2,1,0:T(8,128)(2,1)S(1)}, u32[]{:S(2)}, u32[]{:S(2)}) collective-permute-start(bf16[2,448,448]{2,1,0:T(8,128)(2,1)} %get-tuple-element.106), channel_id=1, source_target_pairs={{0,2},{2,0},{4,6},{6,4},{8,10},{10,8},{12,14},{14,12},{16,18},{18,... | collective-permute-start | bytes 2408456 | tf_op jit(solution)/shard_map/ppermute | solution.py:24
  59.8 26.2 %collective-permute-start.4 = (bf16[1024,448]{0,1:T(8,128)(2,1)}, bf16[1024,448]{0,1:T(8,128)(2,1)}, u32[]{:S(2)}, u32[]{:S(2)}) collective-permute-start(bf16[1024,448]{0,1:T(8,128)(2,1)} %collective-permute-done), channel_id=1, source_target_pairs={{0,8},{2,10},{4,12},{6,14},{8,16},{10,18},{12,20},{14,22},{16,24},... | collective-permute-start | bytes 2752520 | tf_op jit(solution)/shard_map/ppermute | solution.py:27
  63.2 22.8 %collective-permute-start.5 = (bf16[1024,448]{0,1:T(8,128)(2,1)}, bf16[1024,448]{0,1:T(8,128)(2,1)}, u32[]{:S(2)}, u32[]{:S(2)}) collective-permute-start(bf16[1024,448]{0,1:T(8,128)(2,1)} %collective-permute-done.1), channel_id=1, source_target_pairs={{8,0},{10,2},{12,4},{14,6},{16,8},{18,10},{20,12},{22,14},{24,16},... | collective-permute-start | bytes 2752520 | tf_op jit(solution)/shard_map/ppermute | solution.py:30
  64.5 21.5 %collective-permute-start.6 = (bf16[2,448,448]{2,1,0:T(8,128)(2,1)S(1)}, bf16[2,448,448]{2,1,0:T(8,128)(2,1)S(1)}, u32[]{:S(2)}, u32[]{:S(2)}) collective-permute-start(bf16[2,448,448]{2,1,0:T(8,128)(2,1)S(1)} %copy-done.15), channel_id=1, source_target_pairs={{0,6},{2,4},{4,2},{6,0},{8,14},{10,12},{12,10},{14,8},{16,22},{18,... | collective-permute-start | bytes 2408456 | tf_op jit(solution)/shard_map/ppermute | solution.py:24
  88.2 270.7 %all-gather.13.cloned.1.call-start = ((), (), s32[]{:S(2)}) async-start(), calls=%async_computation.3 | async-start | bytes 11010048 | tf_op jit(solution)/shard_map/all_gather | solution.py:157
  88.2 50.8 %collective-permute-start.9 = (bf16[512,1024]{1,0:T(8,128)(2,1)}, bf16[512,1024]{1,0:T(8,128)(2,1)S(1)}, u32[]{:S(2)}, u32[]{:S(2)}) collective-permute-start(bf16[512,1024]{1,0:T(8,128)(2,1)} %get-tuple-element.58), channel_id=1, source_target_pairs={{0,2},{2,0},{4,6},{6,4},{8,10},{10,8},{12,14},{14,12},{16,18},{18,... | collective-permute-start | bytes 3145736 | tf_op jit(solution)/shard_map/ppermute | solution.py:24
  89.7 49.3 %collective-permute-start.10 = (bf16[512,1024]{1,0:T(8,128)(2,1)}, bf16[512,1024]{1,0:T(8,128)(2,1)}, u32[]{:S(2)}, u32[]{:S(2)}) collective-permute-start(bf16[512,1024]{1,0:T(8,128)(2,1)} %get-tuple-element.58), channel_id=1, source_target_pairs={{0,4},{2,6},{4,0},{6,2},{8,12},{10,14},{12,8},{14,10},{16,20},{18,... | collective-permute-start | bytes 3145736 | tf_op jit(solution)/shard_map/ppermute | solution.py:24
  90.4 48.7 %collective-permute-start.7 = (bf16[1024,448]{0,1:T(8,128)(2,1)}, bf16[1024,448]{0,1:T(8,128)(2,1)}, u32[]{:S(2)}, u32[]{:S(2)}) collective-permute-start(bf16[1024,448]{0,1:T(8,128)(2,1)} %collective-permute-done.4), channel_id=1, source_target_pairs={{0,8},{2,10},{4,12},{6,14},{8,16},{10,18},{12,20},{14,22},{16,24},... | collective-permute-start | bytes 2752520 | tf_op jit(solution)/shard_map/ppermute | solution.py:27
  95.6 43.5 %collective-permute-start.8 = (bf16[1024,448]{0,1:T(8,128)(2,1)}, bf16[1024,448]{0,1:T(8,128)(2,1)}, u32[]{:S(2)}, u32[]{:S(2)}) collective-permute-start(bf16[1024,448]{0,1:T(8,128)(2,1)} %collective-permute-done.5), channel_id=1, source_target_pairs={{8,0},{10,2},{12,4},{14,6},{16,8},{18,10},{20,12},{22,14},{24,16},... | collective-permute-start | bytes 2752520 | tf_op jit(solution)/shard_map/ppermute | solution.py:30
  98.6 12.6 %collective-permute-start.13 = (f32[8,128]{1,0:T(8,128)S(1)}, f32[8,128]{1,0:T(8,128)S(1)}, u32[]{:S(2)}, u32[]{:S(2)}) collective-permute-start(f32[8,128]{1,0:T(8,128)S(1)} %broadcast_in_dim.2), channel_id=1, source_target_pairs={{0,6},{2,4},{4,2},{6,0},{8,14},{10,12},{12,10},{14,8},{16,22},{18,... | collective-permute-start | bytes 12296 | tf_op jit(solution)/shard_map/ppermute | solution.py:24
  119.1 5.3 %collective-permute-start.16 = (f32[8,128]{1,0:T(8,128)S(1)}, f32[8,128]{1,0:T(8,128)S(1)}, u32[]{:S(2)}, u32[]{:S(2)}) collective-permute-start(f32[8,128]{1,0:T(8,128)S(1)} %add_add_fusion.2), channel_id=1, source_target_pairs={{0,24},{2,26},{4,28},{6,30},{8,0},{10,2},{12,4},{14,6},{16,8},{18,... | collective-permute-start | bytes 12296 | tf_op jit(solution)/shard_map/ppermute | solution.py:66
  124.3 4.5 %collective-permute-start.15 = (f32[8,128]{1,0:T(8,128)S(1)}, f32[8,128]{1,0:T(8,128)S(1)}, u32[]{:S(2)}, u32[]{:S(2)}) collective-permute-start(f32[8,128]{1,0:T(8,128)S(1)} %add_add_fusion.2), channel_id=1, source_target_pairs={{0,16},{2,18},{4,20},{6,22},{8,24},{10,26},{12,28},{14,30},{16,0},... | collective-permute-start | bytes 12296 | tf_op jit(solution)/shard_map/ppermute | solution.py:66
  128.8 5.7 %collective-permute-start.14 = (f32[8,128]{1,0:T(8,128)S(1)}, f32[8,128]{1,0:T(8,128)S(1)}, u32[]{:S(2)}, u32[]{:S(2)}) collective-permute-start(f32[8,128]{1,0:T(8,128)S(1)} %add_add_fusion.2), channel_id=1, source_target_pairs={{0,8},{2,10},{4,12},{6,14},{8,16},{10,18},{12,20},{14,22},{16,24},... | collective-permute-start | bytes 12296 | tf_op jit(solution)/shard_map/ppermute | solution.py:66
  155.7 14.7 %collective-permute-start.18 = (bf16[512,448]{0,1:T(8,128)(2,1)S(1)}, bf16[512,448]{0,1:T(8,128)(2,1)S(1)}, u32[]{:S(2)}, u32[]{:S(2)}) collective-permute-start(bf16[512,448]{0,1:T(8,128)(2,1)S(1)} %get-tuple-element.109), channel_id=1, source_target_pairs={{0,4},{2,6},{4,0},{6,2},{8,12},{10,14},{12,8},{14,10},{16,20},{18,... | collective-permute-start | bytes 1376264 | tf_op jit(solution)/shard_map/ppermute | solution.py:24
  157.1 12.3 %collective-permute-start.20 = (bf16[512,448]{0,1:T(8,128)(2,1)S(1)}, bf16[512,448]{0,1:T(8,128)(2,1)S(1)}, u32[]{:S(2)}, u32[]{:S(2)}) collective-permute-start(bf16[512,448]{0,1:T(8,128)(2,1)S(1)} %get-tuple-element.110), channel_id=1, source_target_pairs={{0,2},{2,0},{4,6},{6,4},{8,10},{10,8},{12,14},{14,12},{16,18},{18,... | collective-permute-start | bytes 1376264 | tf_op jit(solution)/shard_map/ppermute | solution.py:24
  169.7 21.3 %collective-permute-start.21 = (bf16[1024,448]{0,1:T(8,128)(2,1)S(1)}, bf16[1024,448]{0,1:T(8,128)(2,1)S(1)}, u32[]{:S(2)}, u32[]{:S(2)}) collective-permute-start(bf16[1024,448]{0,1:T(8,128)(2,1)S(1)} %pad_maximum_fusion.6), channel_id=1, source_target_pairs={{0,4},{2,6},{4,0},{6,2},{8,12},{10,14},{12,8},{14,10},{16,20},{18,... | collective-permute-start | bytes 2752520 | tf_op jit(solution)/shard_map/ppermute | solution.py:24
  170.7 21.0 %collective-permute-start.19 = (bf16[1024,448]{0,1:T(8,128)(2,1)S(1)}, bf16[1024,448]{0,1:T(8,128)(2,1)S(1)}, u32[]{:S(2)}, u32[]{:S(2)}) collective-permute-start(bf16[1024,448]{0,1:T(8,128)(2,1)S(1)} %pad_maximum_fusion.5), channel_id=1, source_target_pairs={{0,2},{2,0},{4,6},{6,4},{8,10},{10,8},{12,14},{14,12},{16,18},{18,... | collective-permute-start | bytes 2752520 | tf_op jit(solution)/shard_map/ppermute | solution.py:24
  192.4 20.1 %collective-permute-start.23 = (bf16[1024,448]{0,1:T(8,128)(2,1)S(1)}, bf16[1024,448]{0,1:T(8,128)(2,1)S(1)}, u32[]{:S(2)}, u32[]{:S(2)}) collective-permute-start(bf16[1024,448]{0,1:T(8,128)(2,1)S(1)} %divide_convert_fusion), channel_id=1, source_target_pairs={{0,4},{2,6},{4,0},{6,2},{8,12},{10,14},{12,8},{14,10},{16,20},{18,... | collective-permute-start | bytes 2752520 | tf_op jit(solution)/shard_map/ppermute | solution.py:24
  193.9 21.1 %collective-permute-start.22 = (bf16[1024,448]{0,1:T(8,128)(2,1)S(1)}, bf16[1024,448]{0,1:T(8,128)(2,1)S(1)}, u32[]{:S(2)}, u32[]{:S(2)}) collective-permute-start(bf16[1024,448]{0,1:T(8,128)(2,1)S(1)} %divide_convert_fusion), channel_id=1, source_target_pairs={{0,2},{2,0},{4,6},{6,4},{8,10},{10,8},{12,14},{14,12},{16,18},{18,... | collective-permute-start | bytes 2752520 | tf_op jit(solution)/shard_map/ppermute | solution.py:24
  213.4 12.1 %collective-permute-start.24 = (bf16[512,448]{0,1:T(8,128)(2,1)}, bf16[512,448]{0,1:T(8,128)(2,1)S(1)}, u32[]{:S(2)}, u32[]{:S(2)}) collective-permute-start(bf16[512,448]{0,1:T(8,128)(2,1)} %split.48), channel_id=1, source_target_pairs={{0,2},{2,0},{4,6},{6,4},{8,10},{10,8},{12,14},{14,12},{16,18},{18,... | collective-permute-start | bytes 1376264 | tf_op jit(solution)/shard_map/ppermute | solution.py:24
  215.8 9.7 %collective-permute-start.25 = (bf16[512,448]{0,1:T(8,128)(2,1)}, bf16[512,448]{0,1:T(8,128)(2,1)}, u32[]{:S(2)}, u32[]{:S(2)}) collective-permute-start(bf16[512,448]{0,1:T(8,128)(2,1)} %split.49), channel_id=1, source_target_pairs={{0,4},{2,6},{4,0},{6,2},{8,12},{10,14},{12,8},{14,10},{16,20},{18,... | collective-permute-start | bytes 1376264 | tf_op jit(solution)/shard_map/ppermute | solution.py:24
  234.3 20.2 %collective-permute-start.28 = (bf16[2,512,448]{1,2,0:T(8,128)(2,1)S(1)}, bf16[2,512,448]{1,2,0:T(8,128)(2,1)S(1)}, u32[]{:S(2)}, u32[]{:S(2)}) collective-permute-start(bf16[2,512,448]{1,2,0:T(8,128)(2,1)S(1)} %get-tuple-element.71), channel_id=1, source_target_pairs={{0,2},{2,0},{4,6},{6,4},{8,10},{10,8},{12,14},{14,12},{16,18},{18,... | collective-permute-start | bytes 2752520 | tf_op jit(solution)/shard_map/ppermute | solution.py:24
  234.9 19.6 %collective-permute-start.29 = (bf16[2,512,448]{1,2,0:T(8,128)(2,1)S(1)}, bf16[2,512,448]{1,2,0:T(8,128)(2,1)S(1)}, u32[]{:S(2)}, u32[]{:S(2)}) collective-permute-start(bf16[2,512,448]{1,2,0:T(8,128)(2,1)S(1)} %get-tuple-element.72), channel_id=1, source_target_pairs={{0,4},{2,6},{4,0},{6,2},{8,12},{10,14},{12,8},{14,10},{16,20},{18,... | collective-permute-start | bytes 2752520 | tf_op jit(solution)/shard_map/ppermute | solution.py:24
  235.5 18.9 %collective-permute-start.26 = (bf16[448,1024]{1,0:T(8,128)(2,1)S(1)}, bf16[448,1024]{1,0:T(8,128)(2,1)S(1)}, u32[]{:S(2)}, u32[]{:S(2)}) collective-permute-start(bf16[448,1024]{1,0:T(8,128)(2,1)S(1)} %get-tuple-element.113), channel_id=1, source_target_pairs={{0,8},{2,10},{4,12},{6,14},{8,16},{10,18},{12,20},{14,22},{16,24},... | collective-permute-start | bytes 2752520 | tf_op jit(solution)/shard_map/ppermute | solution.py:27
  237.2 19.8 %collective-permute-start.27 = (bf16[448,1024]{1,0:T(8,128)(2,1)S(1)}, bf16[448,1024]{1,0:T(8,128)(2,1)S(1)}, u32[]{:S(2)}, u32[]{:S(2)}) collective-permute-start(bf16[448,1024]{1,0:T(8,128)(2,1)S(1)} %get-tuple-element.115), channel_id=1, source_target_pairs={{8,0},{10,2},{12,4},{14,6},{16,8},{18,10},{20,12},{22,14},{24,16},... | collective-permute-start | bytes 2752520 | tf_op jit(solution)/shard_map/ppermute | solution.py:30
  257.5 19.1 %collective-permute-start.31 = (bf16[448,1024]{1,0:T(8,128)(2,1)S(1)}, bf16[448,1024]{1,0:T(8,128)(2,1)}, u32[]{:S(2)}, u32[]{:S(2)}) collective-permute-start(bf16[448,1024]{1,0:T(8,128)(2,1)S(1)} %get-tuple-element.107), channel_id=1, source_target_pairs={{8,0},{10,2},{12,4},{14,6},{16,8},{18,10},{20,12},{22,14},{24,16},... | collective-permute-start | bytes 2752520 | tf_op jit(solution)/shard_map/ppermute | solution.py:30
  258.8 18.7 %collective-permute-start.30 = (bf16[448,1024]{1,0:T(8,128)(2,1)S(1)}, bf16[448,1024]{1,0:T(8,128)(2,1)}, u32[]{:S(2)}, u32[]{:S(2)}) collective-permute-start(bf16[448,1024]{1,0:T(8,128)(2,1)S(1)} %get-tuple-element.108), channel_id=1, source_target_pairs={{0,8},{2,10},{4,12},{6,14},{8,16},{10,18},{12,20},{14,22},{16,24},... | collective-permute-start | bytes 2752520 | tf_op jit(solution)/shard_map/ppermute | solution.py:27
  264.3 17.3 %collective-permute-start.32 = (bf16[2,512,448]{1,2,0:T(8,128)(2,1)S(1)}, bf16[2,512,448]{1,2,0:T(8,128)(2,1)S(1)}, u32[]{:S(2)}, u32[]{:S(2)}) collective-permute-start(bf16[2,512,448]{1,2,0:T(8,128)(2,1)S(1)} %get-tuple-element.76), channel_id=1, source_target_pairs={{0,6},{2,4},{4,2},{6,0},{8,14},{10,12},{12,10},{14,8},{16,22},{18,... | collective-permute-start | bytes 2752520 | tf_op jit(solution)/shard_map/ppermute | solution.py:24
  285.9 16.6 %collective-permute-start.33 = (bf16[448,1024]{1,0:T(8,128)(2,1)S(1)}, bf16[448,1024]{1,0:T(8,128)(2,1)S(1)}, u32[]{:S(2)}, u32[]{:S(2)}) collective-permute-start(bf16[448,1024]{1,0:T(8,128)(2,1)S(1)} %fusion.19), channel_id=1, source_target_pairs={{0,8},{2,10},{4,12},{6,14},{8,16},{10,18},{12,20},{14,22},{16,24},... | collective-permute-start | bytes 2752520 | tf_op jit(solution)/shard_map/ppermute | solution.py:27
  290.5 20.3 %collective-permute-start.34 = (bf16[448,1024]{1,0:T(8,128)(2,1)S(1)}, bf16[448,1024]{1,0:T(8,128)(2,1)S(1)}, u32[]{:S(2)}, u32[]{:S(2)}) collective-permute-start(bf16[448,1024]{1,0:T(8,128)(2,1)S(1)} %fusion.12), channel_id=1, source_target_pairs={{8,0},{10,2},{12,4},{14,6},{16,8},{18,10},{20,12},{22,14},{24,16},... | collective-permute-start | bytes 2752520 | tf_op jit(solution)/shard_map/ppermute | solution.py:30
  291.8 9.2 %collective-permute-start.35 = (bf16[256,1024]{1,0:T(8,128)(2,1)S(1)}, bf16[256,1024]{1,0:T(8,128)(2,1)S(1)}, u32[]{:S(2)}, u32[]{:S(2)}) collective-permute-start(bf16[256,1024]{1,0:T(8,128)(2,1)S(1)} %copy-done.16), channel_id=1, source_target_pairs={{0,2},{2,0},{4,6},{6,4},{8,10},{10,8},{12,14},{14,12},{16,18},{18,... | collective-permute-start | bytes 1572872 | tf_op jit(solution)/shard_map/ppermute | solution.py:24
  293.3 9.2 %collective-permute-start.36 = (bf16[256,1024]{1,0:T(8,128)(2,1)S(1)}, bf16[256,1024]{1,0:T(8,128)(2,1)S(1)}, u32[]{:S(2)}, u32[]{:S(2)}) collective-permute-start(bf16[256,1024]{1,0:T(8,128)(2,1)S(1)} %split.41), channel_id=1, source_target_pairs={{0,4},{2,6},{4,0},{6,2},{8,12},{10,14},{12,8},{14,10},{16,20},{18,... | collective-permute-start | bytes 1572872 | tf_op jit(solution)/shard_map/ppermute | solution.py:24
  311.4 20.3 %collective-permute-start.38 = (bf16[448,1024]{1,0:T(8,128)(2,1)S(1)}, bf16[448,1024]{1,0:T(8,128)(2,1)}, u32[]{:S(2)}, u32[]{:S(2)}) collective-permute-start(bf16[448,1024]{1,0:T(8,128)(2,1)S(1)} %fusion.8), channel_id=1, source_target_pairs={{8,0},{10,2},{12,4},{14,6},{16,8},{18,10},{20,12},{22,14},{24,16},... | collective-permute-start | bytes 2752520 | tf_op jit(solution)/shard_map/ppermute | solution.py:30
  312.7 20.3 %collective-permute-start.37 = (bf16[448,1024]{1,0:T(8,128)(2,1)S(1)}, bf16[448,1024]{1,0:T(8,128)(2,1)}, u32[]{:S(2)}, u32[]{:S(2)}) collective-permute-start(bf16[448,1024]{1,0:T(8,128)(2,1)S(1)} %fusion.8), channel_id=1, source_target_pairs={{0,8},{2,10},{4,12},{6,14},{8,16},{10,18},{12,20},{14,22},{16,24},... | collective-permute-start | bytes 2752520 | tf_op jit(solution)/shard_map/ppermute | solution.py:27
  331.7 21.0 %collective-permute-start.39 = (bf16[448,1024]{1,0:T(8,128)(2,1)}, bf16[448,1024]{1,0:T(8,128)(2,1)}, u32[]{:S(2)}, u32[]{:S(2)}) collective-permute-start(bf16[448,1024]{1,0:T(8,128)(2,1)} %collective-permute-done.38), channel_id=1, source_target_pairs={{8,0},{10,2},{12,4},{14,6},{16,8},{18,10},{20,12},{22,14},{24,16},... | collective-permute-start | bytes 2752520 | tf_op jit(solution)/shard_map/ppermute | solution.py:30
  333.0 21.4 %collective-permute-start.41 = (bf16[448,1024]{1,0:T(8,128)(2,1)}, bf16[448,1024]{1,0:T(8,128)(2,1)}, u32[]{:S(2)}, u32[]{:S(2)}) collective-permute-start(bf16[448,1024]{1,0:T(8,128)(2,1)} %collective-permute-done.37), channel_id=1, source_target_pairs={{0,8},{2,10},{4,12},{6,14},{8,16},{10,18},{12,20},{14,22},{16,24},... | collective-permute-start | bytes 2752520 | tf_op jit(solution)/shard_map/ppermute | solution.py:27
  341.3 4.5 %collective-permute-start.45 = (s32[512]{0:T(512)S(1)}, s32[512]{0:T(512)S(1)}, u32[]{:S(2)}, u32[]{:S(2)}) collective-permute-start(s32[512]{0:T(512)S(1)} %copy-done.21), channel_id=1, source_target_pairs={{0,6},{2,4},{4,2},{6,0},{8,14},{10,12},{12,10},{14,8},{16,22},{18,... | collective-permute-start | bytes 6152 | tf_op jit(solution)/shard_map/ppermute | solution.py:24
  352.7 15.9 %collective-permute-start.40 = (bf16[448,1024]{1,0:T(8,128)(2,1)}, bf16[448,1024]{1,0:T(8,128)(2,1)}, u32[]{:S(2)}, u32[]{:S(2)}) collective-permute-start(bf16[448,1024]{1,0:T(8,128)(2,1)} %collective-permute-done.39), channel_id=1, source_target_pairs={{8,0},{10,2},{12,4},{14,6},{16,8},{18,10},{20,12},{22,14},{24,16},... | collective-permute-start | bytes 2752520 | tf_op jit(solution)/shard_map/ppermute | solution.py:30
  354.4 17.9 %collective-permute-start.42 = (bf16[448,1024]{1,0:T(8,128)(2,1)}, bf16[448,1024]{1,0:T(8,128)(2,1)S(1)}, u32[]{:S(2)}, u32[]{:S(2)}) collective-permute-start(bf16[448,1024]{1,0:T(8,128)(2,1)} %collective-permute-done.41), channel_id=1, source_target_pairs={{0,8},{2,10},{4,12},{6,14},{8,16},{10,18},{12,20},{14,22},{16,24},... | collective-permute-start | bytes 2752520 | tf_op jit(solution)/shard_map/ppermute | solution.py:27
  376.8 4.5 %collective-permute-start.48 = (f32[32]{0:T(128)S(1)}, f32[32]{0:T(128)S(1)}, u32[]{:S(2)}, u32[]{:S(2)}) collective-permute-start(f32[32]{0:T(128)S(1)} %convolution_bitcast_fusion), channel_id=1, source_target_pairs={{0,6},{2,4},{4,2},{6,0},{8,14},{10,12},{12,10},{14,8},{16,22},{18,... | collective-permute-start | bytes 392 | tf_op jit(solution)/shard_map/ppermute | solution.py:24
  383.7 4.7 %collective-permute-start.50 = (f32[32]{0:T(128)S(1)}, f32[32]{0:T(128)S(1)}, u32[]{:S(2)}, u32[]{:S(2)}) collective-permute-start(f32[32]{0:T(128)S(1)} %add_add_fusion.4), channel_id=1, source_target_pairs={{0,16},{2,18},{4,20},{6,22},{8,24},{10,26},{12,28},{14,30},{16,0},... | collective-permute-start | bytes 392 | tf_op jit(solution)/shard_map/ppermute | solution.py:66
  386.9 5.3 %collective-permute-start.49 = (f32[32]{0:T(128)S(1)}, f32[32]{0:T(128)S(1)}, u32[]{:S(2)}, u32[]{:S(2)}) collective-permute-start(f32[32]{0:T(128)S(1)} %add_add_fusion.4), channel_id=1, source_target_pairs={{0,8},{2,10},{4,12},{6,14},{8,16},{10,18},{12,20},{14,22},{16,24},... | collective-permute-start | bytes 392 | tf_op jit(solution)/shard_map/ppermute | solution.py:66
  (35 other events, 333.1 us)
Sparse Core Ops, SparseCore 0:
  8.9 12.8 all-gather.8
  23.4 11.7 all-gather.6
  88.3 18.8 all-gather.10
  283.9 18.4 all-gather.12

commit v4 on v3

--- a/solution.py
+++ b/solution.py
@@ -44,7 +44,7 @@
         second = swap(halves(from_x, axis)[1], 2)
         return jnp.concatenate([first, second], axis=axis)
 
-    def line_gather(v, extras, tail=None):
+    def line_gather(v, extras, tail=None, rounds=(), state=None):
         rights, lefts = [v], [v]
         moved = []
         for t in range(outer - 1):
@@ -52,26 +52,35 @@
             if extras:
                 pair, arrived, extras = beside(pair, extras[0], extras[1:])
                 moved += arrived
+            if t < len(rounds):
+                pair, state = lax.optimization_barrier((pair, rounds[t](state)))
             if tail is not None and t == outer - 2:
-                pair, kept = lax.optimization_barrier((pair, tail(moved)))
+                pair, kept = lax.optimization_barrier((pair, tail(moved, state)))
                 moved = (moved, kept)
             rights.append(pair[0])
             lefts.append(pair[1])
         blocks = [v] + [jnp.where(s <= o, rights[s], lefts[outer - s]) for s in range(1, outer)]
         return blocks, moved
 
-    def sum_over_devices(v):
-        v = v + sum(swap(v, j) for j in range(1, IN))
+    def over_plane(v):
+        return v + sum(swap(v, j) for j in range(1, IN))
+
+    def over_line(v):
         shifts = [
             lax.ppermute(v, "dp", [(i, (i + s * IN) % n) for i in range(n)])
             for s in range(1, outer)
         ]
-        v = v + sum(shifts)
+        return v + sum(shifts)
+
+    def over_cores(v):
         m = lax.axis_size("mp")
         others = [
             lax.ppermute(v, "mp", [(i, (i + s) % m) for i in range(m)]) for s in range(1, m)
         ]
         return v + sum(others)
+
+    def sum_over_devices(v):
+        return over_cores(over_line(over_plane(v)))
 
     def pick(gathered, s):
         k = (o - s) % outer
@@ -90,19 +99,21 @@
     x_full = lax.all_gather(inputs, "mp", axis=1, tiled=True)
     proj = jnp.dot(x_full, basis_in, preferred_element_type=F32).astype(BF)
 
-    def prepare(got):
+    def prepare(got, scale_sum):
         q_all = lax.all_gather(jnp.stack([sends[0]] + got[:3], axis=1), "mp", axis=0)
         q_rel = jnp.stack([pick(q_all, s) for s in range(outer)])
-        part_sum = jnp.broadcast_to(jnp.sum(eigen_scales), (8, 128))
-        damping = damping_ratio * sum_over_devices(part_sum)[:1, :1] / (d_in * f_all)
-        return q_rel, damping
+        return q_rel, damping_ratio * scale_sum[:1, :1] / (d_in * f_all)
 
     u_rel, (got, (q_rel, damping)) = line_gather(
         u,
-        [[(sends[1], 1), (sends[2], 2)], [(sends[3], 3)], [(proj, 1), (proj, 2)]],
+        [[(sends[1], 1), (sends[2], 2)], [(sends[3], 3)] + [(segment_ids, j) for j in range(1, IN)],
+         [(proj, 1), (proj, 2)]],
         prepare,
+        (over_plane, over_line, over_cores),
+        jnp.broadcast_to(jnp.sum(eigen_scales), (8, 128)),
     )
-    proj_x, proj_y = got[3:]
+    ids = jnp.concatenate([segment_ids] + got[3:6])
+    proj_x, proj_y = got[6:]
     u_cat = jnp.concatenate(u_rel, axis=1)
 
     def term(j):
@@ -156,7 +167,6 @@
     back_rel, _ = line_gather(back, [])
     g_all = lax.all_gather(jnp.concatenate(g, axis=1), "mp", axis=0)
     projs = [proj, proj_x, proj_y] + moved[3:]
-    ids = jnp.concatenate([segment_ids] + [swap(segment_ids, j) for j in range(1, IN)])
     proj_all = jnp.concatenate(projs)
     score = 0.0
     for s in range(outer):

time: 407 us -> 393 us (0.966)
  waiting for transfers between devices: 169 us -> 159 us
  local copies, waits for them, and re-layouts: 35 us -> 30.2 us
    ppermute x9, waiting for transfers between devices: 1.4 us -> 26.7 us  [right(): return lax.ppermute(v, 'dp', [(i, i + IN) for i in range(n - IN)])]
    ppermute x27, waiting for transfers between devices: 106 us -> 81.6 us  [swap(): return lax.ppermute(v, 'dp', [(i, i ^ j) for i in range(n)])]
    ppermute x8, waiting for transfers between devices: 15.7 us -> 5.77 us  [the longest x6 4.65 us: over_line(): lax.ppermute(v, 'dp', [(i, (i + s * IN) % n) for i in range(n)])]
    all_gather x1, waiting for transfers between devices: 8.03 us -> 2.32 us  [on_device(): w_full = lax.all_gather(query_grad, 'mp', axis=0, tiled=True)]
    ppermute x9, waiting for transfers between devices: 36.7 us -> 41 us  [left(): return lax.ppermute(v, 'dp', [(i, i - IN) for i in range(IN, n)])]
  transfers between devices with their start and end apart: 57 -> 57, of which waited for: 35 -> 32; matrix products, arithmetic and copies ran while one was open for 18% -> 17% of each run, Pallas kernels for 0% -> 0%
where the time goes in v4:
time: 393 us; the launch traced here: 386 us
  waiting for transfers between devices  159 us (40%)
  starting transfers between devices  110 us (28%)
  matrix products  52.7 us (13%)
  local copies, waits for them, and re-layouts  30.2 us (8%)
  other arithmetic  19.5 us (5%)
  between operations  14.8 us (4%)
    ppermute x27, waiting for transfers between devices, swap(): return lax.ppermute(v, 'dp', [(i, i ^ j) for i in range(n)])  81.6 us
    ppermute x9, waiting for transfers between devices, left(): return lax.ppermute(v, 'dp', [(i, i - IN) for i in range(IN, n)])  41 us
    ppermute x9, starting transfers between devices, right(): return lax.ppermute(v, 'dp', [(i, i + IN) for i in range(n - IN)])  40.1 us
    ppermute x27, starting transfers between devices, swap(): return lax.ppermute(v, 'dp', [(i, i ^ j) for i in range(n)])  34.1 us
    ppermute x9, waiting for transfers between devices, right(): return lax.ppermute(v, 'dp', [(i, i + IN) for i in range(n - IN)])  26.7 us
    ppermute x9, starting transfers between devices, left(): return lax.ppermute(v, 'dp', [(i, i - IN) for i in range(IN, n)])  23.6 us
    unnamed x57, local copies, waits for them, and re-layouts  16.4 us
    dot_general x4, matrix products, on_device(): lax.dot_general(pick(g_all, s), back_rel[s], (((1,), (0,)), ((), ())), pr...  14.9 us
  transfers between devices with their start and end apart: 57, of which 32 were waited for; matrix products, arithmetic and copies ran while one was open for 17% of the time, Pallas kernels for 0%

profile of v4, /device:TPU:0, one launch (start us, length us, event | category | flops | bytes accessed | tf_op | source)
XLA Modules:
  0.0 386.5 jit_solution(13373655637913292707)
XLA Ops:
  8.1 2.6 reduce_sum.45
  11.3 4.0 %collective-permute-start.6 = (f32[8,128]{1,0:T(8,128)S(1)}, f32[8,128]{1,0:T(8,128)S(1)}, u32[]{:S(2)}, u32[]{:S(2)}) collective-permute-start(f32[8,128]{1,0:T(8,128)S(1)} %broadcast_in_dim.2), channel_id=1, source_target_pairs={{0,6},{2,4},{4,2},{6,0},{8,14},{10,12},{12,10},{14,8},{16,22},{18,... | collective-permute-start | bytes 12296 | tf_op jit(solution)/shard_map/ppermute | solution.py:24
  15.9 3.6 copy.11
  21.8 5.9 %convolution_convert_fusion.1 = bf16[1024,448]{0,1:T(8,128)(2,1)} fusion(bf16[2048,448]{0,1:T(8,128)(2,1)} %all-gather.9.cloned.1.call-done, bf16[2048,1024]{1,0:T(8,128)(2,1)} %param.8), kind=kOutput, calls=%fused_computation.52 | convolution fusion | flops 1879506944 | bytes 6946816 | tf_op jit(solution)/shard_map/dot_general | solution.py:92
  29.0 5.5 %collective-permute-start = (bf16[1024,448]{0,1:T(8,128)(2,1)}, bf16[1024,448]{0,1:T(8,128)(2,1)}, u32[]{:S(2)}, u32[]{:S(2)}) collective-permute-start(bf16[1024,448]{0,1:T(8,128)(2,1)} %convolution_convert_fusion.1), channel_id=1, source_target_pairs={{0,8},{2,10},{4,12},{6,14},{8,16},{10,18},{12,20},{14,22},{16,24},... | collective-permute-start | bytes 2752520 | tf_op jit(solution)/shard_map/ppermute | solution.py:27
  40.0 6.6 %constant_dynamic-update-slice_fusion.4 = (bf16[2048,1024]{1,0:T(8,128)(2,1)}, bf16[512,1024]{1,0:T(8,128)(2,1)}) fusion(bf16[512,2048]{1,0:T(8,128)(2,1)} %all-gather.7.cloned.1.call-done, bf16[2048,1024]{1,0:T(8,128)(2,1)} %param.8), kind=kOutput, calls=%fused_computation.86 | convolution fusion | flops 2148007936 | bytes 8388608 | tf_op jit(solution)/shard_map/dot_general | solution.py:100
  46.6 11.7 %collective-permute-done.3 = bf16[2,448,448]{2,1,0:T(8,128)(2,1)S(1)} collective-permute-done((bf16[2,448,448]{2,1,0:T(8,128)(2,1)}, bf16[2,448,448]{2,1,0:T(8,128)(2,1)S(1)}, u32[]{:S(2)}, u32[]{:S(2)}) %collective-permute-start.3) | collective-permute-done | bytes 802848 | tf_op jit(solution)/shard_map/ppermute | solution.py:24
  59.8 3.4 collective-permute-start.7
  68.0 17.1 %collective-permute-done.10 = s32[512]{0:T(512)S(1)} collective-permute-done((s32[512]{0:T(512)S(1)}, s32[512]{0:T(512)S(1)}, u32[]{:S(2)}, u32[]{:S(2)}) %collective-permute-start.10) | collective-permute-done | bytes 2080 | tf_op jit(solution)/shard_map/ppermute | solution.py:24
  91.9 4.0 %collective-permute-start.15 = (f32[8,128]{1,0:T(8,128)S(1)}, f32[8,128]{1,0:T(8,128)S(1)}, u32[]{:S(2)}, u32[]{:S(2)}) collective-permute-start(f32[8,128]{1,0:T(8,128)S(1)} %add_add_fusion.2), channel_id=1, source_target_pairs={{0,24},{2,26},{4,28},{6,30},{8,0},{10,2},{12,4},{14,6},{16,8},{18,... | collective-permute-start | bytes 12296 | tf_op jit(solution)/shard_map/ppermute | solution.py:70
  101.3 3.8 collective-permute-start.16
  108.3 10.7 %collective-permute-done.16 = bf16[1024,448]{0,1:T(8,128)(2,1)} collective-permute-done((bf16[1024,448]{0,1:T(8,128)(2,1)}, bf16[1024,448]{0,1:T(8,128)(2,1)}, u32[]{:S(2)}, u32[]{:S(2)}) %collective-permute-start.16) | collective-permute-done | bytes 917536 | tf_op jit(solution)/shard_map/ppermute | solution.py:27
  119.1 5.0 %collective-permute-done.17 = bf16[1024,448]{0,1:T(8,128)(2,1)} collective-permute-done((bf16[1024,448]{0,1:T(8,128)(2,1)}, bf16[1024,448]{0,1:T(8,128)(2,1)}, u32[]{:S(2)}, u32[]{:S(2)}) %collective-permute-start.17) | collective-permute-done | bytes 917536 | tf_op jit(solution)/shard_map/ppermute | solution.py:30
  125.3 3.6 dynamic-slice_bitcast_fusion.3
  131.1 2.4 copy-done
  135.1 3.2 fusion.44
  138.3 3.5 convolution_convert_fusion.2
  143.4 3.1 fusion.43
  146.7 8.2 %collective-permute-done.23 = bf16[512,448]{0,1:T(8,128)(2,1)S(1)} collective-permute-done((bf16[512,448]{0,1:T(8,128)(2,1)S(1)}, bf16[512,448]{0,1:T(8,128)(2,1)S(1)}, u32[]{:S(2)}, u32[]{:S(2)}) %collective-permute-start.23) | collective-permute-done | bytes 458784 | tf_op jit(solution)/shard_map/ppermute | solution.py:24
  157.5 3.3 fusion.45
  160.7 14.0 %collective-permute-done.24 = bf16[1024,448]{0,1:T(8,128)(2,1)S(1)} collective-permute-done((bf16[1024,448]{0,1:T(8,128)(2,1)S(1)}, bf16[1024,448]{0,1:T(8,128)(2,1)S(1)}, u32[]{:S(2)}, u32[]{:S(2)}) %collective-permute-start.24) | collective-permute-done | bytes 917536 | tf_op jit(solution)/shard_map/ppermute | solution.py:24
  178.3 15.9 %collective-permute-done.26 = bf16[1024,448]{0,1:T(8,128)(2,1)S(1)} collective-permute-done((bf16[1024,448]{0,1:T(8,128)(2,1)S(1)}, bf16[1024,448]{0,1:T(8,128)(2,1)S(1)}, u32[]{:S(2)}, u32[]{:S(2)}) %collective-permute-start.26) | collective-permute-done | bytes 917536 | tf_op jit(solution)/shard_map/ppermute | solution.py:24
  198.3 5.9 %copy.12 = bf16[512,3584]{0,1:T(8,128)(2,1)} copy(bf16[512,3584]{1,0:T(8,128)(2,1)} %param.12) | data formatting | bytes 7340032 | tf_op args[5]
  204.2 2.6 dynamic-slice_bitcast_fusion.4
  209.3 3.1 bitcast_convert_fusion
  212.4 3.1 bitcast_convert_fusion.1
  217.5 3.0 collective-permute-start.29
  220.5 13.4 %collective-permute-start.30 = (bf16[448,1024]{1,0:T(8,128)(2,1)S(1)}, bf16[448,1024]{1,0:T(8,128)(2,1)S(1)}, u32[]{:S(2)}, u32[]{:S(2)}) collective-permute-start(bf16[448,1024]{1,0:T(8,128)(2,1)S(1)} %get-tuple-element.145), channel_id=1, source_target_pairs={{8,0},{10,2},{12,4},{14,6},{16,8},{18,10},{20,12},{22,14},{24,16},... | collective-permute-start | bytes 2752520 | tf_op jit(solution)/shard_map/ppermute | solution.py:30
  236.6 6.9 %collective-permute-done.30 = bf16[448,1024]{1,0:T(8,128)(2,1)S(1)} collective-permute-done((bf16[448,1024]{1,0:T(8,128)(2,1)S(1)}, bf16[448,1024]{1,0:T(8,128)(2,1)S(1)}, u32[]{:S(2)}, u32[]{:S(2)}) %collective-permute-start.30) | collective-permute-done | bytes 917536 | tf_op jit(solution)/shard_map/ppermute | solution.py:30
  245.3 5.5 %collective-permute-start.33 = (bf16[448,1024]{1,0:T(8,128)(2,1)S(1)}, bf16[448,1024]{1,0:T(8,128)(2,1)}, u32[]{:S(2)}, u32[]{:S(2)}) collective-permute-start(bf16[448,1024]{1,0:T(8,128)(2,1)S(1)} %get-tuple-element.138), channel_id=1, source_target_pairs={{0,8},{2,10},{4,12},{6,14},{8,16},{10,18},{12,20},{14,22},{16,24},... | collective-permute-start | bytes 2752520 | tf_op jit(solution)/shard_map/ppermute | solution.py:27
  252.4 9.7 %collective-permute-done.34 = bf16[448,1024]{1,0:T(8,128)(2,1)S(1)} collective-permute-done((bf16[448,1024]{1,0:T(8,128)(2,1)S(1)}, bf16[448,1024]{1,0:T(8,128)(2,1)S(1)}, u32[]{:S(2)}, u32[]{:S(2)}) %collective-permute-start.34) | collective-permute-done | bytes 917536 | tf_op jit(solution)/shard_map/ppermute | solution.py:30
  262.1 7.5 %collective-permute-done.33 = bf16[448,1024]{1,0:T(8,128)(2,1)} collective-permute-done((bf16[448,1024]{1,0:T(8,128)(2,1)S(1)}, bf16[448,1024]{1,0:T(8,128)(2,1)}, u32[]{:S(2)}, u32[]{:S(2)}) %collective-permute-start.33) | collective-permute-done | bytes 917536 | tf_op jit(solution)/shard_map/ppermute | solution.py:27
  275.2 3.5 collective-permute-start.36
  280.4 3.4 collective-permute-start.38
  283.9 3.7 fusion.9
  287.6 3.4 collective-permute-done.38
  293.0 4.0 %collective-permute-done.36 = bf16[448,1024]{1,0:T(8,128)(2,1)S(1)} collective-permute-done((bf16[448,1024]{1,0:T(8,128)(2,1)S(1)}, bf16[448,1024]{1,0:T(8,128)(2,1)S(1)}, u32[]{:S(2)}, u32[]{:S(2)}) %collective-permute-start.36) | collective-permute-done | bytes 917536 | tf_op jit(solution)/shard_map/ppermute | solution.py:27
  299.4 5.5 %collective-permute-start.40 = (bf16[448,1024]{1,0:T(8,128)(2,1)S(1)}, bf16[448,1024]{1,0:T(8,128)(2,1)}, u32[]{:S(2)}, u32[]{:S(2)}) collective-permute-start(bf16[448,1024]{1,0:T(8,128)(2,1)S(1)} %fusion.8), channel_id=1, source_target_pairs={{0,8},{2,10},{4,12},{6,14},{8,16},{10,18},{12,20},{14,22},{16,24},... | collective-permute-start | bytes 2752520 | tf_op jit(solution)/shard_map/ppermute | solution.py:27
  304.9 13.5 %collective-permute-done.41 = bf16[448,1024]{1,0:T(8,128)(2,1)} collective-permute-done((bf16[448,1024]{1,0:T(8,128)(2,1)S(1)}, bf16[448,1024]{1,0:T(8,128)(2,1)}, u32[]{:S(2)}, u32[]{:S(2)}) %collective-permute-start.41) | collective-permute-done | bytes 917536 | tf_op jit(solution)/shard_map/ppermute | solution.py:30
  320.1 5.4 %collective-permute-start.44 = (bf16[448,1024]{1,0:T(8,128)(2,1)}, bf16[448,1024]{1,0:T(8,128)(2,1)}, u32[]{:S(2)}, u32[]{:S(2)}) collective-permute-start(bf16[448,1024]{1,0:T(8,128)(2,1)} %collective-permute-done.40), channel_id=1, source_target_pairs={{0,8},{2,10},{4,12},{6,14},{8,16},{10,18},{12,20},{14,22},{16,24},... | collective-permute-start | bytes 2752520 | tf_op jit(solution)/shard_map/ppermute | solution.py:27
  330.1 5.2 %collective-permute-done.42 = bf16[448,1024]{1,0:T(8,128)(2,1)} collective-permute-done((bf16[448,1024]{1,0:T(8,128)(2,1)}, bf16[448,1024]{1,0:T(8,128)(2,1)}, u32[]{:S(2)}, u32[]{:S(2)}) %collective-permute-start.42) | collective-permute-done | bytes 917536 | tf_op jit(solution)/shard_map/ppermute | solution.py:30
  336.5 4.1 %collective-permute-done.44 = bf16[448,1024]{1,0:T(8,128)(2,1)} collective-permute-done((bf16[448,1024]{1,0:T(8,128)(2,1)}, bf16[448,1024]{1,0:T(8,128)(2,1)}, u32[]{:S(2)}, u32[]{:S(2)}) %collective-permute-start.44) | collective-permute-done | bytes 917536 | tf_op jit(solution)/shard_map/ppermute | solution.py:27
  340.7 4.4 %collective-permute-start.45 = (bf16[448,1024]{1,0:T(8,128)(2,1)}, bf16[448,1024]{1,0:T(8,128)(2,1)S(1)}, u32[]{:S(2)}, u32[]{:S(2)}) collective-permute-start(bf16[448,1024]{1,0:T(8,128)(2,1)} %collective-permute-done.44), channel_id=1, source_target_pairs={{0,8},{2,10},{4,12},{6,14},{8,16},{10,18},{12,20},{14,22},{16,24},... | collective-permute-start | bytes 2752520 | tf_op jit(solution)/shard_map/ppermute | solution.py:27
  345.2 5.7 %fusion.2 = f32[2048]{0:T(1024)S(1)} fusion(bf16[2048,1024]{1,0:T(8,128)(2,1)} %constant_dynamic-update-slice_fusion, bf16[2,2,2048,448]{2,3,1,0:T(8,128)(2,1)} %bitcast.131, s32[]{:T(128)S(6)} %select_n.211, s32[]{:T(128)S(6)} %select_n.214, bf16[448,1024]{1,0:T(8,128)(2,1)} %collective-permute-done.44, bf16[448,1024]{1,0:T(8,128)(2,1)} %collective-permute-done.42, ...), kind=kOutput, calls=%fused_computation.6 | convolution fusion | flops 1885796352 | bytes 7872521 | tf_op jit(solution)/shard_map/dot_general | solution.py:173
  351.5 2.7 fusion
  354.1 2.7 fusion.1
  356.8 3.9 fusion.3
  367.6 3.8 collective-permute-start.51
  (183 shorter events, 94.9 us)
Async XLA Ops:
  6.5 15.3 %all-gather.9.cloned.1.call-start = ((), (), s32[]{:S(2)}) async-start(), calls=%async_computation.1 | async-start | bytes 2752512 | tf_op jit(solution)/shard_map/all_gather | solution.py:91
  7.3 32.8 %all-gather.7.cloned.1.call-start = ((), (), s32[]{:S(2)}) async-start(), calls=%async_computation | async-start | bytes 3145728 | tf_op jit(solution)/shard_map/all_gather | solution.py:99
  8.0 117.3 %all-gather.11.cloned.1.call-start = ((), (), s32[]{:S(2)}) async-start(), calls=%async_computation.2 | async-start | bytes 11010048 | tf_op jit(solution)/shard_map/all_gather | solution.py:103
  11.3 24.8 %collective-permute-start.6 = (f32[8,128]{1,0:T(8,128)S(1)}, f32[8,128]{1,0:T(8,128)S(1)}, u32[]{:S(2)}, u32[]{:S(2)}) collective-permute-start(f32[8,128]{1,0:T(8,128)S(1)} %broadcast_in_dim.2), channel_id=1, source_target_pairs={{0,6},{2,4},{4,2},{6,0},{8,14},{10,12},{12,10},{14,8},{16,22},{18,... | collective-permute-start | bytes 12296 | tf_op jit(solution)/shard_map/ppermute | solution.py:24
  15.2 22.6 %collective-permute-start.5 = (f32[8,128]{1,0:T(8,128)S(1)}, f32[8,128]{1,0:T(8,128)S(1)}, u32[]{:S(2)}, u32[]{:S(2)}) collective-permute-start(f32[8,128]{1,0:T(8,128)S(1)} %broadcast_in_dim.2), channel_id=1, source_target_pairs={{0,4},{2,6},{4,0},{6,2},{8,12},{10,14},{12,8},{14,10},{16,20},{18,... | collective-permute-start | bytes 12296 | tf_op jit(solution)/shard_map/ppermute | solution.py:24
  15.8 23.6 %collective-permute-start.4 = (f32[8,128]{1,0:T(8,128)S(1)}, f32[8,128]{1,0:T(8,128)S(1)}, u32[]{:S(2)}, u32[]{:S(2)}) collective-permute-start(f32[8,128]{1,0:T(8,128)S(1)} %broadcast_in_dim.2), channel_id=1, source_target_pairs={{0,2},{2,0},{4,6},{6,4},{8,10},{10,8},{12,14},{14,12},{16,18},{18,... | collective-permute-start | bytes 12296 | tf_op jit(solution)/shard_map/ppermute | solution.py:24
  27.7 32.1 %collective-permute-start.1 = (bf16[1024,448]{0,1:T(8,128)(2,1)}, bf16[1024,448]{0,1:T(8,128)(2,1)}, u32[]{:S(2)}, u32[]{:S(2)}) collective-permute-start(bf16[1024,448]{0,1:T(8,128)(2,1)} %convolution_convert_fusion.1), channel_id=1, source_target_pairs={{8,0},{10,2},{12,4},{14,6},{16,8},{18,10},{20,12},{22,14},{24,16},... | collective-permute-start | bytes 2752520 | tf_op jit(solution)/shard_map/ppermute | solution.py:30
  29.0 30.8 %collective-permute-start = (bf16[1024,448]{0,1:T(8,128)(2,1)}, bf16[1024,448]{0,1:T(8,128)(2,1)}, u32[]{:S(2)}, u32[]{:S(2)}) collective-permute-start(bf16[1024,448]{0,1:T(8,128)(2,1)} %convolution_convert_fusion.1), channel_id=1, source_target_pairs={{0,8},{2,10},{4,12},{6,14},{8,16},{10,18},{12,20},{14,22},{16,24},... | collective-permute-start | bytes 2752520 | tf_op jit(solution)/shard_map/ppermute | solution.py:27
  36.1 22.2 %collective-permute-start.3 = (bf16[2,448,448]{2,1,0:T(8,128)(2,1)}, bf16[2,448,448]{2,1,0:T(8,128)(2,1)S(1)}, u32[]{:S(2)}, u32[]{:S(2)}) collective-permute-start(bf16[2,448,448]{2,1,0:T(8,128)(2,1)} %get-tuple-element.135), channel_id=1, source_target_pairs={{0,4},{2,6},{4,0},{6,2},{8,12},{10,14},{12,8},{14,10},{16,20},{18,... | collective-permute-start | bytes 2408456 | tf_op jit(solution)/shard_map/ppermute | solution.py:24
  37.9 21.9 %collective-permute-start.2 = (bf16[2,448,448]{2,1,0:T(8,128)(2,1)}, bf16[2,448,448]{2,1,0:T(8,128)(2,1)S(1)}, u32[]{:S(2)}, u32[]{:S(2)}) collective-permute-start(bf16[2,448,448]{2,1,0:T(8,128)(2,1)} %get-tuple-element.136), channel_id=1, source_target_pairs={{0,2},{2,0},{4,6},{6,4},{8,10},{10,8},{12,14},{14,12},{16,18},{18,... | collective-permute-start | bytes 2408456 | tf_op jit(solution)/shard_map/ppermute | solution.py:24
  59.8 29.9 %collective-permute-start.7 = (bf16[1024,448]{0,1:T(8,128)(2,1)}, bf16[1024,448]{0,1:T(8,128)(2,1)}, u32[]{:S(2)}, u32[]{:S(2)}) collective-permute-start(bf16[1024,448]{0,1:T(8,128)(2,1)} %collective-permute-done), channel_id=1, source_target_pairs={{0,8},{2,10},{4,12},{6,14},{8,16},{10,18},{12,20},{14,22},{16,24},... | collective-permute-start | bytes 2752520 | tf_op jit(solution)/shard_map/ppermute | solution.py:27
  63.2 26.5 %collective-permute-start.8 = (bf16[1024,448]{0,1:T(8,128)(2,1)}, bf16[1024,448]{0,1:T(8,128)(2,1)}, u32[]{:S(2)}, u32[]{:S(2)}) collective-permute-start(bf16[1024,448]{0,1:T(8,128)(2,1)} %collective-permute-done.1), channel_id=1, source_target_pairs={{8,0},{10,2},{12,4},{14,6},{16,8},{18,10},{20,12},{22,14},{24,16},... | collective-permute-start | bytes 2752520 | tf_op jit(solution)/shard_map/ppermute | solution.py:30
  64.5 25.2 %collective-permute-start.9 = (bf16[2,448,448]{2,1,0:T(8,128)(2,1)S(1)}, bf16[2,448,448]{2,1,0:T(8,128)(2,1)S(1)}, u32[]{:S(2)}, u32[]{:S(2)}) collective-permute-start(bf16[2,448,448]{2,1,0:T(8,128)(2,1)S(1)} %copy-done.13), channel_id=1, source_target_pairs={{0,6},{2,4},{4,2},{6,0},{8,14},{10,12},{12,10},{14,8},{16,22},{18,... | collective-permute-start | bytes 2408456 | tf_op jit(solution)/shard_map/ppermute | solution.py:24
  66.0 19.1 %collective-permute-start.10 = (s32[512]{0:T(512)S(1)}, s32[512]{0:T(512)S(1)}, u32[]{:S(2)}, u32[]{:S(2)}) collective-permute-start(s32[512]{0:T(512)S(1)} %copy-done.19), channel_id=1, source_target_pairs={{0,2},{2,0},{4,6},{6,4},{8,10},{10,8},{12,14},{14,12},{16,18},{18,... | collective-permute-start | bytes 6152 | tf_op jit(solution)/shard_map/ppermute | solution.py:24
  66.6 20.9 %collective-permute-start.11 = (s32[512]{0:T(512)S(1)}, s32[512]{0:T(512)S(1)}, u32[]{:S(2)}, u32[]{:S(2)}) collective-permute-start(s32[512]{0:T(512)S(1)} %copy-done.19), channel_id=1, source_target_pairs={{0,4},{2,6},{4,0},{6,2},{8,12},{10,14},{12,8},{14,10},{16,20},{18,... | collective-permute-start | bytes 6152 | tf_op jit(solution)/shard_map/ppermute | solution.py:24
  91.8 253.3 %all-gather.13.cloned.1.call-start = ((), (), s32[]{:S(2)}) async-start(), calls=%async_computation.3 | async-start | bytes 11010048 | tf_op jit(solution)/shard_map/all_gather | solution.py:168
  91.9 8.3 %collective-permute-start.15 = (f32[8,128]{1,0:T(8,128)S(1)}, f32[8,128]{1,0:T(8,128)S(1)}, u32[]{:S(2)}, u32[]{:S(2)}) collective-permute-start(f32[8,128]{1,0:T(8,128)S(1)} %add_add_fusion.2), channel_id=1, source_target_pairs={{0,24},{2,26},{4,28},{6,30},{8,0},{10,2},{12,4},{14,6},{16,8},{18,... | collective-permute-start | bytes 12296 | tf_op jit(solution)/shard_map/ppermute | solution.py:70
  95.9 5.4 %collective-permute-start.13 = (f32[8,128]{1,0:T(8,128)S(1)}, f32[8,128]{1,0:T(8,128)S(1)}, u32[]{:S(2)}, u32[]{:S(2)}) collective-permute-start(f32[8,128]{1,0:T(8,128)S(1)} %add_add_fusion.2), channel_id=1, source_target_pairs={{0,8},{2,10},{4,12},{6,14},{8,16},{10,18},{12,20},{14,22},{16,24},... | collective-permute-start | bytes 12296 | tf_op jit(solution)/shard_map/ppermute | solution.py:70
  97.3 26.8 %collective-permute-start.18 = (bf16[512,1024]{1,0:T(8,128)(2,1)}, bf16[512,1024]{1,0:T(8,128)(2,1)S(1)}, u32[]{:S(2)}, u32[]{:S(2)}) collective-permute-start(bf16[512,1024]{1,0:T(8,128)(2,1)} %get-tuple-element.81), channel_id=1, source_target_pairs={{0,2},{2,0},{4,6},{6,4},{8,10},{10,8},{12,14},{14,12},{16,18},{18,... | collective-permute-start | bytes 3145736 | tf_op jit(solution)/shard_map/ppermute | solution.py:24
  98.7 25.4 %collective-permute-start.19 = (bf16[512,1024]{1,0:T(8,128)(2,1)}, bf16[512,1024]{1,0:T(8,128)(2,1)S(1)}, u32[]{:S(2)}, u32[]{:S(2)}) collective-permute-start(bf16[512,1024]{1,0:T(8,128)(2,1)} %get-tuple-element.81), channel_id=1, source_target_pairs={{0,4},{2,6},{4,0},{6,2},{8,12},{10,14},{12,8},{14,10},{16,20},{18,... | collective-permute-start | bytes 3145736 | tf_op jit(solution)/shard_map/ppermute | solution.py:24
  101.3 17.8 %collective-permute-start.16 = (bf16[1024,448]{0,1:T(8,128)(2,1)}, bf16[1024,448]{0,1:T(8,128)(2,1)}, u32[]{:S(2)}, u32[]{:S(2)}) collective-permute-start(bf16[1024,448]{0,1:T(8,128)(2,1)} %collective-permute-done.7), channel_id=1, source_target_pairs={{0,8},{2,10},{4,12},{6,14},{8,16},{10,18},{12,20},{14,22},{16,24},... | collective-permute-start | bytes 2752520 | tf_op jit(solution)/shard_map/ppermute | solution.py:27
  105.1 19.0 %collective-permute-start.17 = (bf16[1024,448]{0,1:T(8,128)(2,1)}, bf16[1024,448]{0,1:T(8,128)(2,1)}, u32[]{:S(2)}, u32[]{:S(2)}) collective-permute-start(bf16[1024,448]{0,1:T(8,128)(2,1)} %collective-permute-done.8), channel_id=1, source_target_pairs={{8,0},{10,2},{12,4},{14,6},{16,8},{18,10},{20,12},{22,14},{24,16},... | collective-permute-start | bytes 2752520 | tf_op jit(solution)/shard_map/ppermute | solution.py:30
  141.8 14.6 %collective-permute-start.21 = (bf16[512,448]{0,1:T(8,128)(2,1)S(1)}, bf16[512,448]{0,1:T(8,128)(2,1)S(1)}, u32[]{:S(2)}, u32[]{:S(2)}) collective-permute-start(bf16[512,448]{0,1:T(8,128)(2,1)S(1)} %get-tuple-element.139), channel_id=1, source_target_pairs={{0,4},{2,6},{4,0},{6,2},{8,12},{10,14},{12,8},{14,10},{16,20},{18,... | collective-permute-start | bytes 1376264 | tf_op jit(solution)/shard_map/ppermute | solution.py:24
  142.8 12.1 %collective-permute-start.23 = (bf16[512,448]{0,1:T(8,128)(2,1)S(1)}, bf16[512,448]{0,1:T(8,128)(2,1)S(1)}, u32[]{:S(2)}, u32[]{:S(2)}) collective-permute-start(bf16[512,448]{0,1:T(8,128)(2,1)S(1)} %get-tuple-element.140), channel_id=1, source_target_pairs={{0,2},{2,0},{4,6},{6,4},{8,10},{10,8},{12,14},{14,12},{16,18},{18,... | collective-permute-start | bytes 1376264 | tf_op jit(solution)/shard_map/ppermute | solution.py:24
  155.2 19.5 %collective-permute-start.24 = (bf16[1024,448]{0,1:T(8,128)(2,1)S(1)}, bf16[1024,448]{0,1:T(8,128)(2,1)S(1)}, u32[]{:S(2)}, u32[]{:S(2)}) collective-permute-start(bf16[1024,448]{0,1:T(8,128)(2,1)S(1)} %pad_maximum_fusion.6), channel_id=1, source_target_pairs={{0,4},{2,6},{4,0},{6,2},{8,12},{10,14},{12,8},{14,10},{16,20},{18,... | collective-permute-start | bytes 2752520 | tf_op jit(solution)/shard_map/ppermute | solution.py:24
  156.7 18.8 %collective-permute-start.22 = (bf16[1024,448]{0,1:T(8,128)(2,1)S(1)}, bf16[1024,448]{0,1:T(8,128)(2,1)S(1)}, u32[]{:S(2)}, u32[]{:S(2)}) collective-permute-start(bf16[1024,448]{0,1:T(8,128)(2,1)S(1)} %pad_maximum_fusion.5), channel_id=1, source_target_pairs={{0,2},{2,0},{4,6},{6,4},{8,10},{10,8},{12,14},{14,12},{16,18},{18,... | collective-permute-start | bytes 2752520 | tf_op jit(solution)/shard_map/ppermute | solution.py:24
  176.1 18.1 %collective-permute-start.26 = (bf16[1024,448]{0,1:T(8,128)(2,1)S(1)}, bf16[1024,448]{0,1:T(8,128)(2,1)S(1)}, u32[]{:S(2)}, u32[]{:S(2)}) collective-permute-start(bf16[1024,448]{0,1:T(8,128)(2,1)S(1)} %divide_convert_fusion), channel_id=1, source_target_pairs={{0,4},{2,6},{4,0},{6,2},{8,12},{10,14},{12,8},{14,10},{16,20},{18,... | collective-permute-start | bytes 2752520 | tf_op jit(solution)/shard_map/ppermute | solution.py:24
  177.8 18.3 %collective-permute-start.25 = (bf16[1024,448]{0,1:T(8,128)(2,1)S(1)}, bf16[1024,448]{0,1:T(8,128)(2,1)S(1)}, u32[]{:S(2)}, u32[]{:S(2)}) collective-permute-start(bf16[1024,448]{0,1:T(8,128)(2,1)S(1)} %divide_convert_fusion), channel_id=1, source_target_pairs={{0,2},{2,0},{4,6},{6,4},{8,10},{10,8},{12,14},{14,12},{16,18},{18,... | collective-permute-start | bytes 2752520 | tf_op jit(solution)/shard_map/ppermute | solution.py:24
  195.1 11.7 %collective-permute-start.27 = (bf16[512,448]{0,1:T(8,128)(2,1)}, bf16[512,448]{0,1:T(8,128)(2,1)S(1)}, u32[]{:S(2)}, u32[]{:S(2)}) collective-permute-start(bf16[512,448]{0,1:T(8,128)(2,1)} %split.48), channel_id=1, source_target_pairs={{0,2},{2,0},{4,6},{6,4},{8,10},{10,8},{12,14},{14,12},{16,18},{18,... | collective-permute-start | bytes 1376264 | tf_op jit(solution)/shard_map/ppermute | solution.py:24
  197.2 9.6 %collective-permute-start.28 = (bf16[512,448]{0,1:T(8,128)(2,1)}, bf16[512,448]{0,1:T(8,128)(2,1)}, u32[]{:S(2)}, u32[]{:S(2)}) collective-permute-start(bf16[512,448]{0,1:T(8,128)(2,1)} %split.49), channel_id=1, source_target_pairs={{0,4},{2,6},{4,0},{6,2},{8,12},{10,14},{12,8},{14,10},{16,20},{18,... | collective-permute-start | bytes 1376264 | tf_op jit(solution)/shard_map/ppermute | solution.py:24
  215.5 21.1 %collective-permute-start.31 = (bf16[2,512,448]{1,2,0:T(8,128)(2,1)S(1)}, bf16[2,512,448]{1,2,0:T(8,128)(2,1)S(1)}, u32[]{:S(2)}, u32[]{:S(2)}) collective-permute-start(bf16[2,512,448]{1,2,0:T(8,128)(2,1)S(1)} %get-tuple-element.98), channel_id=1, source_target_pairs={{0,2},{2,0},{4,6},{6,4},{8,10},{10,8},{12,14},{14,12},{16,18},{18,... | collective-permute-start | bytes 2752520 | tf_op jit(solution)/shard_map/ppermute | solution.py:24
  217.2 19.3 %collective-permute-start.32 = (bf16[2,512,448]{1,2,0:T(8,128)(2,1)S(1)}, bf16[2,512,448]{1,2,0:T(8,128)(2,1)S(1)}, u32[]{:S(2)}, u32[]{:S(2)}) collective-permute-start(bf16[2,512,448]{1,2,0:T(8,128)(2,1)S(1)} %get-tuple-element.99), channel_id=1, source_target_pairs={{0,4},{2,6},{4,0},{6,2},{8,12},{10,14},{12,8},{14,10},{16,20},{18,... | collective-permute-start | bytes 2752520 | tf_op jit(solution)/shard_map/ppermute | solution.py:24
  217.5 19.1 %collective-permute-start.29 = (bf16[448,1024]{1,0:T(8,128)(2,1)S(1)}, bf16[448,1024]{1,0:T(8,128)(2,1)S(1)}, u32[]{:S(2)}, u32[]{:S(2)}) collective-permute-start(bf16[448,1024]{1,0:T(8,128)(2,1)S(1)} %get-tuple-element.143), channel_id=1, source_target_pairs={{0,8},{2,10},{4,12},{6,14},{8,16},{10,18},{12,20},{14,22},{16,24},... | collective-permute-start | bytes 2752520 | tf_op jit(solution)/shard_map/ppermute | solution.py:27
  220.5 23.0 %collective-permute-start.30 = (bf16[448,1024]{1,0:T(8,128)(2,1)S(1)}, bf16[448,1024]{1,0:T(8,128)(2,1)S(1)}, u32[]{:S(2)}, u32[]{:S(2)}) collective-permute-start(bf16[448,1024]{1,0:T(8,128)(2,1)S(1)} %get-tuple-element.145), channel_id=1, source_target_pairs={{8,0},{10,2},{12,4},{14,6},{16,8},{18,10},{20,12},{22,14},{24,16},... | collective-permute-start | bytes 2752520 | tf_op jit(solution)/shard_map/ppermute | solution.py:30
  244.0 18.1 %collective-permute-start.34 = (bf16[448,1024]{1,0:T(8,128)(2,1)S(1)}, bf16[448,1024]{1,0:T(8,128)(2,1)S(1)}, u32[]{:S(2)}, u32[]{:S(2)}) collective-permute-start(bf16[448,1024]{1,0:T(8,128)(2,1)S(1)} %get-tuple-element.137), channel_id=1, source_target_pairs={{8,0},{10,2},{12,4},{14,6},{16,8},{18,10},{20,12},{22,14},{24,16},... | collective-permute-start | bytes 2752520 | tf_op jit(solution)/shard_map/ppermute | solution.py:30
  245.3 24.3 %collective-permute-start.33 = (bf16[448,1024]{1,0:T(8,128)(2,1)S(1)}, bf16[448,1024]{1,0:T(8,128)(2,1)}, u32[]{:S(2)}, u32[]{:S(2)}) collective-permute-start(bf16[448,1024]{1,0:T(8,128)(2,1)S(1)} %get-tuple-element.138), channel_id=1, source_target_pairs={{0,8},{2,10},{4,12},{6,14},{8,16},{10,18},{12,20},{14,22},{16,24},... | collective-permute-start | bytes 2752520 | tf_op jit(solution)/shard_map/ppermute | solution.py:27
  250.8 20.0 %collective-permute-start.35 = (bf16[2,512,448]{1,2,0:T(8,128)(2,1)S(1)}, bf16[2,512,448]{1,2,0:T(8,128)(2,1)S(1)}, u32[]{:S(2)}, u32[]{:S(2)}) collective-permute-start(bf16[2,512,448]{1,2,0:T(8,128)(2,1)S(1)} %get-tuple-element.103), channel_id=1, source_target_pairs={{0,6},{2,4},{4,2},{6,0},{8,14},{10,12},{12,10},{14,8},{16,22},{18,... | collective-permute-start | bytes 2752520 | tf_op jit(solution)/shard_map/ppermute | solution.py:24
  275.2 21.8 %collective-permute-start.36 = (bf16[448,1024]{1,0:T(8,128)(2,1)S(1)}, bf16[448,1024]{1,0:T(8,128)(2,1)S(1)}, u32[]{:S(2)}, u32[]{:S(2)}) collective-permute-start(bf16[448,1024]{1,0:T(8,128)(2,1)S(1)} %fusion.19), channel_id=1, source_target_pairs={{0,8},{2,10},{4,12},{6,14},{8,16},{10,18},{12,20},{14,22},{16,24},... | collective-permute-start | bytes 2752520 | tf_op jit(solution)/shard_map/ppermute | solution.py:27
  279.1 18.5 %collective-permute-start.37 = (bf16[448,1024]{1,0:T(8,128)(2,1)S(1)}, bf16[448,1024]{1,0:T(8,128)(2,1)S(1)}, u32[]{:S(2)}, u32[]{:S(2)}) collective-permute-start(bf16[448,1024]{1,0:T(8,128)(2,1)S(1)} %fusion.12), channel_id=1, source_target_pairs={{8,0},{10,2},{12,4},{14,6},{16,8},{18,10},{20,12},{22,14},{24,16},... | collective-permute-start | bytes 2752520 | tf_op jit(solution)/shard_map/ppermute | solution.py:30
  280.4 10.6 %collective-permute-start.38 = (bf16[256,1024]{1,0:T(8,128)(2,1)S(1)}, bf16[256,1024]{1,0:T(8,128)(2,1)S(1)}, u32[]{:S(2)}, u32[]{:S(2)}) collective-permute-start(bf16[256,1024]{1,0:T(8,128)(2,1)S(1)} %copy-done.14), channel_id=1, source_target_pairs={{0,2},{2,0},{4,6},{6,4},{8,10},{10,8},{12,14},{14,12},{16,18},{18,... | collective-permute-start | bytes 1572872 | tf_op jit(solution)/shard_map/ppermute | solution.py:24
  283.9 9.2 %collective-permute-start.39 = (bf16[256,1024]{1,0:T(8,128)(2,1)S(1)}, bf16[256,1024]{1,0:T(8,128)(2,1)S(1)}, u32[]{:S(2)}, u32[]{:S(2)}) collective-permute-start(bf16[256,1024]{1,0:T(8,128)(2,1)S(1)} %split.41), channel_id=1, source_target_pairs={{0,4},{2,6},{4,0},{6,2},{8,12},{10,14},{12,8},{14,10},{16,20},{18,... | collective-permute-start | bytes 1572872 | tf_op jit(solution)/shard_map/ppermute | solution.py:24
  298.1 20.3 %collective-permute-start.41 = (bf16[448,1024]{1,0:T(8,128)(2,1)S(1)}, bf16[448,1024]{1,0:T(8,128)(2,1)}, u32[]{:S(2)}, u32[]{:S(2)}) collective-permute-start(bf16[448,1024]{1,0:T(8,128)(2,1)S(1)} %fusion.8), channel_id=1, source_target_pairs={{8,0},{10,2},{12,4},{14,6},{16,8},{18,10},{20,12},{22,14},{24,16},... | collective-permute-start | bytes 2752520 | tf_op jit(solution)/shard_map/ppermute | solution.py:30
  299.4 20.6 %collective-permute-start.40 = (bf16[448,1024]{1,0:T(8,128)(2,1)S(1)}, bf16[448,1024]{1,0:T(8,128)(2,1)}, u32[]{:S(2)}, u32[]{:S(2)}) collective-permute-start(bf16[448,1024]{1,0:T(8,128)(2,1)S(1)} %fusion.8), channel_id=1, source_target_pairs={{0,8},{2,10},{4,12},{6,14},{8,16},{10,18},{12,20},{14,22},{16,24},... | collective-permute-start | bytes 2752520 | tf_op jit(solution)/shard_map/ppermute | solution.py:27
  318.5 16.8 %collective-permute-start.42 = (bf16[448,1024]{1,0:T(8,128)(2,1)}, bf16[448,1024]{1,0:T(8,128)(2,1)}, u32[]{:S(2)}, u32[]{:S(2)}) collective-permute-start(bf16[448,1024]{1,0:T(8,128)(2,1)} %collective-permute-done.41), channel_id=1, source_target_pairs={{8,0},{10,2},{12,4},{14,6},{16,8},{18,10},{20,12},{22,14},{24,16},... | collective-permute-start | bytes 2752520 | tf_op jit(solution)/shard_map/ppermute | solution.py:30
  320.1 20.6 %collective-permute-start.44 = (bf16[448,1024]{1,0:T(8,128)(2,1)}, bf16[448,1024]{1,0:T(8,128)(2,1)}, u32[]{:S(2)}, u32[]{:S(2)}) collective-permute-start(bf16[448,1024]{1,0:T(8,128)(2,1)} %collective-permute-done.40), channel_id=1, source_target_pairs={{0,8},{2,10},{4,12},{6,14},{8,16},{10,18},{12,20},{14,22},{16,24},... | collective-permute-start | bytes 2752520 | tf_op jit(solution)/shard_map/ppermute | solution.py:27
  335.3 18.9 %collective-permute-start.43 = (bf16[448,1024]{1,0:T(8,128)(2,1)}, bf16[448,1024]{1,0:T(8,128)(2,1)S(1)}, u32[]{:S(2)}, u32[]{:S(2)}) collective-permute-start(bf16[448,1024]{1,0:T(8,128)(2,1)} %collective-permute-done.42), channel_id=1, source_target_pairs={{8,0},{10,2},{12,4},{14,6},{16,8},{18,10},{20,12},{22,14},{24,16},... | collective-permute-start | bytes 2752520 | tf_op jit(solution)/shard_map/ppermute | solution.py:30
  340.7 16.1 %collective-permute-start.45 = (bf16[448,1024]{1,0:T(8,128)(2,1)}, bf16[448,1024]{1,0:T(8,128)(2,1)S(1)}, u32[]{:S(2)}, u32[]{:S(2)}) collective-permute-start(bf16[448,1024]{1,0:T(8,128)(2,1)} %collective-permute-done.44), channel_id=1, source_target_pairs={{0,8},{2,10},{4,12},{6,14},{8,16},{10,18},{12,20},{14,22},{16,24},... | collective-permute-start | bytes 2752520 | tf_op jit(solution)/shard_map/ppermute | solution.py:27
  367.6 6.9 %collective-permute-start.51 = (f32[32]{0:T(128)S(1)}, f32[32]{0:T(128)S(1)}, u32[]{:S(2)}, u32[]{:S(2)}) collective-permute-start(f32[32]{0:T(128)S(1)} %add_add_fusion.4), channel_id=1, source_target_pairs={{0,24},{2,26},{4,28},{6,30},{8,0},{10,2},{12,4},{14,6},{16,8},{18,... | collective-permute-start | bytes 392 | tf_op jit(solution)/shard_map/ppermute | solution.py:70
  (35 other events, 307.7 us)
Sparse Core Ops, SparseCore 0:
  8.9 12.8 all-gather.8
  23.4 11.7 all-gather.6
  91.9 19.7 all-gather.10
  273.1 18.2 all-gather.12
